TPU v7x, 128 devices: a whole 4x4x4 slice. The times are simulated.
128 devices in a mesh: wide: 32 (over x, z, core), narrow: 4 (over y).
Axes of the slice: x: 4, y: 4, z: 4, core: 2. Of those that a mesh axis runs over, the one named last changes fastest.
Arguments:
- ref_local: float32 [3, 128, 16, 128], P(None, 'wide', 'narrow'), may hold values from 0 to 8, as said below
- displacement: float32 [3, 128, 16, 128], P(None, 'wide', 'narrow'), may hold values from -0.3125 to 0.3125
- velocity: float32 [3, 128, 16, 128], P(None, 'wide', 'narrow'), may hold values from -4 to 4
- acceleration: float32 [3, 128, 16, 128], P(None, 'wide', 'narrow'), may hold values from -12 to 12
- history: float32 [128, 16, 6, 128, 128], P('wide', 'narrow'), may hold values from 0 to 1.5
- critical: float32 [128, 16, 6], P('wide', 'narrow'), may hold values from 0.003 to 0.03
- active: int32 [128, 16, 6], P('wide', 'narrow'), may hold values 0 or 1
- partners: int32 [128, 16, 6], P('wide', 'narrow'), may hold values from 0 to 8, as said below
- move_src: int32 [32, 4, 2, 2], P('wide', 'narrow'), may hold values from -1 to 15, as said below
- move_dst: int32 [32, 4, 2, 2], P('wide', 'narrow'), may hold values from -1 to 15, as said below
Outputs:
- ref_out: float32 [3, 128, 16, 128], P(None, 'wide', 'narrow')
- disp_out: float32 [3, 128, 16, 128], P(None, 'wide', 'narrow')
- vel_out: float32 [3, 128, 16, 128], P(None, 'wide', 'narrow')
- acc_out: float32 [3, 128, 16, 128], P(None, 'wide', 'narrow')
- hist_out: float32 [128, 16, 6, 128, 128], P('wide', 'narrow')
Inputs may be any that keep to these rules, and one draw needn't show every extreme that they name: ref_local[:, i, j, p] lies in [0, 4] x [0, 4] x [0, 8]; two points of the grid are at least 0.6 apart. `partners`: slot 0 names the cluster itself (offset 4); the other slots of a cluster name distinct offsets other than 4. move_src[w, n, 0, :] lists the clusters tile (w, n) hands to tile (w + 1, n), move_src[w, n, 1, :] those it hands to tile (w - 1, n), used entries first and -1 after them; a tile hands on distinct clusters. Across each boundary between tiles (w, n) and (w + 1, n) equally many clusters go each way, 1 to 2, and 2 across some boundary of every n. `move_dst`: -1 exactly where move_src is -1; the slots that a tile hands on are exactly the slots that arriving clusters take, one each.
All inputs are finite; a program needn't handle non-finite values. No bound on the sum of `active` on one device may be relied on, other than what follows from the above.
Results may differ from a plain program's by a relative error of at most 0.0003.
Values sent between devices are 32-bit elements; how exact they have to be, the bound alone decides.
A program may use at most 128 MiB of HBM per device.

v0:
```python
import jax
import jax.numpy as jnp
from jax import lax
from jax.sharding import PartitionSpec as P

STIFFNESS = 8.0
DAMPING = 0.8
TIME_STEP = 0.1
RANGE_SQ = 9.0
CELL_SPAN = 4.0


def extended(value, sides, width):
    for axis, dim in sides:
        size, length = (lax.axis_size(axis), value.shape[dim])
        up = [(i, (i + 1) % size) for i in range(size - 1)]
        down = [(j, i) for i, j in up]
        last = lax.slice_in_dim(value, length - width, length, axis=dim)
        first = lax.slice_in_dim(value, 0, width, axis=dim)
        before = lax.ppermute(last, axis, up)
        after = lax.ppermute(first, axis, down)
        value = jnp.concatenate([before, value, after], axis=dim)
    return value


def from_behind(value, axis, by):
    length = lax.axis_size(axis)
    pairs = [(i, i + by) for i in range(length) if 0 <= i + by < length]
    return lax.ppermute(value, axis, pairs)


def advance(displacement, velocity, acceleration):
    disp_new = displacement + TIME_STEP * velocity + 0.5 * TIME_STEP * TIME_STEP * acceleration
    vel_half = velocity + 0.5 * TIME_STEP * acceleration
    return (disp_new, vel_half)


def bond_terms(
    own_rows, other_rows, shift_w, shift_n, history_rows, limit_rows, switch, same_cluster
):
    points = own_rows.shape[2]
    unit_eye = jnp.eye(points, dtype=jnp.float32)
    live_mask = switch[:, None, None] * (1.0 - same_cluster[:, None, None] * unit_eye[None])
    anchors = (CELL_SPAN * shift_w, CELL_SPAN * shift_n, jnp.zeros_like(shift_w))
    ref_sq = jnp.zeros(live_mask.shape, jnp.float32)
    cur_sq = jnp.zeros(live_mask.shape, jnp.float32)
    closing = jnp.zeros(live_mask.shape, jnp.float32)
    cur_gaps = []
    for axis_id in range(3):
        anchor = anchors[axis_id][:, None, None]
        ref_gap = other_rows[axis_id][:, None, :] + anchor - own_rows[axis_id][:, :, None]
        cur_gap = other_rows[3 + axis_id][:, None, :] + anchor - own_rows[3 + axis_id][:, :, None]
        vel_gap = other_rows[6 + axis_id][:, None, :] - own_rows[6 + axis_id][:, :, None]
        ref_sq = ref_sq + ref_gap * ref_gap
        cur_sq = cur_sq + cur_gap * cur_gap
        closing = closing + vel_gap * cur_gap
        cur_gaps.append(cur_gap)
    bonded = live_mask > 0.5
    rest_len = jnp.where(bonded, jnp.sqrt(ref_sq), 1.0)
    now_len = jnp.where(bonded, jnp.sqrt(cur_sq), 1.0)
    stretch = jnp.where(bonded, (now_len - rest_len) / rest_len, 0.0)
    safe_limit = jnp.where(limit_rows > 0.0, limit_rows, 1.0)
    history_new = jnp.where(
        bonded, jnp.maximum(history_rows, stretch / safe_limit[:, None, None]), history_rows
    )
    intact = jnp.clip(2.0 - history_new, 0.0, 1.0)
    weight = jnp.exp(-ref_sq / RANGE_SQ) * intact * live_mask
    factor = weight * (STIFFNESS * stretch + DAMPING * closing / now_len) / now_len
    slot_pulls = jnp.stack([jnp.sum(factor * gap_axis, axis=2) for gap_axis in cur_gaps], 0)
    return (slot_pulls, history_new)


def cluster_rows(state_rows):
    return jnp.transpose(state_rows, (1, 0, 2)).reshape(state_rows.shape[1], -1)


def pick_rows(row_table, chosen_ids):
    chosen = jnp.take(row_table, jnp.maximum(chosen_ids, 0), axis=0)
    return jnp.where((chosen_ids >= 0)[:, None], chosen, 0.0)


def outgoing(row_table, chosen_ids, dest_ids, points):
    tag_values = jnp.where(chosen_ids >= 0, dest_ids + 1, 0).astype(jnp.float32)
    tag_block = jnp.concatenate(
        [tag_values[:, None], jnp.zeros((chosen_ids.shape[0], points - 1), jnp.float32)], 1
    )
    return jnp.concatenate([pick_rows(row_table, chosen_ids), tag_block], 1)


def place_rows(cluster_count, targets):
    slot_ids = jnp.arange(cluster_count, dtype=jnp.int32)
    hit_table = targets[None, :] == slot_ids[:, None]
    landed = jnp.any(hit_table, axis=1)
    arrival = jnp.sum(
        jnp.where(hit_table, jnp.arange(targets.shape[0], dtype=jnp.int32)[None, :], 0), axis=1
    )
    return jnp.where(landed, cluster_count + arrival, slot_ids)


def per_device(
    ref_local,
    displacement,
    velocity,
    acceleration,
    history,
    critical,
    active,
    partners,
    move_src,
    move_dst,
):
    clus_w, clus_n, points = (ref_local.shape[1], ref_local.shape[2], ref_local.shape[3])
    cluster_count = clus_w * clus_n
    slot_total = partners.shape[2]
    disp_new, vel_half = advance(displacement, velocity, acceleration)
    grid_field = jnp.concatenate([ref_local, ref_local + disp_new, vel_half], 0)
    row_ids = jnp.arange(clus_w, dtype=jnp.int32)[:, None, None]
    col_ids = jnp.arange(clus_n, dtype=jnp.int32)[None, :, None]
    grid_row = lax.axis_index("wide") * clus_w + row_ids
    grid_col = lax.axis_index("narrow") * clus_n + col_ids
    rows_all = clus_w * lax.axis_size("wide")
    cols_all = clus_n * lax.axis_size("narrow")
    shift_w = partners // 3 - 1
    shift_n = partners % 3 - 1
    inside = (
        (grid_row + shift_w >= 0)
        & (grid_row + shift_w < rows_all)
        & (grid_col + shift_n >= 0)
        & (grid_col + shift_n < cols_all)
    )
    switch = (inside & (active > 0)).astype(jnp.float32).reshape(cluster_count, slot_total)
    same_cluster = (partners == 4).astype(jnp.float32).reshape(cluster_count, slot_total)
    limits = critical.reshape(cluster_count, slot_total)
    shift_wf = shift_w.astype(jnp.float32).reshape(cluster_count, slot_total)
    shift_nf = shift_n.astype(jnp.float32).reshape(cluster_count, slot_total)
    pick_ids = ((row_ids + 1 + shift_w) * (clus_n + 2) + col_ids + 1 + shift_n).reshape(
        cluster_count, slot_total
    )
    own_rows = grid_field.reshape(9, cluster_count, points)
    history_rows = history.reshape(cluster_count, slot_total, points, points)
    right_ids = move_src[0, 0, 0]
    left_ids = move_src[0, 0, 1]
    right_dest = move_dst[0, 0, 0]
    left_dest = move_dst[0, 0, 1]
    padded = extended(grid_field, (("wide", 1), ("narrow", 2)), 1)
    padded_flat = padded.reshape(9, (clus_w + 2) * (clus_n + 2), points)
    pulls_total = jnp.zeros((3, cluster_count, points), jnp.float32)
    hist_list = []
    neighbours = []
    for slot_id in range(slot_total):
        other_rows = jnp.take(padded_flat, pick_ids[:, slot_id], axis=1)
        slot_pulls, hist_slot = bond_terms(
            own_rows,
            other_rows,
            shift_wf[:, slot_id],
            shift_nf[:, slot_id],
            history_rows[:, slot_id],
            limits[:, slot_id],
            switch[:, slot_id],
            same_cluster[:, slot_id],
        )
        pulls_total = pulls_total + slot_pulls
        hist_list.append(hist_slot)
        neighbours.append(other_rows)
    acc_new = pulls_total.reshape(3, clus_w, clus_n, points)
    vel_new = vel_half + 0.5 * TIME_STEP * acc_new
    hist_new = jnp.stack(hist_list, 1)
    state_new = jnp.concatenate([ref_local, disp_new, vel_new, acc_new], 0).reshape(
        12, cluster_count, points
    )
    own_table = jnp.concatenate([hist_new.reshape(cluster_count, -1), cluster_rows(state_new)], 1)
    table_width = own_table.shape[1]
    from_left = from_behind(outgoing(own_table, right_ids, right_dest, points), "wide", 1)
    from_right = from_behind(outgoing(own_table, left_ids, left_dest, points), "wide", -1)
    arrivals = jnp.concatenate([from_left, from_right], 0)
    incoming_rows = arrivals[:, :table_width]
    targets = arrivals[:, table_width].astype(jnp.int32) - 1
    source = place_rows(cluster_count, targets)
    merged = jnp.take(jnp.concatenate([own_table, incoming_rows], 0), source, axis=0)
    hist_size = slot_total * points * points
    hist_out = merged[:, :hist_size].reshape(clus_w, clus_n, slot_total, points, points)
    state_out = jnp.transpose(
        merged[:, hist_size:].reshape(cluster_count, 12, points), (1, 0, 2)
    ).reshape(12, clus_w, clus_n, points)
    return (state_out[0:3], state_out[3:6], state_out[6:9], state_out[9:12], hist_out)


def solution(mesh):
    placed = (
        P(None, "wide", "narrow", None),
        P(None, "wide", "narrow", None),
        P(None, "wide", "narrow", None),
        P(None, "wide", "narrow", None),
        P("wide", "narrow", None, None, None),
        P("wide", "narrow", None),
        P("wide", "narrow", None),
        P("wide", "narrow", None),
        P("wide", "narrow", None, None),
        P("wide", "narrow", None, None),
    )
    return jax.shard_map(
        per_device,
        mesh=mesh,
        in_specs=placed,
        out_specs=(
            P(None, "wide", "narrow", None),
            P(None, "wide", "narrow", None),
            P(None, "wide", "narrow", None),
            P(None, "wide", "narrow", None),
            P("wide", "narrow", None, None, None),
        ),
        check_vma=False,
    )
```

profile of v0, /device:TPU:30, one launch (start us, length us, event | category | flops | bytes accessed | tf_op | source)
XLA Modules:
  0.0 143.6 jit_solution(3101531013804360404)
XLA Ops:
  0.6 0.8 fusion.167
  1.5 0.7 pad_maximum_fusion.10
  2.2 5.7 %collective-permute-start.1 = (f32[9,1,4,128]{3,2,1,0:T(4,128)S(1)}, f32[9,1,4,128]{3,2,1,0:T(4,128)S(1)}, u32[]{:S(2)}, u32[]{:S(2)}) collective-permute-start(f32[9,1,4,128]{3,2,1,0:T(4,128)S(1)} %get-tuple-element.150), channel_id=1, source_target_pairs={{4,0},{8,4},{12,8},{16,12},{20,16},{24,20},{28,24},{32,28},{36,32}... | collective-permute-start | bytes 55304 | tf_op jit(solution)/shard_map/ppermute | solution.py:21
  7.8 1.9 %collective-permute-start = (f32[9,1,4,128]{3,2,1,0:T(4,128)S(1)}, f32[9,1,4,128]{3,2,1,0:T(4,128)S(1)}, u32[]{:S(2)}, u32[]{:S(2)}) collective-permute-start(f32[9,1,4,128]{3,2,1,0:T(4,128)S(1)} %get-tuple-element.149), channel_id=1, source_target_pairs={{0,4},{4,8},{8,12},{12,16},{16,20},{20,24},{24,28},{28,32},{32,36}... | collective-permute-start | bytes 55304 | tf_op jit(solution)/shard_map/ppermute | solution.py:20
  9.8 0.7 fusion.177
  10.5 0.8 fusion.166
  11.7 0.8 compare_and_fusion.1
  12.4 0.8 compare_bitcast_fusion.1
  13.2 1.2 slice_reduce_fusion
  14.9 0.8 and_convert_fusion
  16.3 0.8 fusion.161
  17.1 0.9 pad_maximum_fusion.7
  18.0 2.6 %collective-permute-start.3 = (f32[9,6,1,128]{3,2,1,0:T(1,128)S(1)}, f32[9,6,1,128]{3,2,1,0:T(1,128)S(1)}, u32[]{:S(2)}, u32[]{:S(2)}) collective-permute-start(f32[9,6,1,128]{3,2,1,0:T(1,128)S(1)} %get-tuple-element.148), channel_id=1, source_target_pairs={{1,0},{2,1},{3,2},{5,4},{6,5},{7,6},{9,8},{10,9},{11,10},{13,12},{... | collective-permute-start | bytes 82952 | tf_op jit(solution)/shard_map/ppermute | solution.py:21
  20.6 1.3 collective-permute-start.2
  22.0 0.8 copy.98
  22.9 3.5 %collective-permute-done.2 = f32[9,6,1,128]{3,2,1,0:T(1,128)S(1)} collective-permute-done((f32[9,6,1,128]{3,2,1,0:T(1,128)S(1)}, f32[9,6,1,128]{3,2,1,0:T(1,128)S(1)}, u32[]{:S(2)}, u32[]{:S(2)}) %collective-permute-start.2) | collective-permute-done | bytes 27680 | tf_op jit(solution)/shard_map/ppermute | solution.py:20
  26.4 0.8 pad_maximum_fusion.1
  27.3 0.6 gather_fusion.1
  28.0 0.6 gather_fusion.2
  28.7 0.6 gather_fusion.3
  29.5 0.6 gather_fusion.4
  30.2 0.6 gather_fusion.5
  30.9 0.6 gather_fusion.6
  32.5 4.0 %bitcast_dynamic-update-slice_fusion.5 = f32[16,6,128,128]{3,2,1,0:T(8,128)S(1)} fusion(f32[16,6,128,128]{3,2,1,0:T(8,128)} %bitcast.255, f32[16]{0:T(128)S(1)} %get-tuple-element.201, f32[16,128]{1,0:T(8,128)S(1)} %bitcast.313, f32[16,128]{1,0:T(8,128)S(1)} %bitcast.333, f32[16,128]{1,0:T(8,128)S(1)} %bitcast.305, f32[16,128]{1,0:T(8,128)S(1)} %get-tuple-element.195, ...), kind=kLoop, calls=%fused_computation.224 | loop fusion | flops 7340031 | bytes 2261184
  36.5 3.6 %bitcast_dynamic-update-slice_fusion.4 = f32[16,6,128,128]{3,2,1,0:T(8,128)S(1)} fusion(f32[16,6,128,128]{3,2,1,0:T(8,128)S(1)} %bitcast_dynamic-update-slice_fusion.5, f32[16,6,128,128]{3,2,1,0:T(8,128)} %bitcast.256, f32[16]{0:T(128)S(1)} %get-tuple-element.200, f32[16,128]{1,0:T(8,128)S(1)} %bitcast.349, f32[16,128]{1,0:T(8,128)S(1)} %get-tuple-element.191, ...), kind=kLoop, calls=%fused_computation.223 | loop fusion | flops 7340032 | bytes 2262528
  40.2 3.6 %bitcast_dynamic-update-slice_fusion.3 = f32[16,6,128,128]{3,2,1,0:T(8,128)S(1)} fusion(f32[16,6,128,128]{3,2,1,0:T(8,128)S(1)} %bitcast_dynamic-update-slice_fusion.4, f32[16,6,128,128]{3,2,1,0:T(8,128)} %bitcast.257, f32[16]{0:T(128)S(1)} %get-tuple-element.199, f32[16,128]{1,0:T(8,128)S(1)} %bitcast.353, f32[16,128]{1,0:T(8,128)S(1)} %get-tuple-element.187, ...), kind=kLoop, calls=%fused_computation.222 | loop fusion | flops 7340032 | bytes 2262528
  43.8 2.0 %bitcast_dynamic-update-slice_fusion.2 = f32[16,6,128,128]{3,2,1,0:T(8,128)S(1)} fusion(f32[16,6,128,128]{3,2,1,0:T(8,128)S(1)} %bitcast_dynamic-update-slice_fusion.3, f32[16,6,128,128]{3,2,1,0:T(8,128)S(1)} %bitcast.258, f32[16]{0:T(128)S(1)} %get-tuple-element.198, f32[16,128]{1,0:T(8,128)S(1)} %bitcast.337, f32[16,128]{1,0:T(8,128)S(1)} %get-tuple-element.183, ...), kind=kLoop, calls=%fused_computation.221 | loop fusion | flops 7340032 | bytes 2262528
  45.8 2.0 %bitcast_dynamic-update-slice_fusion.1 = f32[16,6,128,128]{3,2,1,0:T(8,128)S(1)} fusion(f32[16,6,128,128]{3,2,1,0:T(8,128)S(1)} %bitcast_dynamic-update-slice_fusion.2, f32[16,6,128,128]{3,2,1,0:T(8,128)S(1)} %bitcast.259, f32[16]{0:T(128)S(1)} %get-tuple-element.197, f32[16,128]{1,0:T(8,128)S(1)} %bitcast.341, f32[16,128]{1,0:T(8,128)S(1)} %get-tuple-element.179, ...), kind=kLoop, calls=%fused_computation.220 | loop fusion | flops 7340032 | bytes 2262528
  47.7 2.0 %fusion.128 = f32[16,6,128,128]{3,2,1,0:T(8,128)S(1)} fusion(f32[16,6,128,128]{3,2,1,0:T(8,128)S(1)} %bitcast_dynamic-update-slice_fusion.1, f32[16,6,128,128]{3,2,1,0:T(8,128)S(1)} %bitcast.260, f32[16]{0:T(128)S(1)} %get-tuple-element.196, f32[16,128]{1,0:T(8,128)S(1)} %bitcast.345, f32[16,128]{1,0:T(8,128)S(1)} %get-tuple-element.175, ...), kind=kLoop, calls=%fused_computation.219 | loop fusion | flops 7340032 | bytes 2262528 | tf_op jit(solution)/shard_map/stack | solution.py:167
  49.7 6.3 %bitcast_dynamic-update-slice_fusion = f32[16,99840]{1,0:T(8,128)} fusion(f32[2,8,768,128]{3,2,1,0:T(8,128)S(1)} %bitcast.254), kind=kLoop, calls=%fused_computation.11 | loop fusion | bytes 12582912
  56.0 8.2 %fusion.77 = (f32[16,128]{1,0:T(8,128)S(1)}, f32[16,128]{1,0:T(8,128)S(1)}, f32[16,128]{1,0:T(8,128)S(1)}, f32[16,128]{1,0:T(8,128)S(1)}, f32[16,128]{1,0:T(8,128)S(1)}, /*index=5*/f32[16,128]{1,0:T(8,128)S(1)}) fusion(f32[16,128]{1,0:T(8,128)S(1)} %get-tuple-element.188, f32[16,128]{1,0:T(8,128)S(1)} %bitcast.295, f32[16,128]{1,0:T(8,128)S(1)} %bitcast.287, ...), kind=kLoop, calls=%fused_computation.167 | loop fusion | flops 28299264 | bytes 2433408 | tf_op jit(solution)/shard_map/reduce_sum | solution.py:69
  64.3 13.7 %fusion.65 = (f32[16,128]{1,0:T(8,128)S(1)}, f32[16,128]{1,0:T(8,128)S(1)}, f32[16,128]{1,0:T(8,128)S(1)}, f32[16,128]{1,0:T(8,128)S(1)}, f32[16,128]{1,0:T(8,12...) fusion(f32[16,128]{1,0:T(8,128)S(1)} %bitcast.296, ...), kind=kLoop, calls=%fused_computation.155 | loop fusion | flops 56598528 | bytes 4727552 | tf_op jit(solution)/shard_map/reduce_sum | solution.py:69
  78.2 0.7 bitcast_dynamic-update-slice_fusion.6
  78.9 4.2 %gather_fusion.8 = f32[2,99840]{1,0:T(2,128)S(1)} fusion(f32[16,99840]{1,0:T(8,128)} %bitcast_dynamic-update-slice_fusion.6, s32[1024]{0:T(1024)S(1)} %get-tuple-element.217), kind=kCustom, calls=%fused_computation.7.clone | custom fusion | bytes 1597448 | tf_op jit(solution)/shard_map/jit(_take)/gather | solution.py:78
  83.9 4.3 %collective-permute-start.5 = (f32[2,99968]{1,0:T(2,128)S(1)}, f32[2,99968]{1,0:T(2,128)S(1)}, u32[]{:S(2)}, u32[]{:S(2)}) collective-permute-start(f32[2,99968]{1,0:T(2,128)S(1)} %dynamic-update-slice.2), channel_id=1, source_target_pairs={{4,0},{8,4},{12,8},{16,12},{20,16},{24,20},{28,24},{32,28},{36,32}... | collective-permute-start | bytes 2399240 | tf_op jit(solution)/shard_map/ppermute | solution.py:29
  88.3 4.2 %gather_fusion.7 = f32[2,99840]{1,0:T(2,128)S(1)} fusion(f32[16,99840]{1,0:T(8,128)} %bitcast_dynamic-update-slice_fusion.6, s32[1024]{0:T(1024)S(1)} %get-tuple-element.218), kind=kCustom, calls=%fused_computation.1.clone | custom fusion | bytes 1597448 | tf_op jit(solution)/shard_map/jit(_take)/gather | solution.py:78
  93.3 1.9 %collective-permute-start.4 = (f32[2,99968]{1,0:T(2,128)S(1)}, f32[2,99968]{1,0:T(2,128)S(1)}, u32[]{:S(2)}, u32[]{:S(2)}) collective-permute-start(f32[2,99968]{1,0:T(2,128)S(1)} %dynamic-update-slice.5), channel_id=1, source_target_pairs={{0,4},{4,8},{8,12},{12,16},{16,20},{20,24},{24,28},{28,32},{32,36}... | collective-permute-start | bytes 2399240 | tf_op jit(solution)/shard_map/ppermute | solution.py:29
  95.2 2.7 %collective-permute-done.5 = f32[2,99968]{1,0:T(2,128)S(1)} collective-permute-done((f32[2,99968]{1,0:T(2,128)S(1)}, f32[2,99968]{1,0:T(2,128)S(1)}, u32[]{:S(2)}, u32[]{:S(2)}) %collective-permute-start.5) | collective-permute-done | bytes 799776 | tf_op jit(solution)/shard_map/ppermute | solution.py:29
  97.9 11.0 %collective-permute-done.4 = f32[2,99968]{1,0:T(2,128)S(1)} collective-permute-done((f32[2,99968]{1,0:T(2,128)S(1)}, f32[2,99968]{1,0:T(2,128)S(1)}, u32[]{:S(2)}, u32[]{:S(2)}) %collective-permute-start.4) | collective-permute-done | bytes 799776 | tf_op jit(solution)/shard_map/ppermute | solution.py:29
  109.2 7.5 %fusion = f32[20,99840]{1,0:T(8,128)} fusion(f32[2,99968]{1,0:T(2,128)S(1)} %collective-permute-done.5, f32[2,99968]{1,0:T(2,128)S(1)} %collective-permute-done.4, f32[16,99840]{1,0:T(8,128)} %bitcast_dynamic-update-slice_fusion.6), kind=kLoop, calls=%fused_computation.10 | loop fusion | flops 3993600 | bytes 15976448 | tf_op jit(solution)/shard_map/concatenate | solution.py:179
  116.7 11.4 %gather_fusion = f32[16,99840]{1,0:T(8,128)} fusion(f32[20,99840]{1,0:T(8,128)} %fusion, s32[1024]{0:T(1024)S(1)} %pad_clamp_fusion), kind=kCustom, calls=%fused_computation.8 | custom fusion | bytes 12779584 | tf_op jit(solution)/shard_map/jit(_take)/gather | solution.py:179
  128.0 3.3 %broadcast_select_fusion = f32[16,99840]{1,0:T(8,128)S(1)} fusion(f32[16,99840]{1,0:T(8,128)} %gather_fusion, pred[16]{0:T(512)(128)(4,1)S(1)} %compare_and_fusion.8), kind=kLoop, calls=%fused_computation.13 | loop fusion | flops 1597440 | bytes 12779536 | tf_op jit(solution)/shard_map/jit(_take)/select_n | solution.py:179
  131.4 3.1 %slice_bitcast_fusion = f32[2,8,768,128]{3,1,2,0:T(8,128)} fusion(f32[16,99840]{1,0:T(8,128)S(1)} %broadcast_select_fusion), kind=kLoop, calls=%fused_computation.12 | loop fusion | bytes 12582912
  134.5 0.6 copy.103
  135.1 0.6 copy.104
  135.7 0.6 copy.105
  136.3 0.6 copy.106
  136.9 6.7 %copy.126 = f32[2,8,768,128]{3,2,1,0:T(8,128)} copy(f32[2,8,768,128]{3,1,2,0:T(8,128)} %slice_bitcast_fusion) | data formatting | bytes 12582912
  (78 shorter events, 5.5 us)
Async XLA Ops:
  2.2 14.9 %collective-permute-start.1 = (f32[9,1,4,128]{3,2,1,0:T(4,128)S(1)}, f32[9,1,4,128]{3,2,1,0:T(4,128)S(1)}, u32[]{:S(2)}, u32[]{:S(2)}) collective-permute-start(f32[9,1,4,128]{3,2,1,0:T(4,128)S(1)} %get-tuple-element.150), channel_id=1, source_target_pairs={{4,0},{8,4},{12,8},{16,12},{20,16},{24,20},{28,24},{32,28},{36,32}... | collective-permute-start | bytes 55304 | tf_op jit(solution)/shard_map/ppermute | solution.py:21
  7.8 9.3 %collective-permute-start = (f32[9,1,4,128]{3,2,1,0:T(4,128)S(1)}, f32[9,1,4,128]{3,2,1,0:T(4,128)S(1)}, u32[]{:S(2)}, u32[]{:S(2)}) collective-permute-start(f32[9,1,4,128]{3,2,1,0:T(4,128)S(1)} %get-tuple-element.149), channel_id=1, source_target_pairs={{0,4},{4,8},{8,12},{12,16},{16,20},{20,24},{24,28},{28,32},{32,36}... | collective-permute-start | bytes 55304 | tf_op jit(solution)/shard_map/ppermute | solution.py:20
  18.0 4.9 %collective-permute-start.3 = (f32[9,6,1,128]{3,2,1,0:T(1,128)S(1)}, f32[9,6,1,128]{3,2,1,0:T(1,128)S(1)}, u32[]{:S(2)}, u32[]{:S(2)}) collective-permute-start(f32[9,6,1,128]{3,2,1,0:T(1,128)S(1)} %get-tuple-element.148), channel_id=1, source_target_pairs={{1,0},{2,1},{3,2},{5,4},{6,5},{7,6},{9,8},{10,9},{11,10},{13,12},{... | collective-permute-start | bytes 82952 | tf_op jit(solution)/shard_map/ppermute | solution.py:21
  20.6 5.8 %collective-permute-start.2 = (f32[9,6,1,128]{3,2,1,0:T(1,128)S(1)}, f32[9,6,1,128]{3,2,1,0:T(1,128)S(1)}, u32[]{:S(2)}, u32[]{:S(2)}) collective-permute-start(f32[9,6,1,128]{3,2,1,0:T(1,128)S(1)} %get-tuple-element.147), channel_id=1, source_target_pairs={{0,1},{1,2},{2,3},{4,5},{5,6},{6,7},{8,9},{9,10},{10,11},{12,13},{... | collective-permute-start | bytes 82952 | tf_op jit(solution)/shard_map/ppermute | solution.py:20
  31.5 12.3 %copy-start = (f32[4,4,6,128,128]{4,3,2,1,0:T(8,128)S(1)}, f32[4,4,6,128,128]{4,3,2,1,0:T(8,128)}, u32[]{:S(2)}) copy-start(f32[4,4,6,128,128]{4,3,2,1,0:T(8,128)} %param.18) | copy-start | bytes 18874372
  83.9 14.0 %collective-permute-start.5 = (f32[2,99968]{1,0:T(2,128)S(1)}, f32[2,99968]{1,0:T(2,128)S(1)}, u32[]{:S(2)}, u32[]{:S(2)}) collective-permute-start(f32[2,99968]{1,0:T(2,128)S(1)} %dynamic-update-slice.2), channel_id=1, source_target_pairs={{4,0},{8,4},{12,8},{16,12},{20,16},{24,20},{28,24},{32,28},{36,32}... | collective-permute-start | bytes 2399240 | tf_op jit(solution)/shard_map/ppermute | solution.py:29
  93.3 15.6 %collective-permute-start.4 = (f32[2,99968]{1,0:T(2,128)S(1)}, f32[2,99968]{1,0:T(2,128)S(1)}, u32[]{:S(2)}, u32[]{:S(2)}) collective-permute-start(f32[2,99968]{1,0:T(2,128)S(1)} %dynamic-update-slice.5), channel_id=1, source_target_pairs={{0,4},{4,8},{8,12},{12,16},{16,20},{20,24},{24,28},{28,32},{32,36}... | collective-permute-start | bytes 2399240 | tf_op jit(solution)/shard_map/ppermute | solution.py:29
where the time goes:
time: 145 us; the launch traced here: 144 us
  other arithmetic  60.4 us (42%)
  local copies, waits for them, and re-layouts  47.2 us (33%)
  starting transfers between devices  17.7 us (12%)
  waiting for transfers between devices  17.1 us (12%)
    reduce_sum x2, other arithmetic, bond_terms(): jnp.sum(factor * gap_axis, axis=2)  21.9 us
    unnamed x11, local copies, waits for them, and re-layouts  18.6 us
    unnamed x7, other arithmetic  16.1 us
    ppermute x2, waiting for transfers between devices, from_behind(): return lax.ppermute(value, axis, pairs)  13.6 us
    gather x1, local copies, waits for them, and re-layouts, per_device(): jnp.take(jnp.concatenate([own_table, incoming_rows], 0), source, axis=0)  11.4 us
    gather x2, local copies, waits for them, and re-layouts, pick_rows(): chosen = jnp.take(row_table, jnp.maximum(chosen_ids, 0), axis=0)  8.46 us
    ppermute x2, starting transfers between devices, extended(): after = lax.ppermute(first, axis, down)  8.3 us
    concatenate x1, other arithmetic, per_device(): jnp.concatenate([own_table, incoming_rows], 0)  7.47 us
  transfers between devices with their start and end apart: 6, of which 3 were waited for; matrix products, arithmetic and copies ran while one was open for 9% of the time, Pallas kernels for 0%

commit v1 on v0

v1 whole, which is shorter than its diff:
```python
import functools

import jax
import jax.numpy as jnp
import numpy as np
from jax import lax
from jax.experimental import pallas as pl
from jax.experimental.pallas import tpu as pltpu
from jax.sharding import PartitionSpec as P

STIFFNESS = 8.0
DAMPING = 0.8
TIME_STEP = 0.1
CELL_SPAN = 4.0
FALLOFF = float(-np.log2(np.e) / 9.0)
FAR = 1000.0
APART = 1.0e6

F32 = jnp.float32
MESH = pl.DeviceIdType.MESH
CW = CN = 4
CLUSTERS = CW * CN
SLOTS = 6
POINTS = 128
HALO = CN + 2
STAYS = 15
CHUNK = 32
SIDES = tuple((i, j) for i in (-1, 0, 1) for j in (-1, 0, 1) if (i, j) != (0, 0))


def sorted_four(a, b, c, d):
    lo, hi = jnp.minimum, jnp.maximum
    a, b, c, d = lo(a, b), hi(a, b), lo(c, d), hi(c, d)
    a, c, b, d = lo(a, c), hi(a, c), lo(b, d), hi(b, d)
    return (a, lo(b, c), hi(b, c), d)


def moved_ids(move_src):
    ids = [move_src[0, 0, d, m] for d in range(2) for m in range(2)]
    return sorted_four(*[jnp.where(i >= 0, i, 99) for i in ids])


def step_kernel(
    wide_size, narrow_size,
    ref_local, displacement, velocity, acceleration, critical, active, partners, move_src, move_dst, history,
    hist_rows, state_rows,
    held, table, columns, pulls, partner_rows, apart,
    load_sem, halo_send, halo_recv, hist_send, hist_recv, state_send, state_recv,
):
    me_w, me_n = lax.axis_index("wide"), lax.axis_index("narrow")
    loads = [pltpu.make_async_copy(history.at[c], held.at[c], load_sem.at[c]) for c in range(CLUSTERS)]
    for copy in loads:
        copy.start()

    def device(dw, dn):
        return (lax.rem(me_w + dw + wide_size, wide_size), lax.rem(me_n + dn + narrow_size, narrow_size))

    barrier = pltpu.get_barrier_semaphore()
    for dw, dn in SIDES:
        pl.semaphore_signal(barrier, inc=1, device_id=device(dw, dn), device_id_type=MESH)

    for a in range(CW):
        for b in range(CN):
            spot = (a + 1) * HALO + b + 1
            for d in range(3):
                r = ref_local[d, a, b:b + 1]
                v = velocity[d, a, b:b + 1]
                acc = acceleration[d, a, b:b + 1]
                u = displacement[d, a, b:b + 1] + TIME_STEP * v + 0.5 * TIME_STEP * TIME_STEP * acc
                table[spot, d:d + 1] = r
                table[spot, 3 + d:4 + d] = r + u
                table[spot, 6 + d:7 + d] = v + 0.5 * TIME_STEP * acc
                table[spot, 9 + d:10 + d] = u
            table[spot, 12:16] = jnp.zeros((4, POINTS), F32)

    pl.semaphore_wait(barrier, len(SIDES))
    halos = []
    for n, (dw, dn) in enumerate(SIDES):
        rows = range(1, CW + 1) if dw == 0 else (CW if dw > 0 else 1,)
        for m, row in enumerate(rows):
            to_row = row if dw == 0 else (0 if dw > 0 else CW + 1)
            if dn == 0:
                first, to_first, count = 1, 1, CN
            else:
                first, to_first, count = (CN, 0, 1) if dn > 0 else (1, CN + 1, 1)
            halos.append(pltpu.make_async_remote_copy(
                src_ref=table.at[pl.ds(row * HALO + first, count)],
                dst_ref=table.at[pl.ds(to_row * HALO + to_first, count)],
                send_sem=halo_send.at[n, m], recv_sem=halo_recv.at[n, m],
                device_id=device(dw, dn), device_id_type=MESH,
            ))
    for copy in halos:
        copy.start()

    sub = lax.broadcasted_iota(jnp.int32, (POINTS, POINTS), 0)
    lane = lax.broadcasted_iota(jnp.int32, (POINTS, POINTS), 1)
    apart[...] = jnp.where(sub == lane, APART, 0.0).astype(F32)

    for copy in loads:
        copy.wait()
    for copy in halos:
        copy.wait()

    def cluster(c, out, after_chunk):
        a, b = c // CN, lax.rem(c, CN)
        own = table[(a + 1) * HALO + b + 1]
        columns[...] = jnp.transpose(own)
        for k in range(SLOTS):
            o = partners[a, b, k]
            dw, dn = o // 3 - 1, lax.rem(o, 3) - 1
            gw, gn = me_w * CW + a + dw, me_n * CN + b + dn
            inside = (gw >= 0) & (gw < wide_size * CW) & (gn >= 0) & (gn < narrow_size * CN)
            on = inside & (active[a, b, k] > 0)
            other = table[(a + 1 + dw) * HALO + b + 1 + dn]
            shift = (CELL_SPAN * dw.astype(F32), CELL_SPAN * dn.astype(F32), jnp.where(on, 0.0, FAR))
            for f in range(9):
                row = other[f:f + 1]
                if f < 6:
                    row = row + shift[f % 3]
                partner_rows[k, f] = jnp.broadcast_to(row, (8, POINTS))
            limit = jnp.full((8, POINTS), critical[a, b, k], F32)
            partner_rows[k, 9] = jnp.where(on, 1.0, 0.0) / limit

        def chunk(i, carry):
            for u in range(CHUNK // 8):
                r = pl.ds(pl.multiple_of(i * CHUNK + u * 8, 8), 8)
                mine = columns[r, :]
                mine = [jnp.broadcast_to(mine[:, f:f + 1], (8, POINTS)) for f in range(9)]
                total = None
                for k in range(SLOTS):
                    q = [partner_rows[k, f] for f in range(10)]
                    x = [q[d] - mine[d] for d in range(3)]
                    e = [q[3 + d] - mine[3 + d] for d in range(3)]
                    v = [q[6 + d] - mine[6 + d] for d in range(3)]
                    rest_sq = x[0] * x[0] + x[1] * x[1] + x[2] * x[2]
                    now_sq = e[0] * e[0] + e[1] * e[1] + e[2] * e[2]
                    rate = v[0] * e[0] + v[1] * e[1] + v[2] * e[2]
                    if k == 0:
                        same = apart[r, :]
                        rest_sq = rest_sq + same
                        now_sq = now_sq + same
                    rest_inv = lax.rsqrt(rest_sq)
                    now_inv = lax.rsqrt(now_sq)
                    stretch = now_sq * now_inv * rest_inv - 1.0
                    scaled = stretch * q[9]
                    if k == 0:
                        scaled = scaled - same
                    hist = jnp.maximum(held[c, k, r, :], scaled)
                    hist_rows[out, k, r, :] = hist
                    weight = jnp.exp2(rest_sq * FALLOFF) * jnp.minimum(jnp.maximum(2.0 - hist, 0.0), 1.0)
                    factor = weight * (stretch + (DAMPING / STIFFNESS) * (rate * now_inv)) * now_inv
                    term = [factor * e[d] for d in range(3)]
                    total = term if total is None else [total[d] + term[d] for d in range(3)]
                for d in range(3):
                    pulls[r, d:d + 1] = STIFFNESS * jnp.sum(total[d], axis=1, keepdims=True)
            after_chunk(i)
            return carry

        lax.fori_loop(0, POINTS // CHUNK, chunk, 0)
        acc = jnp.transpose(pulls[...])[0:3]
        state_rows[out, 0:3] = own[0:3]
        state_rows[out, 3:6] = own[9:12]
        state_rows[out, 6:9] = own[6:9] + 0.5 * TIME_STEP * acc
        state_rows[out, 9:12] = acc

    def hist_copy(e, i):
        part = pl.ds(pl.multiple_of(i * CHUNK, 8), CHUNK)
        return pltpu.make_async_remote_copy(
            src_ref=hist_rows.at[STAYS + 4 + e, :, part, :], dst_ref=hist_rows.at[STAYS + e, :, part, :],
            send_sem=hist_send.at[e, i], recv_sem=hist_recv.at[e, i],
            device_id=device(1 - 2 * lax.rem(e, 2), 0), device_id_type=MESH,
        )

    def state_copy(e):
        return pltpu.make_async_remote_copy(
            src_ref=state_rows.at[STAYS + 4 + e], dst_ref=state_rows.at[STAYS + e],
            send_sem=state_send.at[e], recv_sem=state_recv.at[e],
            device_id=device(1 - 2 * lax.rem(e, 2), 0), device_id_type=MESH,
        )

    def hand_on(e, carry):
        d, m = lax.rem(e, 2), e // 2
        c = jnp.maximum(move_src[0, 0, d, m], 0)
        cluster(c, STAYS + 4 + e, lambda i: hist_copy(e, i).start())
        tag = jnp.full((4, POINTS), move_dst[0, 0, d, m], jnp.int32).astype(F32)
        state_rows[STAYS + 4 + e, 12:16] = tag
        state_copy(e).start()
        return carry

    lax.fori_loop(0, 4, hand_on, 0)

    moved = moved_ids(move_src)

    def stay(j, carry):
        c = j
        for m in moved:
            c = jnp.where(m <= c, c + 1, c)
        cluster(jnp.minimum(c, CLUSTERS - 1), j, lambda i: None)
        state_rows[j, 12:16] = jnp.zeros((4, POINTS), F32)
        return carry

    lax.fori_loop(0, jnp.where((me_w == 0) | (me_w == wide_size - 1), STAYS, STAYS - 1), stay, 0)

    for e in range(4):
        for i in range(POINTS // CHUNK):
            hist_copy(e, i).wait()
        state_copy(e).wait()


def place_kernel(hist_rows, state_rows, move_src, ref_out, disp_out, vel_out, acc_out, hist_out, sem):
    moved = moved_ids(move_src)
    tags = [jnp.max(state_rows[STAYS + e, 12:13, :]).astype(jnp.int32) for e in range(4)]
    copies = []
    for o in range(CLUSTERS):
        source = o
        for m in moved:
            source = jnp.where(m < o, source - 1, source)
        for e in range(4):
            source = jnp.where(tags[e] == o, STAYS + e, source)
        copies.append(pltpu.make_async_copy(hist_rows.at[source], hist_out.at[o], sem.at[o]))
        copies[-1].start()
        rows = state_rows[source]
        for f, ref in enumerate((ref_out, disp_out, vel_out, acc_out)):
            for d in range(3):
                ref[d, o // CN, o % CN:o % CN + 1] = rows[3 * f + d:3 * f + d + 1]
    for copy in copies:
        copy.wait()


def per_device(
    wide_size, narrow_size,
    ref_local, displacement, velocity, acceleration, history, critical, active, partners, move_src, move_dst,
):
    vmem, smem, anywhere = (pl.BlockSpec(memory_space=m) for m in (pltpu.VMEM, pltpu.SMEM, pl.ANY))
    total = STAYS + 8
    hist_shape, state_shape = (total, SLOTS, POINTS, POINTS), (total, 16, POINTS)
    hist_rows, state_rows = pl.pallas_call(
        functools.partial(step_kernel, wide_size, narrow_size),
        out_shape=(pltpu.VMEM(hist_shape, F32), pltpu.VMEM(state_shape, F32)),
        in_specs=[vmem] * 4 + [smem] * 5 + [anywhere],
        out_specs=(vmem, vmem),
        scratch_shapes=[
            pltpu.VMEM((CLUSTERS, SLOTS, POINTS, POINTS), F32),
            pltpu.VMEM((HALO * HALO, 16, POINTS), F32),
            pltpu.VMEM((POINTS, 16), F32),
            pltpu.VMEM((POINTS, 8), F32),
            pltpu.VMEM((SLOTS, 10, 8, POINTS), F32),
            pltpu.VMEM((POINTS, POINTS), F32),
            pltpu.SemaphoreType.DMA((CLUSTERS,)),
            pltpu.SemaphoreType.DMA((8, 4)),
            pltpu.SemaphoreType.DMA((8, 4)),
            pltpu.SemaphoreType.DMA((4, POINTS // CHUNK)),
            pltpu.SemaphoreType.DMA((4, POINTS // CHUNK)),
            pltpu.SemaphoreType.DMA((4,)),
            pltpu.SemaphoreType.DMA((4,)),
        ],
        compiler_params=pltpu.CompilerParams(
            collective_id=0, has_side_effects=True, vmem_limit_bytes=16 << 20
        ),
        name="step",
    )(
        ref_local, displacement, velocity, acceleration, critical, active, partners, move_src, move_dst,
        history.reshape(CLUSTERS, SLOTS, POINTS, POINTS),
    )
    hist_rows = pltpu.with_memory_space_constraint(hist_rows, pltpu.VMEM)
    state_rows = pltpu.with_memory_space_constraint(state_rows, pltpu.VMEM)
    state = jax.ShapeDtypeStruct(ref_local.shape, F32)
    outs = pl.pallas_call(
        place_kernel,
        out_shape=(state,) * 4 + (jax.ShapeDtypeStruct((CLUSTERS, SLOTS, POINTS, POINTS), F32),),
        in_specs=[anywhere, vmem, smem],
        out_specs=(vmem,) * 4 + (anywhere,),
        scratch_shapes=[pltpu.SemaphoreType.DMA((CLUSTERS,))],
        compiler_params=pltpu.CompilerParams(vmem_limit_bytes=8 << 20),
        name="place",
    )(hist_rows, state_rows, move_src)
    return outs[:4] + (outs[4].reshape(history.shape),)


def solution(mesh):
    field = P(None, "wide", "narrow", None)
    blocks = P("wide", "narrow", None)
    hist = P("wide", "narrow", None, None, None)
    moves = P("wide", "narrow", None, None)
    return jax.shard_map(
        functools.partial(per_device, mesh.shape["wide"], mesh.shape["narrow"]),
        mesh=mesh,
        in_specs=(field,) * 4 + (hist,) + (blocks,) * 3 + (moves,) * 2,
        out_specs=(field,) * 4 + (hist,),
        check_vma=False,
    )
```

time: 145 us -> 57.8 us (0.40)
  the two profiles are of different devices: /device:TPU:30 before, /device:TPU:0 now
where the time goes in v1:
time: 57.8 us; the launch traced here: 57.3 us
  Pallas kernels  47.4 us (82%)
  local copies, waits for them, and re-layouts  9.17 us (16%)
  between operations  0.66 us (1%)
    pallas_call x1, Pallas kernels, per_device(): pl.pallas_call(functools.partial(step_kernel, wide_size, narrow_size), ou...  43.3 us
    unnamed x20, local copies, waits for them, and re-layouts  9.17 us
    pallas_call x1, Pallas kernels, per_device(): pl.pallas_call(place_kernel, out_shape=(state,) * 4 + (jax.ShapeDtypeStru...  4.09 us

profile of v1, /device:TPU:0, one launch (start us, length us, event | category | flops | bytes accessed | tf_op | source)
XLA Modules:
  0.0 57.3 jit_solution(14268856457548556220)
XLA Ops:
  0.6 0.0 copy-start
  0.6 2.8 %copy-done = f32[4,4,6,128,128]{4,3,2,1,0:T(8,128)S(1)} copy-done((f32[4,4,6,128,128]{4,3,2,1,0:T(8,128)S(1)}, f32[4,4,6,128,128]{4,3,2,1,0:T(8,128)}, u32[]{:S(2)}) %copy-start) | copy-done | bytes 6291480
  3.4 0.0 copy-start.1
  3.4 0.7 %copy-done.1 = f32[3,4,4,128]{3,2,1,0:T(4,128)S(1)} copy-done((f32[3,4,4,128]{3,2,1,0:T(4,128)S(1)}, f32[3,4,4,128]{3,2,1,0:T(4,128)}, u32[]{:S(2)}) %copy-start.1) | copy-done | bytes 24600
  4.2 0.0 copy-start.2
  4.2 0.7 %copy-done.2 = f32[3,4,4,128]{3,2,1,0:T(4,128)S(1)} copy-done((f32[3,4,4,128]{3,2,1,0:T(4,128)S(1)}, f32[3,4,4,128]{3,2,1,0:T(4,128)}, u32[]{:S(2)}) %copy-start.2) | copy-done | bytes 24600
  4.9 0.0 copy-start.3
  4.9 0.7 %copy-done.3 = f32[3,4,4,128]{3,2,1,0:T(4,128)S(1)} copy-done((f32[3,4,4,128]{3,2,1,0:T(4,128)S(1)}, f32[3,4,4,128]{3,2,1,0:T(4,128)}, u32[]{:S(2)}) %copy-start.3) | copy-done | bytes 24600
  5.6 0.0 copy-start.4
  5.6 0.7 %copy-done.4 = f32[3,4,4,128]{3,2,1,0:T(4,128)S(1)} copy-done((f32[3,4,4,128]{3,2,1,0:T(4,128)S(1)}, f32[3,4,4,128]{3,2,1,0:T(4,128)}, u32[]{:S(2)}) %copy-start.4) | copy-done | bytes 24600
  6.4 0.0 copy-start.5
  6.4 0.7 %copy-done.5 = f32[4,4,6]{2,1,0:T(4,128)S(1)} copy-done((f32[4,4,6]{2,1,0:T(4,128)S(1)}, f32[4,4,6]{2,1,0:T(4,128)}, u32[]{:S(2)}) %copy-start.5) | copy-done | bytes 408
  7.1 0.0 copy-start.6
  7.1 0.7 %copy-done.6 = s32[4,4,6]{2,1,0:T(4,128)S(1)} copy-done((s32[4,4,6]{2,1,0:T(4,128)S(1)}, s32[4,4,6]{2,1,0:T(4,128)}, u32[]{:S(2)}) %copy-start.6) | copy-done | bytes 408
  7.8 0.0 copy-start.7
  7.8 0.7 %copy-done.7 = s32[4,4,6]{2,1,0:T(4,128)S(1)} copy-done((s32[4,4,6]{2,1,0:T(4,128)S(1)}, s32[4,4,6]{2,1,0:T(4,128)}, u32[]{:S(2)}) %copy-start.7) | copy-done | bytes 408
  8.5 0.0 copy-start.8
  8.5 0.7 %copy-done.8 = s32[1,1,2,2]{3,2,1,0:T(2,128)S(1)} copy-done((s32[1,1,2,2]{3,2,1,0:T(2,128)S(1)}, s32[1,1,2,2]{3,2,1,0:T(2,128)}, u32[]{:S(2)}) %copy-start.8) | copy-done | bytes 40
  9.1 0.0 copy-start.9
  9.1 0.7 %copy-done.9 = s32[1,1,2,2]{3,2,1,0:T(2,128)S(1)} copy-done((s32[1,1,2,2]{3,2,1,0:T(2,128)S(1)}, s32[1,1,2,2]{3,2,1,0:T(2,128)}, u32[]{:S(2)}) %copy-start.9) | copy-done | bytes 40
  9.8 43.3 %step.1 = (f32[23,6,128,128]{3,2,1,0:T(8,128)S(1)}, f32[23,16,128]{2,1,0:T(8,128)S(1)}) custom-call(f32[3,4,4,128]{3,2,1,0:T(4,128)S(1)} %copy-done.1, f32[3,4,4,128]{3,2,1,0:T(4,128)S(1)} %copy-done.2, f32[3,4,4,128]{3,2,1,0:T(4,128)S(1)} %copy-done.3, f32[3,4,4,128]{3,2,1,0:T(4,128)S(1)} %copy-done.4, f32[4,4,6]{2,1,0:T(4,128)S(1)} %copy-done.5, ...), custom_call_target="tpu_custom_call" | custom-call | tf_op jit(solution)/shard_map/step/pallas_call | solution.py:237
  53.2 4.1 %place.1 = (f32[3,4,4,128]{3,2,1,0:T(4,128)}, f32[3,4,4,128]{3,2,1,0:T(4,128)}, f32[3,4,4,128]{3,2,1,0:T(4,128)}, f32[3,4,4,128]{3,2,1,0:T(4,128)}, f32[16,6,128,128]{3,2,1,0:T(8,128)}) custom-call(f32[23,6,128,128]{3,2,1,0:T(8,128)S(1)} %get-tuple-element.12.hist_rows, f32[23,16,128]{2,1,0:T(8,128)S(1)} %get-tuple-element.13.state_rows, ...), custom_call_target="tpu_custom_call" | custom-call | tf_op jit(solution)/shard_map/place/pallas_call | solution.py:268
Async XLA Ops:
  0.6 2.8 %copy-start = (f32[4,4,6,128,128]{4,3,2,1,0:T(8,128)S(1)}, f32[4,4,6,128,128]{4,3,2,1,0:T(8,128)}, u32[]{:S(2)}) copy-start(f32[4,4,6,128,128]{4,3,2,1,0:T(8,128)} %param.14) | copy-start | bytes 18874372
  3.4 0.7 %copy-start.1 = (f32[3,4,4,128]{3,2,1,0:T(4,128)S(1)}, f32[3,4,4,128]{3,2,1,0:T(4,128)}, u32[]{:S(2)}) copy-start(f32[3,4,4,128]{3,2,1,0:T(4,128)} %ref_local.1) | copy-start | bytes 73732
  4.2 0.7 %copy-start.2 = (f32[3,4,4,128]{3,2,1,0:T(4,128)S(1)}, f32[3,4,4,128]{3,2,1,0:T(4,128)}, u32[]{:S(2)}) copy-start(f32[3,4,4,128]{3,2,1,0:T(4,128)} %displacement.1) | copy-start | bytes 73732
  4.9 0.7 %copy-start.3 = (f32[3,4,4,128]{3,2,1,0:T(4,128)S(1)}, f32[3,4,4,128]{3,2,1,0:T(4,128)}, u32[]{:S(2)}) copy-start(f32[3,4,4,128]{3,2,1,0:T(4,128)} %velocity.1) | copy-start | bytes 73732
  5.6 0.7 %copy-start.4 = (f32[3,4,4,128]{3,2,1,0:T(4,128)S(1)}, f32[3,4,4,128]{3,2,1,0:T(4,128)}, u32[]{:S(2)}) copy-start(f32[3,4,4,128]{3,2,1,0:T(4,128)} %acceleration.1) | copy-start | bytes 73732
  6.4 0.7 %copy-start.5 = (f32[4,4,6]{2,1,0:T(4,128)S(1)}, f32[4,4,6]{2,1,0:T(4,128)}, u32[]{:S(2)}) copy-start(f32[4,4,6]{2,1,0:T(4,128)} %critical.1) | copy-start | bytes 1156
  7.1 0.7 %copy-start.6 = (s32[4,4,6]{2,1,0:T(4,128)S(1)}, s32[4,4,6]{2,1,0:T(4,128)}, u32[]{:S(2)}) copy-start(s32[4,4,6]{2,1,0:T(4,128)} %active.1) | copy-start | bytes 1156
  7.8 0.7 %copy-start.7 = (s32[4,4,6]{2,1,0:T(4,128)S(1)}, s32[4,4,6]{2,1,0:T(4,128)}, u32[]{:S(2)}) copy-start(s32[4,4,6]{2,1,0:T(4,128)} %partners.1) | copy-start | bytes 1156
  8.5 0.7 %copy-start.8 = (s32[1,1,2,2]{3,2,1,0:T(2,128)S(1)}, s32[1,1,2,2]{3,2,1,0:T(2,128)}, u32[]{:S(2)}) copy-start(s32[1,1,2,2]{3,2,1,0:T(2,128)} %move_src.3) | copy-start | bytes 52
  9.1 0.7 %copy-start.9 = (s32[1,1,2,2]{3,2,1,0:T(2,128)S(1)}, s32[1,1,2,2]{3,2,1,0:T(2,128)}, u32[]{:S(2)}) copy-start(s32[1,1,2,2]{3,2,1,0:T(2,128)} %move_dst.1) | copy-start | bytes 52

commit v2 on v1

v2 whole, which is shorter than its diff:
```python
import functools

import jax
import jax.numpy as jnp
import numpy as np
from jax import lax
from jax.experimental import pallas as pl
from jax.experimental.pallas import tpu as pltpu
from jax.sharding import PartitionSpec as P

STIFFNESS = 8.0
DAMPING = 0.8
TIME_STEP = 0.1
CELL_SPAN = 4.0
FALLOFF = float(-np.log2(np.e) / 9.0)
FAR = 1024.0
APART = 1.0e6
TINY = 1.0e-12

F32 = jnp.float32
BF16 = jnp.bfloat16
MESH = pl.DeviceIdType.MESH
CW = CN = 4
CLUSTERS = CW * CN
SLOTS = 6
POINTS = 128
STAYS = 15
TILES = CLUSTERS + 20
SIDES = ((-1, 0), (1, 0), (0, -1), (0, 1), (-1, -1), (-1, 1), (1, -1), (1, 1))
SIDE_AT = (16, 20, 24, 28, 32, 33, 34, 35)
SIDE_COUNT = (4, 4, 4, 4, 1, 1, 1, 1)

ROW_R, ROW_U, ROW_V, ROW_Y, ROW_SQ, ROW_ONE = 0, 3, 6, 9, 12, 15
PARTS = ((0, 0), (1, 0), (0, 1), (1, 1), (2, 0), (0, 2))


def pairing():
    s = np.zeros((3, 96, 48), np.float32)
    for block, (q, p) in enumerate(PARTS):
        for d in range(3):
            s[0, block * 16 + ROW_R + d, p * 16 + ROW_R + d] = -2
            s[1, block * 16 + ROW_U + d, p * 16 + ROW_Y + d] = -2
            s[1, block * 16 + ROW_R + d, p * 16 + ROW_U + d] = -2
            s[2, block * 16 + ROW_Y + d, p * 16 + ROW_V + d] = -1
            s[2, block * 16 + ROW_V + d, p * 16 + ROW_Y + d] = -1
    for g in range(3):
        for part in range(3):
            s[g, PARTS.index((part, 0)) * 16 + ROW_SQ + g, ROW_ONE] = 1
            s[g, PARTS.index((0, part)) * 16 + ROW_ONE, part * 16 + ROW_SQ + g] = 1
    return s


def dot(a, b):
    return lax.dot_general(a, b, (((1,), (0,)), ((), ())), preferred_element_type=F32)


def dot_t(a, b):
    return lax.dot_general(a, b, (((1,), (1,)), ((), ())), preferred_element_type=F32)


def sorted_four(a, b, c, d):
    lo, hi = jnp.minimum, jnp.maximum
    a, b, c, d = lo(a, b), hi(a, b), lo(c, d), hi(c, d)
    a, c, b, d = lo(a, c), hi(a, c), lo(b, d), hi(b, d)
    return (a, lo(b, c), hi(b, c), d)


def moved_ids(move_src):
    ids = [move_src[0, 0, d, m] for d in range(2) for m in range(2)]
    return sorted_four(*[jnp.where(i >= 0, i, 99) for i in ids])


def tile_index(i, j):
    if 0 <= i < CW and 0 <= j < CN:
        return i * CN + j
    if 0 <= j < CN:
        return (16 if i < 0 else 20) + j
    if 0 <= i < CW:
        return (24 if j < 0 else 28) + i
    return 32 + 2 * (i > 0) + (j > 0)


def step_kernel(
    wide_size, narrow_size,
    ref_hbm, disp_hbm, vel_hbm, acc_hbm, critical_hbm, active_hbm, partners_hbm, src_hbm, dst_hbm, pairs_hbm, history,
    hist_rows, state_rows,
    held, ref_local, displacement, velocity, acceleration, critical, active, partners, move_src, move_dst, pairs, where_is,
    plain, table, leaving, split, left, forms, apart,
    small_sem, load_sem, halo_send, halo_recv, hist_send, hist_recv, state_send, state_recv,
):
    me_w, me_n = lax.axis_index("wide"), lax.axis_index("narrow")
    small = [
        pltpu.make_async_copy(source, target, small_sem.at[n])
        for n, (source, target) in enumerate((
            (ref_hbm, ref_local), (disp_hbm, displacement), (vel_hbm, velocity), (acc_hbm, acceleration),
            (pairs_hbm, pairs), (critical_hbm, critical), (active_hbm, active), (partners_hbm, partners),
            (src_hbm, move_src), (dst_hbm, move_dst),
        ))
    ]
    for copy in small:
        copy.start()
    loads = [pltpu.make_async_copy(history.at[c], held.at[c], load_sem.at[c]) for c in range(CLUSTERS)]
    for copy in loads:
        copy.start()

    def device(dw, dn):
        return (lax.rem(me_w + dw + wide_size, wide_size), lax.rem(me_n + dn + narrow_size, narrow_size))

    barrier = pltpu.get_barrier_semaphore()
    for dw, dn in SIDES:
        pl.semaphore_signal(barrier, inc=1, device_id=device(dw, dn), device_id_type=MESH)

    sub = lax.broadcasted_iota(jnp.int32, (POINTS, POINTS), 0)
    lane = lax.broadcasted_iota(jnp.int32, (POINTS, POINTS), 1)
    apart[...] = jnp.where(sub == lane, APART, 0.0).astype(F32)
    eye = jnp.where(sub == lane, 1.0, 0.0).astype(BF16)
    far_row = lax.broadcasted_iota(jnp.int32, (48, POINTS), 0)
    far = jnp.where((far_row == ROW_R) | (far_row == ROW_Y), FAR, 0.0)
    far = jnp.where(far_row == ROW_SQ, FAR * FAR, far)
    far = jnp.where(far_row == ROW_ONE, 1.0, far)
    split[TILES] = far.astype(BF16)
    for i in range(CW + 2):
        for j in range(CN + 2):
            where_is[i * (CN + 2) + j] = tile_index(i - 1, j - 1)

    for copy in small[:4]:
        copy.wait()
    column = lax.broadcasted_iota(jnp.int32, (CN, POINTS), 0)
    anchor_n = column.astype(F32) * CELL_SPAN - CELL_SPAN * CN / 2
    hop_n = jnp.where(column == 0, CELL_SPAN * CN, jnp.where(column == CN - 1, -CELL_SPAN * CN, 0.0))

    def fill(target, spots, a, up_w, up_n, fields):
        base, u, v = fields
        r = [base[0] + (CELL_SPAN * (a - CW / 2) + up_w), base[1] + (anchor_n + up_n), base[2] - CELL_SPAN]
        y = [r[d] + u[d] for d in range(3)]
        squares = [
            r[0] * r[0] + r[1] * r[1] + r[2] * r[2],
            u[0] * (r[0] + y[0]) + u[1] * (r[1] + y[1]) + u[2] * (r[2] + y[2]),
            v[0] * y[0] + v[1] * y[1] + v[2] * y[2],
        ]
        rows = r + u + v + y + squares + [jnp.ones_like(u[0])]
        for b, spot in spots:
            for f, row in enumerate(rows):
                target[spot, f:f + 1] = row[b:b + 1]

    for a in range(CW):
        base, u, v = [], [], []
        for d in range(3):
            ref = ref_local[d, a]
            speed = velocity[d, a]
            push = acceleration[d, a]
            move = displacement[d, a] + TIME_STEP * speed + 0.5 * TIME_STEP * TIME_STEP * push
            half = speed + 0.5 * TIME_STEP * push
            base.append(ref)
            u.append(move)
            v.append(half * (DAMPING / STIFFNESS))
            for b in range(CN):
                for f, row in ((d, ref), (3 + d, move), (6 + d, half)):
                    plain[a * CN + b, f:f + 1] = row[b:b + 1]
        fields = (base, u, v)
        fill(table, [(b, a * CN + b) for b in range(CN)], a, 0.0, 0.0, fields)
        fill(leaving, [(0, 24 + a - 16), (CN - 1, 28 + a - 16)], a, 0.0, hop_n, fields)
        if a in (0, CW - 1):
            hop_w = CELL_SPAN * CW if a == 0 else -CELL_SPAN * CW
            at = 0 if a == 0 else 4
            fill(leaving, [(b, at + b) for b in range(CN)], a, hop_w, 0.0, fields)
            at = 16 if a == 0 else 18
            fill(leaving, [(0, at), (CN - 1, at + 1)], a, hop_w, hop_n, fields)

    pl.semaphore_wait(barrier, len(SIDES))
    halos = []
    for n, (dw, dn) in enumerate(SIDES):
        landing = SIDE_AT[SIDES.index((-dw, -dn))]
        halos.append(pltpu.make_async_remote_copy(
            src_ref=leaving.at[pl.ds(SIDE_AT[n] - CLUSTERS, SIDE_COUNT[n])],
            dst_ref=table.at[pl.ds(landing, SIDE_COUNT[n])],
            send_sem=halo_send.at[n], recv_sem=halo_recv.at[n],
            device_id=device(dw, dn), device_id_type=MESH,
        ))
    for copy in halos:
        copy.start()

    def split_tile(t, carry):
        tile = table[t]
        high = tile.astype(BF16)
        rest = tile - high.astype(F32)
        middle = rest.astype(BF16)
        split[t, 0:16] = high
        split[t, 16:32] = middle
        split[t, 32:48] = (rest - middle.astype(F32)).astype(BF16)
        return carry

    lax.fori_loop(0, CLUSTERS, split_tile, 0)
    for copy in small[4:]:
        copy.wait()

    def left_side(c, carry):
        for g in range(3):
            rows = dot(pairs[g], split[c]).astype(BF16)
            left[c, g * POINTS:(g + 1) * POINTS, :] = dot_t(eye, rows).astype(BF16)
        return carry

    lax.fori_loop(0, CLUSTERS, left_side, 0)
    for copy in loads:
        copy.wait()
    for copy in halos:
        copy.wait()
    lax.fori_loop(CLUSTERS, TILES, split_tile, 0)

    def cluster(c, out):
        a, b = c // CN, lax.rem(c, CN)
        mine = left[c]
        tiles, inverse = [], []
        for k in range(SLOTS):
            o = partners[a, b, k]
            dw, dn = o // 3 - 1, lax.rem(o, 3) - 1
            gw, gn = me_w * CW + a + dw, me_n * CN + b + dn
            inside = (gw >= 0) & (gw < wide_size * CW) & (gn >= 0) & (gn < narrow_size * CN)
            on = inside & (active[a, b, k] > 0)
            spot = where_is[(a + 1 + dw) * (CN + 2) + b + 1 + dn]
            tiles.append(jnp.where(on, spot, TILES))
            inverse.append(jnp.where(on, 1.0, 0.0) / jnp.full((1, POINTS), critical[a, b, k], F32))
        for pair in range(SLOTS // 2):
            theirs = []
            for k in (2 * pair, 2 * pair + 1):
                tile = split[tiles[k]]
                theirs.append(jnp.concatenate([tile[q * 16:q * 16 + 16] for q, _ in PARTS], 0))
            forms[pair] = dot(mine, jnp.concatenate(theirs, 1))
        sums = None
        for k in range(SLOTS):
            pair, at = k // 2, pl.ds((k % 2) * POINTS, POINTS)
            rest_sq = forms[pair, 0:POINTS, at]
            if k == 0:
                rest_sq = rest_sq + apart[...]
            now_sq = jnp.maximum(rest_sq + forms[pair, POINTS:2 * POINTS, at], TINY)
            rate = forms[pair, 2 * POINTS:3 * POINTS, at]
            rest_inv = lax.rsqrt(rest_sq)
            now_inv = lax.rsqrt(now_sq)
            stretch = now_sq * now_inv * rest_inv - 1.0
            scaled = stretch * inverse[k]
            if k == 0:
                scaled = scaled - apart[...]
            hist = jnp.maximum(held[c, k], scaled)
            hist_rows[out, k] = hist
            weight = jnp.exp2(rest_sq * FALLOFF) * jnp.minimum(jnp.maximum(2.0 - hist, 0.0), 1.0)
            factor = weight * (stretch + rate * now_inv) * now_inv
            high = factor.astype(BF16)
            low = (factor - high.astype(F32)).astype(BF16)
            tile = split[tiles[k]]
            term = dot_t(jnp.concatenate([high, low], 1), jnp.concatenate([tile, tile], 1))
            sums = term if sums is None else sums + term
        sums = jnp.transpose(sums)
        sums = sums[0:16] + sums[16:32] + sums[32:48]
        here = table[c]
        own = plain[c]
        acc = STIFFNESS * (sums[ROW_Y:ROW_Y + 3] - here[ROW_Y:ROW_Y + 3] * sums[ROW_ONE:ROW_ONE + 1])
        state_rows[out, 0:6] = own[0:6]
        state_rows[out, 6:9] = own[6:9] + 0.5 * TIME_STEP * acc
        state_rows[out, 9:12] = acc

    def hist_copy(e):
        return pltpu.make_async_remote_copy(
            src_ref=hist_rows.at[STAYS + 4 + e], dst_ref=hist_rows.at[STAYS + e],
            send_sem=hist_send.at[e], recv_sem=hist_recv.at[e],
            device_id=device(1 - 2 * lax.rem(e, 2), 0), device_id_type=MESH,
        )

    def state_copy(e):
        return pltpu.make_async_remote_copy(
            src_ref=state_rows.at[STAYS + 4 + e], dst_ref=state_rows.at[STAYS + e],
            send_sem=state_send.at[e], recv_sem=state_recv.at[e],
            device_id=device(1 - 2 * lax.rem(e, 2), 0), device_id_type=MESH,
        )

    def hand_on(e, carry):
        d, m = lax.rem(e, 2), e // 2
        cluster(jnp.maximum(move_src[0, 0, d, m], 0), STAYS + 4 + e)
        hist_copy(e).start()
        tag = jnp.full((4, POINTS), move_dst[0, 0, d, m], jnp.int32).astype(F32)
        state_rows[STAYS + 4 + e, 12:16] = tag
        state_copy(e).start()
        return carry

    lax.fori_loop(0, 4, hand_on, 0)

    moved = moved_ids(move_src)

    def stay(j, carry):
        c = j
        for m in moved:
            c = jnp.where(m <= c, c + 1, c)
        cluster(jnp.minimum(c, CLUSTERS - 1), j)
        state_rows[j, 12:16] = jnp.zeros((4, POINTS), F32)
        return carry

    lax.fori_loop(0, jnp.where((me_w == 0) | (me_w == wide_size - 1), STAYS, STAYS - 1), stay, 0)

    for e in range(4):
        hist_copy(e).wait()
        state_copy(e).wait()


def place_kernel(hist_rows, state_rows, src_hbm, ref_out, disp_out, vel_out, acc_out, hist_out, move_src, src_sem, sem):
    ids = pltpu.make_async_copy(src_hbm, move_src, src_sem)
    ids.start()
    tags = [jnp.max(state_rows[STAYS + e, 12:13, :]).astype(jnp.int32) for e in range(4)]
    ids.wait()
    moved = moved_ids(move_src)
    copies = []
    for o in range(CLUSTERS):
        source = o
        for m in moved:
            source = jnp.where(m < o, source - 1, source)
        for e in range(4):
            source = jnp.where(tags[e] == o, STAYS + e, source)
        copies.append(pltpu.make_async_copy(hist_rows.at[source], hist_out.at[o], sem.at[o]))
        copies[-1].start()
        rows = state_rows[source]
        for f, ref in enumerate((ref_out, disp_out, vel_out, acc_out)):
            for d in range(3):
                ref[d, o // CN, o % CN:o % CN + 1] = rows[3 * f + d:3 * f + d + 1]
    for copy in copies:
        copy.wait()


def per_device(
    wide_size, narrow_size,
    ref_local, displacement, velocity, acceleration, history, critical, active, partners, move_src, move_dst,
):
    vmem, anywhere = (pl.BlockSpec(memory_space=m) for m in (pltpu.VMEM, pl.ANY))
    total = STAYS + 8
    hist_shape, state_shape = (total, SLOTS, POINTS, POINTS), (total, 16, POINTS)
    operands = [
        ref_local, displacement, velocity, acceleration, critical, active, partners, move_src, move_dst,
        jnp.asarray(pairing(), BF16), history.reshape(CLUSTERS, SLOTS, POINTS, POINTS),
    ]
    operands = [pltpu.with_memory_space_constraint(x, pltpu.HBM) for x in operands]
    hist_rows, state_rows = pl.pallas_call(
        functools.partial(step_kernel, wide_size, narrow_size),
        out_shape=(pltpu.VMEM(hist_shape, F32), pltpu.VMEM(state_shape, F32)),
        in_specs=[anywhere] * len(operands),
        out_specs=(vmem, vmem),
        scratch_shapes=[
            pltpu.VMEM((CLUSTERS, SLOTS, POINTS, POINTS), F32),
            *[pltpu.VMEM(ref_local.shape, F32)] * 4,
            pltpu.SMEM(critical.shape, F32),
            pltpu.SMEM(active.shape, jnp.int32),
            pltpu.SMEM(partners.shape, jnp.int32),
            pltpu.SMEM(move_src.shape, jnp.int32),
            pltpu.SMEM(move_dst.shape, jnp.int32),
            pltpu.VMEM((3, 96, 48), BF16),
            pltpu.SMEM(((CW + 2) * (CN + 2),), jnp.int32),
            pltpu.VMEM((CLUSTERS, 16, POINTS), F32),
            pltpu.VMEM((TILES, 16, POINTS), F32),
            pltpu.VMEM((TILES - CLUSTERS, 16, POINTS), F32),
            pltpu.VMEM((TILES + 1, 48, POINTS), BF16),
            pltpu.VMEM((CLUSTERS, 3 * POINTS, 96), BF16),
            pltpu.VMEM((SLOTS // 2, 3 * POINTS, 2 * POINTS), F32),
            pltpu.VMEM((POINTS, POINTS), F32),
            pltpu.SemaphoreType.DMA((10,)),
            pltpu.SemaphoreType.DMA((CLUSTERS,)),
            pltpu.SemaphoreType.DMA((8,)),
            pltpu.SemaphoreType.DMA((8,)),
            pltpu.SemaphoreType.DMA((4,)),
            pltpu.SemaphoreType.DMA((4,)),
            pltpu.SemaphoreType.DMA((4,)),
            pltpu.SemaphoreType.DMA((4,)),
        ],
        compiler_params=pltpu.CompilerParams(
            collective_id=0, has_side_effects=True, vmem_limit_bytes=20 << 20
        ),
        name="step",
    )(*operands)
    hist_rows = pltpu.with_memory_space_constraint(hist_rows, pltpu.VMEM)
    state_rows = pltpu.with_memory_space_constraint(state_rows, pltpu.VMEM)
    state = jax.ShapeDtypeStruct(ref_local.shape, F32)
    outs = pl.pallas_call(
        place_kernel,
        out_shape=(state,) * 4 + (jax.ShapeDtypeStruct((CLUSTERS, SLOTS, POINTS, POINTS), F32),),
        in_specs=[anywhere, vmem, anywhere],
        out_specs=(vmem,) * 4 + (anywhere,),
        scratch_shapes=[
            pltpu.SMEM(move_src.shape, jnp.int32),
            pltpu.SemaphoreType.DMA,
            pltpu.SemaphoreType.DMA((CLUSTERS,)),
        ],
        compiler_params=pltpu.CompilerParams(vmem_limit_bytes=8 << 20),
        name="place",
    )(hist_rows, state_rows, pltpu.with_memory_space_constraint(move_src, pltpu.HBM))
    return outs[:4] + (outs[4].reshape(history.shape),)


def solution(mesh):
    field = P(None, "wide", "narrow", None)
    blocks = P("wide", "narrow", None)
    hist = P("wide", "narrow", None, None, None)
    moves = P("wide", "narrow", None, None)
    return jax.shard_map(
        functools.partial(per_device, mesh.shape["wide"], mesh.shape["narrow"]),
        mesh=mesh,
        in_specs=(field,) * 4 + (hist,) + (blocks,) * 3 + (moves,) * 2,
        out_specs=(field,) * 4 + (hist,),
        check_vma=False,
    )
```

time: 57.8 us -> 35 us (0.61)
  Pallas kernels: 47.4 us -> 34.2 us
  local copies, waits for them, and re-layouts: 9.17 us -> 0 us
    pallas_call x1, Pallas kernels: 43.3 us -> 30.1 us  [per_device(): pl.pallas_call(functools.partial(step_kernel, wide_size, narrow_size), ou...]
    unnamed x20 -> x0, local copies, waits for them, and re-layouts: 9.17 us -> none
where the time goes in v2:
time: 35 us; the launch traced here: 34.8 us
  Pallas kernels  34.2 us (98%)
  between operations  0.64 us (2%)
    pallas_call x1, Pallas kernels, per_device(): pl.pallas_call(functools.partial(step_kernel, wide_size, narrow_size), ou...  30.1 us
    pallas_call x1, Pallas kernels, per_device(): pl.pallas_call(place_kernel, out_shape=(state,) * 4 + (jax.ShapeDtypeStru...  4.13 us

profile of v2, /device:TPU:0, one launch (start us, length us, event | category | flops | bytes accessed | tf_op | source)
XLA Modules:
  0.0 34.8 jit_solution(14479756446633856310)
XLA Ops:
  0.6 30.1 %step.1 = (f32[23,6,128,128]{3,2,1,0:T(8,128)S(1)}, f32[23,16,128]{2,1,0:T(8,128)S(1)}) custom-call(f32[3,4,4,128]{3,2,1,0:T(4,128)} %ref_hbm.1, f32[3,4,4,128]{3,2,1,0:T(4,128)} %disp_hbm.1, f32[3,4,4,128]{3,2,1,0:T(4,128)} %vel_hbm.1, f32[3,4,4,128]{3,2,1,0:T(4,128)} %acc_hbm.1, f32[4,4,6]{2,1,0:T(4,128)} %critical_hbm.1, s32[4,4,6]{2,1,0:T(4,128)} %active_hbm.1, ...), custom_call_target="tpu_custom_call" | custom-call | tf_op jit(solution)/shard_map/step/pallas_call | solution.py:338
  30.7 4.1 %place.1 = (f32[3,4,4,128]{3,2,1,0:T(4,128)}, f32[3,4,4,128]{3,2,1,0:T(4,128)}, f32[3,4,4,128]{3,2,1,0:T(4,128)}, f32[3,4,4,128]{3,2,1,0:T(4,128)}, f32[16,6,128,128]{3,2,1,0:T(8,128)}) custom-call(f32[23,6,128,128]{3,2,1,0:T(8,128)S(1)} %get-tuple-element.12.hist_rows, f32[23,16,128]{2,1,0:T(8,128)S(1)} %get-tuple-element.13.state_rows, s32[1,1,2,2]{3,2,1,0:T(2,128)} %src_hbm.3), custom_call_target="tpu_custom_call" | custom-call | tf_op jit(solution)/shard_map/place/pallas_call | solution.py:377

commit v3 on v2

--- a/solution.py
+++ b/solution.py
@@ -25,10 +25,11 @@
 SLOTS = 6
 POINTS = 128
 STAYS = 15
-TILES = CLUSTERS + 20
+TILES = CLUSTERS + 22
 SIDES = ((-1, 0), (1, 0), (0, -1), (0, 1), (-1, -1), (-1, 1), (1, -1), (1, 1))
-SIDE_AT = (16, 20, 24, 28, 32, 33, 34, 35)
-SIDE_COUNT = (4, 4, 4, 4, 1, 1, 1, 1)
+SIDE_AT = (16, 21, 26, 30, 34, 35, 36, 37)
+SIDE_COUNT = (5, 5, 4, 4, 1, 1, 1, 1)
+TAGS_AT = (20, 25)
 
 ROW_R, ROW_U, ROW_V, ROW_Y, ROW_SQ, ROW_ONE = 0, 3, 6, 9, 12, 15
 PARTS = ((0, 0), (1, 0), (0, 1), (1, 1), (2, 0), (0, 2))
@@ -50,6 +51,11 @@
     return s
 
 
+def around(i, size):
+    i = jnp.where(i < 0, i + size, i)
+    return jnp.where(i >= size, i - size, i)
+
+
 def dot(a, b):
     return lax.dot_general(a, b, (((1,), (0,)), ((), ())), preferred_element_type=F32)
 
@@ -74,27 +80,27 @@
     if 0 <= i < CW and 0 <= j < CN:
         return i * CN + j
     if 0 <= j < CN:
-        return (16 if i < 0 else 20) + j
+        return (16 if i < 0 else 21) + j
     if 0 <= i < CW:
-        return (24 if j < 0 else 28) + i
-    return 32 + 2 * (i > 0) + (j > 0)
+        return (26 if j < 0 else 30) + i
+    return 34 + 2 * (i > 0) + (j > 0)
 
 
 def step_kernel(
     wide_size, narrow_size,
     ref_hbm, disp_hbm, vel_hbm, acc_hbm, critical_hbm, active_hbm, partners_hbm, src_hbm, dst_hbm, pairs_hbm, history,
-    hist_rows, state_rows,
+    hist_rows, state_rows, sources,
     held, ref_local, displacement, velocity, acceleration, critical, active, partners, move_src, move_dst, pairs, where_is,
-    plain, table, leaving, split, left, forms, apart,
-    small_sem, load_sem, halo_send, halo_recv, hist_send, hist_recv, state_send, state_recv,
+    plain, table, leaving, split, left, forms, apart, tags,
+    small_sem, tag_sem, load_sem, halo_send, halo_recv, hist_send, hist_recv, state_send, state_recv,
 ):
     me_w, me_n = lax.axis_index("wide"), lax.axis_index("narrow")
     small = [
         pltpu.make_async_copy(source, target, small_sem.at[n])
         for n, (source, target) in enumerate((
             (ref_hbm, ref_local), (disp_hbm, displacement), (vel_hbm, velocity), (acc_hbm, acceleration),
-            (pairs_hbm, pairs), (critical_hbm, critical), (active_hbm, active), (partners_hbm, partners),
-            (src_hbm, move_src), (dst_hbm, move_dst),
+            (dst_hbm, move_dst), (pairs_hbm, pairs), (critical_hbm, critical), (active_hbm, active), (partners_hbm, partners),
+            (src_hbm, move_src),
         ))
     ]
     for copy in small:
@@ -104,7 +110,7 @@
         copy.start()
 
     def device(dw, dn):
-        return (lax.rem(me_w + dw + wide_size, wide_size), lax.rem(me_n + dn + narrow_size, narrow_size))
+        return (around(me_w + dw, wide_size), around(me_n + dn, narrow_size))
 
     barrier = pltpu.get_barrier_semaphore()
     for dw, dn in SIDES:
@@ -123,14 +129,23 @@
         for j in range(CN + 2):
             where_is[i * (CN + 2) + j] = tile_index(i - 1, j - 1)
 
-    for copy in small[:4]:
+    for copy in small[:5]:
         copy.wait()
     column = lax.broadcasted_iota(jnp.int32, (CN, POINTS), 0)
     anchor_n = column.astype(F32) * CELL_SPAN - CELL_SPAN * CN / 2
     hop_n = jnp.where(column == 0, CELL_SPAN * CN, jnp.where(column == CN - 1, -CELL_SPAN * CN, 0.0))
 
-    def fill(target, spots, a, up_w, up_n, fields):
-        base, u, v = fields
+    def advanced(a):
+        base, u, half, v = [], [], [], []
+        for d in range(3):
+            speed, push = velocity[d, a], acceleration[d, a]
+            base.append(ref_local[d, a])
+            u.append(displacement[d, a] + TIME_STEP * speed + 0.5 * TIME_STEP * TIME_STEP * push)
+            half.append(speed + 0.5 * TIME_STEP * push)
+            v.append(half[d] * (DAMPING / STIFFNESS))
+        return base, u, half, v
+
+    def tile_rows(a, up_w, up_n, base, u, v):
         r = [base[0] + (CELL_SPAN * (a - CW / 2) + up_w), base[1] + (anchor_n + up_n), base[2] - CELL_SPAN]
         y = [r[d] + u[d] for d in range(3)]
         squares = [
@@ -138,34 +153,26 @@
             u[0] * (r[0] + y[0]) + u[1] * (r[1] + y[1]) + u[2] * (r[2] + y[2]),
             v[0] * y[0] + v[1] * y[1] + v[2] * y[2],
         ]
-        rows = r + u + v + y + squares + [jnp.ones_like(u[0])]
-        for b, spot in spots:
-            for f, row in enumerate(rows):
-                target[spot, f:f + 1] = row[b:b + 1]
+        return r + u + v + y + squares + [jnp.ones_like(u[0])]
 
     for a in range(CW):
-        base, u, v = [], [], []
-        for d in range(3):
-            ref = ref_local[d, a]
-            speed = velocity[d, a]
-            push = acceleration[d, a]
-            move = displacement[d, a] + TIME_STEP * speed + 0.5 * TIME_STEP * TIME_STEP * push
-            half = speed + 0.5 * TIME_STEP * push
-            base.append(ref)
-            u.append(move)
-            v.append(half * (DAMPING / STIFFNESS))
-            for b in range(CN):
-                for f, row in ((d, ref), (3 + d, move), (6 + d, half)):
-                    plain[a * CN + b, f:f + 1] = row[b:b + 1]
-        fields = (base, u, v)
-        fill(table, [(b, a * CN + b) for b in range(CN)], a, 0.0, 0.0, fields)
-        fill(leaving, [(0, 24 + a - 16), (CN - 1, 28 + a - 16)], a, 0.0, hop_n, fields)
+        base, u, half, v = advanced(a)
+        for f, row in enumerate(tile_rows(a, 0.0, hop_n, base, u, v)):
+            leaving[SIDE_AT[2] - CLUSTERS + a, f:f + 1] = row[0:1]
+            leaving[SIDE_AT[3] - CLUSTERS + a, f:f + 1] = row[CN - 1:CN]
         if a in (0, CW - 1):
-            hop_w = CELL_SPAN * CW if a == 0 else -CELL_SPAN * CW
-            at = 0 if a == 0 else 4
-            fill(leaving, [(b, at + b) for b in range(CN)], a, hop_w, 0.0, fields)
-            at = 16 if a == 0 else 18
-            fill(leaving, [(0, at), (CN - 1, at + 1)], a, hop_w, hop_n, fields)
+            side, hop_w = (0, CELL_SPAN * CW) if a == 0 else (1, -CELL_SPAN * CW)
+            at = SIDE_AT[side] - CLUSTERS
+            for f, row in enumerate(tile_rows(a, hop_w, 0.0, base, u, v)):
+                leaving[at:at + CN, f] = row
+            at = SIDE_AT[4 + 2 * side] - CLUSTERS
+            for f, row in enumerate(tile_rows(a, hop_w, hop_n, base, u, v)):
+                leaving[at, f:f + 1] = row[0:1]
+                leaving[at + 1, f:f + 1] = row[CN - 1:CN]
+    for side in range(2):
+        for m in range(2):
+            tag = jnp.full((8, POINTS), move_dst[0, 0, 1 - side, m], jnp.int32).astype(F32)
+            leaving[TAGS_AT[side] - CLUSTERS, 8 * m:8 * m + 8] = tag
 
     pl.semaphore_wait(barrier, len(SIDES))
     halos = []
@@ -180,6 +187,16 @@
     for copy in halos:
         copy.start()
 
+    for a in range(CW):
+        base, u, half, v = advanced(a)
+        here = pl.ds(a * CN, CN)
+        for f, row in enumerate(base + u + half):
+            plain[here, f] = row
+        for f in range(9, 16):
+            plain[here, f] = jnp.zeros((CN, POINTS), F32)
+        for f, row in enumerate(tile_rows(a, 0.0, 0.0, base, u, v)):
+            table[here, f] = row
+
     def split_tile(t, carry):
         tile = table[t]
         high = tile.astype(BF16)
@@ -190,8 +207,8 @@
         split[t, 32:48] = (rest - middle.astype(F32)).astype(BF16)
         return carry
 
-    lax.fori_loop(0, CLUSTERS, split_tile, 0)
-    for copy in small[4:]:
+    lax.fori_loop(0, CLUSTERS, split_tile, 0, unroll=4)
+    for copy in small[5:]:
         copy.wait()
 
     def left_side(c, carry):
@@ -200,12 +217,17 @@
             left[c, g * POINTS:(g + 1) * POINTS, :] = dot_t(eye, rows).astype(BF16)
         return carry
 
-    lax.fori_loop(0, CLUSTERS, left_side, 0)
+    lax.fori_loop(0, CLUSTERS, left_side, 0, unroll=4)
     for copy in loads:
         copy.wait()
     for copy in halos:
         copy.wait()
-    lax.fori_loop(CLUSTERS, TILES, split_tile, 0)
+    tag_copies = [
+        pltpu.make_async_copy(table.at[TAGS_AT[side]], tags.at[side], tag_sem.at[side]) for side in range(2)
+    ]
+    for copy in tag_copies:
+        copy.start()
+    lax.fori_loop(CLUSTERS, TILES, split_tile, 0, unroll=2)
 
     def cluster(c, out):
         a, b = c // CN, lax.rem(c, CN)
@@ -257,6 +279,7 @@
         state_rows[out, 0:6] = own[0:6]
         state_rows[out, 6:9] = own[6:9] + 0.5 * TIME_STEP * acc
         state_rows[out, 9:12] = acc
+        state_rows[out, 12:16] = own[12:16]
 
     def hist_copy(e):
         return pltpu.make_async_remote_copy(
@@ -276,8 +299,6 @@
         d, m = lax.rem(e, 2), e // 2
         cluster(jnp.maximum(move_src[0, 0, d, m], 0), STAYS + 4 + e)
         hist_copy(e).start()
-        tag = jnp.full((4, POINTS), move_dst[0, 0, d, m], jnp.int32).astype(F32)
-        state_rows[STAYS + 4 + e, 12:16] = tag
         state_copy(e).start()
         return carry
 
@@ -290,35 +311,38 @@
         for m in moved:
             c = jnp.where(m <= c, c + 1, c)
         cluster(jnp.minimum(c, CLUSTERS - 1), j)
-        state_rows[j, 12:16] = jnp.zeros((4, POINTS), F32)
         return carry
 
     lax.fori_loop(0, jnp.where((me_w == 0) | (me_w == wide_size - 1), STAYS, STAYS - 1), stay, 0)
 
-    for e in range(4):
-        hist_copy(e).wait()
-        state_copy(e).wait()
-
-
-def place_kernel(hist_rows, state_rows, src_hbm, ref_out, disp_out, vel_out, acc_out, hist_out, move_src, src_sem, sem):
-    ids = pltpu.make_async_copy(src_hbm, move_src, src_sem)
-    ids.start()
-    tags = [jnp.max(state_rows[STAYS + e, 12:13, :]).astype(jnp.int32) for e in range(4)]
-    ids.wait()
-    moved = moved_ids(move_src)
-    copies = []
+    for copy in tag_copies:
+        copy.wait()
     for o in range(CLUSTERS):
         source = o
         for m in moved:
             source = jnp.where(m < o, source - 1, source)
         for e in range(4):
-            source = jnp.where(tags[e] == o, STAYS + e, source)
-        copies.append(pltpu.make_async_copy(hist_rows.at[source], hist_out.at[o], sem.at[o]))
+            source = jnp.where(tags[e % 2, 8 * (e // 2), 0] == float(o), STAYS + e, source)
+        sources[o] = source
+
+    for e in range(4):
+        hist_copy(e).wait()
+        state_copy(e).wait()
+
+
+def place_kernel(hist_rows, state_rows, sources, ref_out, disp_out, vel_out, acc_out, hist_out, states, state_sem, sem):
+    copies = []
+    for o in range(CLUSTERS):
+        copies.append(pltpu.make_async_copy(hist_rows.at[sources[o]], hist_out.at[o], sem.at[o]))
         copies[-1].start()
-        rows = state_rows[source]
-        for f, ref in enumerate((ref_out, disp_out, vel_out, acc_out)):
+    for o in range(CLUSTERS):
+        rows = state_rows[sources[o]]
+        for f in range(4):
             for d in range(3):
-                ref[d, o // CN, o % CN:o % CN + 1] = rows[3 * f + d:3 * f + d + 1]
+                states[f, d, o // CN, o % CN:o % CN + 1] = rows[3 * f + d:3 * f + d + 1]
+    for f, ref in enumerate((ref_out, disp_out, vel_out, acc_out)):
+        copies.append(pltpu.make_async_copy(states.at[f], ref, state_sem.at[f]))
+        copies[-1].start()
     for copy in copies:
         copy.wait()
 
@@ -327,7 +351,7 @@
     wide_size, narrow_size,
     ref_local, displacement, velocity, acceleration, history, critical, active, partners, move_src, move_dst,
 ):
-    vmem, anywhere = (pl.BlockSpec(memory_space=m) for m in (pltpu.VMEM, pl.ANY))
+    vmem, smem, anywhere = (pl.BlockSpec(memory_space=m) for m in (pltpu.VMEM, pltpu.SMEM, pl.ANY))
     total = STAYS + 8
     hist_shape, state_shape = (total, SLOTS, POINTS, POINTS), (total, 16, POINTS)
     operands = [
@@ -335,11 +359,11 @@
         jnp.asarray(pairing(), BF16), history.reshape(CLUSTERS, SLOTS, POINTS, POINTS),
     ]
     operands = [pltpu.with_memory_space_constraint(x, pltpu.HBM) for x in operands]
-    hist_rows, state_rows = pl.pallas_call(
+    hist_rows, state_rows, sources = pl.pallas_call(
         functools.partial(step_kernel, wide_size, narrow_size),
-        out_shape=(pltpu.VMEM(hist_shape, F32), pltpu.VMEM(state_shape, F32)),
+        out_shape=(pltpu.VMEM(hist_shape, F32), pltpu.VMEM(state_shape, F32), pltpu.SMEM((CLUSTERS,), jnp.int32)),
         in_specs=[anywhere] * len(operands),
-        out_specs=(vmem, vmem),
+        out_specs=(vmem, vmem, smem),
         scratch_shapes=[
             pltpu.VMEM((CLUSTERS, SLOTS, POINTS, POINTS), F32),
             *[pltpu.VMEM(ref_local.shape, F32)] * 4,
@@ -357,7 +381,9 @@
             pltpu.VMEM((CLUSTERS, 3 * POINTS, 96), BF16),
             pltpu.VMEM((SLOTS // 2, 3 * POINTS, 2 * POINTS), F32),
             pltpu.VMEM((POINTS, POINTS), F32),
+            pltpu.SMEM((2, 16, POINTS), F32),
             pltpu.SemaphoreType.DMA((10,)),
+            pltpu.SemaphoreType.DMA((2,)),
             pltpu.SemaphoreType.DMA((CLUSTERS,)),
             pltpu.SemaphoreType.DMA((8,)),
             pltpu.SemaphoreType.DMA((8,)),
@@ -373,20 +399,21 @@
     )(*operands)
     hist_rows = pltpu.with_memory_space_constraint(hist_rows, pltpu.VMEM)
     state_rows = pltpu.with_memory_space_constraint(state_rows, pltpu.VMEM)
+    sources = pltpu.with_memory_space_constraint(sources, pltpu.SMEM)
     state = jax.ShapeDtypeStruct(ref_local.shape, F32)
     outs = pl.pallas_call(
         place_kernel,
         out_shape=(state,) * 4 + (jax.ShapeDtypeStruct((CLUSTERS, SLOTS, POINTS, POINTS), F32),),
-        in_specs=[anywhere, vmem, anywhere],
-        out_specs=(vmem,) * 4 + (anywhere,),
+        in_specs=[anywhere, vmem, smem],
+        out_specs=(anywhere,) * 5,
         scratch_shapes=[
-            pltpu.SMEM(move_src.shape, jnp.int32),
-            pltpu.SemaphoreType.DMA,
+            pltpu.VMEM((4,) + ref_local.shape, F32),
+            pltpu.SemaphoreType.DMA((4,)),
             pltpu.SemaphoreType.DMA((CLUSTERS,)),
         ],
         compiler_params=pltpu.CompilerParams(vmem_limit_bytes=8 << 20),
         name="place",
-    )(hist_rows, state_rows, pltpu.with_memory_space_constraint(move_src, pltpu.HBM))
+    )(hist_rows, state_rows, sources)
     return outs[:4] + (outs[4].reshape(history.shape),)
 
 

time: 35 us -> 31 us (0.89)
  Pallas kernels: 34.2 us -> 30.2 us
    pallas_call x1, Pallas kernels: 30.1 us -> 27.4 us  [per_device(): pl.pallas_call(functools.partial(step_kernel, wide_size, narrow_size), ou...]
    pallas_call x1, Pallas kernels: 4.13 us -> 2.86 us  [per_device(): pl.pallas_call(place_kernel, out_shape=(state,) * 4 + (jax.ShapeDtypeStru...]
where the time goes in v3:
time: 31 us; the launch traced here: 30.9 us
  Pallas kernels  30.2 us (97%)
  between operations  0.64 us (2%)
    pallas_call x1, Pallas kernels, per_device(): pl.pallas_call(functools.partial(step_kernel, wide_size, narrow_size), ou...  27.4 us
    pallas_call x1, Pallas kernels, per_device(): pl.pallas_call(place_kernel, out_shape=(state,) * 4 + (jax.ShapeDtypeStru...  2.86 us

profile of v3, /device:TPU:0, one launch (start us, length us, event | category | flops | bytes accessed | tf_op | source)
XLA Modules:
  0.0 30.9 jit_solution(15934644723083568580)
XLA Ops:
  0.6 27.4 %step.1 = (f32[23,6,128,128]{3,2,1,0:T(8,128)S(1)}, f32[23,16,128]{2,1,0:T(8,128)S(1)}, s32[16]{0:T(128)S(4)}) custom-call(f32[3,4,4,128]{3,2,1,0:T(4,128)} %ref_hbm.1, f32[3,4,4,128]{3,2,1,0:T(4,128)} %disp_hbm.1, f32[3,4,4,128]{3,2,1,0:T(4,128)} %vel_hbm.1, f32[3,4,4,128]{3,2,1,0:T(4,128)} %acc_hbm.1, f32[4,4,6]{2,1,0:T(4,128)} %critical_hbm.1, ...), custom_call_target="tpu_custom_call" | custom-call | tf_op jit(solution)/shard_map/step/pallas_call | solution.py:362
  28.0 2.9 %place.1 = (f32[3,4,4,128]{3,2,1,0:T(4,128)}, f32[3,4,4,128]{3,2,1,0:T(4,128)}, f32[3,4,4,128]{3,2,1,0:T(4,128)}, f32[3,4,4,128]{3,2,1,0:T(4,128)}, f32[16,6,128,128]{3,2,1,0:T(8,128)}) custom-call(f32[23,6,128,128]{3,2,1,0:T(8,128)S(1)} %get-tuple-element.13.hist_rows, f32[23,16,128]{2,1,0:T(8,128)S(1)} %get-tuple-element.14.state_rows, ...), custom_call_target="tpu_custom_call" | custom-call | tf_op jit(solution)/shard_map/place/pallas_call | solution.py:404

commit v4 on v3

--- a/solution.py
+++ b/solution.py
@@ -24,14 +24,14 @@
 CLUSTERS = CW * CN
 SLOTS = 6
 POINTS = 128
-STAYS = 15
 TILES = CLUSTERS + 22
 SIDES = ((-1, 0), (1, 0), (0, -1), (0, 1), (-1, -1), (-1, 1), (1, -1), (1, 1))
 SIDE_AT = (16, 21, 26, 30, 34, 35, 36, 37)
 SIDE_COUNT = (5, 5, 4, 4, 1, 1, 1, 1)
 TAGS_AT = (20, 25)
 
-ROW_R, ROW_U, ROW_V, ROW_Y, ROW_SQ, ROW_ONE = 0, 3, 6, 9, 12, 15
+ROW_R, ROW_U, ROW_V, ROW_Y, ROW_SQ, ROW_ONE = 0, 3, 8, 11, (6, 7, 14), 15
+PACK_ROWS = 16 + 8 * SLOTS + 8
 PARTS = ((0, 0), (1, 0), (0, 1), (1, 1), (2, 0), (0, 2))
 
 
@@ -46,8 +46,8 @@
             s[2, block * 16 + ROW_V + d, p * 16 + ROW_Y + d] = -1
     for g in range(3):
         for part in range(3):
-            s[g, PARTS.index((part, 0)) * 16 + ROW_SQ + g, ROW_ONE] = 1
-            s[g, PARTS.index((0, part)) * 16 + ROW_ONE, part * 16 + ROW_SQ + g] = 1
+            s[g, PARTS.index((part, 0)) * 16 + ROW_SQ[g], ROW_ONE] = 1
+            s[g, PARTS.index((0, part)) * 16 + ROW_ONE, part * 16 + ROW_SQ[g]] = 1
     return s
 
 
@@ -62,18 +62,6 @@
 
 def dot_t(a, b):
     return lax.dot_general(a, b, (((1,), (1,)), ((), ())), preferred_element_type=F32)
-
-
-def sorted_four(a, b, c, d):
-    lo, hi = jnp.minimum, jnp.maximum
-    a, b, c, d = lo(a, b), hi(a, b), lo(c, d), hi(c, d)
-    a, c, b, d = lo(a, c), hi(a, c), lo(b, d), hi(b, d)
-    return (a, lo(b, c), hi(b, c), d)
-
-
-def moved_ids(move_src):
-    ids = [move_src[0, 0, d, m] for d in range(2) for m in range(2)]
-    return sorted_four(*[jnp.where(i >= 0, i, 99) for i in ids])
 
 
 def tile_index(i, j):
@@ -89,10 +77,10 @@
 def step_kernel(
     wide_size, narrow_size,
     ref_hbm, disp_hbm, vel_hbm, acc_hbm, critical_hbm, active_hbm, partners_hbm, src_hbm, dst_hbm, pairs_hbm, history,
-    hist_rows, state_rows, sources,
+    hist_rows, state_rows, state_in, sources,
     held, ref_local, displacement, velocity, acceleration, critical, active, partners, move_src, move_dst, pairs, where_is,
-    plain, table, leaving, split, left, forms, apart, tags,
-    small_sem, tag_sem, load_sem, halo_send, halo_recv, hist_send, hist_recv, state_send, state_recv,
+    plain, table, leaving, split, left, forms, apart, tags, raw, pack, packed, sent_state,
+    small_sem, tag_sem, load_sem, halo_send, halo_recv, hist_send, hist_recv, pack_send, pack_recv, state_send, state_recv,
 ):
     me_w, me_n = lax.axis_index("wide"), lax.axis_index("narrow")
     small = [
@@ -120,11 +108,10 @@
     lane = lax.broadcasted_iota(jnp.int32, (POINTS, POINTS), 1)
     apart[...] = jnp.where(sub == lane, APART, 0.0).astype(F32)
     eye = jnp.where(sub == lane, 1.0, 0.0).astype(BF16)
-    far_row = lax.broadcasted_iota(jnp.int32, (48, POINTS), 0)
-    far = jnp.where((far_row == ROW_R) | (far_row == ROW_Y), FAR, 0.0)
-    far = jnp.where(far_row == ROW_SQ, FAR * FAR, far)
-    far = jnp.where(far_row == ROW_ONE, 1.0, far)
-    split[TILES] = far.astype(BF16)
+    row = lax.broadcasted_iota(jnp.int32, (16, POINTS), 0)
+    far = jnp.where((row == ROW_R) | (row == ROW_Y), FAR, 0.0)
+    far = jnp.where(row == ROW_SQ[0], FAR * FAR, far)
+    table[TILES] = jnp.where(row == ROW_ONE, 1.0, far)
     for i in range(CW + 2):
         for j in range(CN + 2):
             where_is[i * (CN + 2) + j] = tile_index(i - 1, j - 1)
@@ -153,7 +140,7 @@
             u[0] * (r[0] + y[0]) + u[1] * (r[1] + y[1]) + u[2] * (r[2] + y[2]),
             v[0] * y[0] + v[1] * y[1] + v[2] * y[2],
         ]
-        return r + u + v + y + squares + [jnp.ones_like(u[0])]
+        return r + u + squares[:2] + v + y + squares[2:] + [jnp.ones_like(u[0])]
 
     for a in range(CW):
         base, u, half, v = advanced(a)
@@ -197,19 +184,58 @@
         for f, row in enumerate(tile_rows(a, 0.0, 0.0, base, u, v)):
             table[here, f] = row
 
-    def split_tile(t, carry):
-        tile = table[t]
+    def split_parts(tile):
         high = tile.astype(BF16)
         rest = tile - high.astype(F32)
         middle = rest.astype(BF16)
-        split[t, 0:16] = high
-        split[t, 16:32] = middle
-        split[t, 32:48] = (rest - middle.astype(F32)).astype(BF16)
-        return carry
-
-    lax.fori_loop(0, CLUSTERS, split_tile, 0, unroll=4)
+        return high, middle, (rest - middle.astype(F32)).astype(BF16)
+
+    def split_tile(t, carry):
+        for n, part in enumerate(split_parts(table[t])):
+            split[t, n * 16:n * 16 + 16] = part
+        return carry
+
+    def toward(e):
+        return device(1 - 2 * lax.rem(e, 2), 0)
+
+    def hist_copy(e):
+        return pltpu.make_async_remote_copy(
+            src_ref=raw.at[e], dst_ref=hist_rows.at[CLUSTERS + e], send_sem=hist_send.at[e], recv_sem=hist_recv.at[e],
+            device_id=toward(e), device_id_type=MESH,
+        )
+
+    def pack_copy(e):
+        return pltpu.make_async_remote_copy(
+            src_ref=pack.at[e], dst_ref=packed.at[e], send_sem=pack_send.at[e], recv_sem=pack_recv.at[e],
+            device_id=toward(e), device_id_type=MESH,
+        )
+
+    def state_copy(e):
+        return pltpu.make_async_remote_copy(
+            src_ref=sent_state.at[e], dst_ref=state_in.at[e],
+            send_sem=state_send.at[e], recv_sem=state_recv.at[e],
+            device_id=toward(e), device_id_type=MESH,
+        )
+
+    def leaver(e):
+        return jnp.maximum(move_src[0, 0, lax.rem(e, 2), e // 2], 0)
+
     for copy in small[5:]:
         copy.wait()
+    for copy in loads:
+        copy.wait()
+
+    def send_hist(e, carry):
+        c = leaver(e)
+        for k in range(SLOTS):
+            raw[e, k] = held[c, k]
+        hist_copy(e).start()
+        return carry
+
+    lax.fori_loop(0, 4, send_hist, 0)
+
+    lax.fori_loop(0, CLUSTERS, split_tile, 0, unroll=4)
+    split_tile(TILES, 0)
 
     def left_side(c, carry):
         for g in range(3):
@@ -218,20 +244,9 @@
         return carry
 
     lax.fori_loop(0, CLUSTERS, left_side, 0, unroll=4)
-    for copy in loads:
-        copy.wait()
-    for copy in halos:
-        copy.wait()
-    tag_copies = [
-        pltpu.make_async_copy(table.at[TAGS_AT[side]], tags.at[side], tag_sem.at[side]) for side in range(2)
-    ]
-    for copy in tag_copies:
-        copy.start()
-    lax.fori_loop(CLUSTERS, TILES, split_tile, 0, unroll=2)
-
-    def cluster(c, out):
+
+    def partner_tiles(c):
         a, b = c // CN, lax.rem(c, CN)
-        mine = left[c]
         tiles, inverse = [], []
         for k in range(SLOTS):
             o = partners[a, b, k]
@@ -242,11 +257,16 @@
             spot = where_is[(a + 1 + dw) * (CN + 2) + b + 1 + dn]
             tiles.append(jnp.where(on, spot, TILES))
             inverse.append(jnp.where(on, 1.0, 0.0) / jnp.full((1, POINTS), critical[a, b, k], F32))
+        return tiles, inverse
+
+    def right_side(tile):
+        return jnp.concatenate([tile[q * 16:q * 16 + 16] for q, _ in PARTS], 0)
+
+    def cluster(c):
+        mine = left[c]
+        tiles, inverse = partner_tiles(c)
         for pair in range(SLOTS // 2):
-            theirs = []
-            for k in (2 * pair, 2 * pair + 1):
-                tile = split[tiles[k]]
-                theirs.append(jnp.concatenate([tile[q * 16:q * 16 + 16] for q, _ in PARTS], 0))
+            theirs = [right_side(split[tiles[k]]) for k in (2 * pair, 2 * pair + 1)]
             forms[pair] = dot(mine, jnp.concatenate(theirs, 1))
         sums = None
         for k in range(SLOTS):
@@ -263,7 +283,7 @@
             if k == 0:
                 scaled = scaled - apart[...]
             hist = jnp.maximum(held[c, k], scaled)
-            hist_rows[out, k] = hist
+            hist_rows[c, k] = hist
             weight = jnp.exp2(rest_sq * FALLOFF) * jnp.minimum(jnp.maximum(2.0 - hist, 0.0), 1.0)
             factor = weight * (stretch + rate * now_inv) * now_inv
             high = factor.astype(BF16)
@@ -276,67 +296,101 @@
         here = table[c]
         own = plain[c]
         acc = STIFFNESS * (sums[ROW_Y:ROW_Y + 3] - here[ROW_Y:ROW_Y + 3] * sums[ROW_ONE:ROW_ONE + 1])
-        state_rows[out, 0:6] = own[0:6]
-        state_rows[out, 6:9] = own[6:9] + 0.5 * TIME_STEP * acc
-        state_rows[out, 9:12] = acc
-        state_rows[out, 12:16] = own[12:16]
-
-    def hist_copy(e):
-        return pltpu.make_async_remote_copy(
-            src_ref=hist_rows.at[STAYS + 4 + e], dst_ref=hist_rows.at[STAYS + e],
-            send_sem=hist_send.at[e], recv_sem=hist_recv.at[e],
-            device_id=device(1 - 2 * lax.rem(e, 2), 0), device_id_type=MESH,
-        )
-
-    def state_copy(e):
-        return pltpu.make_async_remote_copy(
-            src_ref=state_rows.at[STAYS + 4 + e], dst_ref=state_rows.at[STAYS + e],
-            send_sem=state_send.at[e], recv_sem=state_recv.at[e],
-            device_id=device(1 - 2 * lax.rem(e, 2), 0), device_id_type=MESH,
-        )
-
-    def hand_on(e, carry):
-        d, m = lax.rem(e, 2), e // 2
-        cluster(jnp.maximum(move_src[0, 0, d, m], 0), STAYS + 4 + e)
-        hist_copy(e).start()
+        state_rows[c, 0:6] = own[0:6]
+        state_rows[c, 6:9] = own[6:9] + 0.5 * TIME_STEP * acc
+        state_rows[c, 9:12] = acc
+        state_rows[c, 12:16] = own[12:16]
+
+    tag_copies = [
+        pltpu.make_async_copy(table.at[TAGS_AT[side]], tags.at[side], tag_sem.at[side]) for side in range(2)
+    ]
+
+    def send_pack(e, carry):
+        c = leaver(e)
+        tiles, inverse = partner_tiles(c)
+        pack[e, 0:16] = table[c]
+        for k in range(SLOTS):
+            pack[e, 16 + 8 * k:24 + 8 * k] = table[tiles[k], 0:8]
+            pack[e, 16 + 8 * SLOTS + k:17 + 8 * SLOTS + k] = inverse[k]
+        pack[e, 16 + 9 * SLOTS:PACK_ROWS] = jnp.zeros((8 - SLOTS, POINTS), F32)
+        pack_copy(e).start()
+        return carry
+
+    def one(i, carry):
+        @pl.when(i == 4)
+        def _():
+            for copy in halos:
+                copy.wait()
+            for copy in tag_copies:
+                copy.start()
+            lax.fori_loop(CLUSTERS, TILES, split_tile, 0, unroll=2)
+            lax.fori_loop(0, 4, send_pack, 0)
+
+        inner = 5 + lax.rem(i, 2) + 4 * (i // 2)
+        side = 4 + 4 * ((i - 8) // 2) + 3 * lax.rem(i, 2)
+        c = jnp.where(i < 4, inner, jnp.where(i < 8, i - 4, jnp.where(i < 12, side, i)))
+        cluster(c)
+        return carry
+
+    lax.fori_loop(0, CLUSTERS, one, 0)
+
+    def send_state(e, carry):
+        sent_state[e] = state_rows[leaver(e)]
         state_copy(e).start()
         return carry
 
-    lax.fori_loop(0, 4, hand_on, 0)
-
-    moved = moved_ids(move_src)
-
-    def stay(j, carry):
-        c = j
-        for m in moved:
-            c = jnp.where(m <= c, c + 1, c)
-        cluster(jnp.minimum(c, CLUSTERS - 1), j)
-        return carry
-
-    lax.fori_loop(0, jnp.where((me_w == 0) | (me_w == wide_size - 1), STAYS, STAYS - 1), stay, 0)
+    lax.fori_loop(0, 4, send_state, 0)
+
+    tail = jnp.where(lax.broadcasted_iota(jnp.int32, (8, POINTS), 0) == ROW_ONE - 8, 1.0, 0.0)
+
+    def arrive(e, carry):
+        pack_copy(e).wait()
+        own = jnp.concatenate(split_parts(packed[e, 0:16]), 0)
+        mine = []
+        for g in range(2):
+            mine.append(dot_t(eye, dot(pairs[g], own).astype(BF16)).astype(BF16))
+        mine = jnp.concatenate(mine, 0)
+        for pair in range(SLOTS // 2):
+            theirs = []
+            for k in (2 * pair, 2 * pair + 1):
+                tile = jnp.concatenate([packed[e, 16 + 8 * k:24 + 8 * k], tail], 0)
+                theirs.append(right_side(jnp.concatenate(split_parts(tile), 0)))
+            forms[pair, 0:2 * POINTS] = dot(mine, jnp.concatenate(theirs, 1))
+        hist_copy(e).wait()
+        for k in range(SLOTS):
+            pair, at = k // 2, pl.ds((k % 2) * POINTS, POINTS)
+            rest_sq = forms[pair, 0:POINTS, at]
+            if k == 0:
+                rest_sq = rest_sq + apart[...]
+            now_sq = jnp.maximum(rest_sq + forms[pair, POINTS:2 * POINTS, at], TINY)
+            stretch = now_sq * lax.rsqrt(now_sq) * lax.rsqrt(rest_sq) - 1.0
+            scaled = stretch * packed[e, 16 + 8 * SLOTS + k:17 + 8 * SLOTS + k]
+            if k == 0:
+                scaled = scaled - apart[...]
+            hist_rows[CLUSTERS + e, k] = jnp.maximum(hist_rows[CLUSTERS + e, k], scaled)
+        return carry
+
+    lax.fori_loop(0, 4, arrive, 0)
 
     for copy in tag_copies:
         copy.wait()
     for o in range(CLUSTERS):
         source = o
-        for m in moved:
-            source = jnp.where(m < o, source - 1, source)
         for e in range(4):
-            source = jnp.where(tags[e % 2, 8 * (e // 2), 0] == float(o), STAYS + e, source)
+            source = jnp.where(tags[e % 2, 8 * (e // 2), 0] == float(o), CLUSTERS + e, source)
         sources[o] = source
-
     for e in range(4):
-        hist_copy(e).wait()
         state_copy(e).wait()
 
 
-def place_kernel(hist_rows, state_rows, sources, ref_out, disp_out, vel_out, acc_out, hist_out, states, state_sem, sem):
+def place_kernel(hist_rows, state_rows, state_in, sources, ref_out, disp_out, vel_out, acc_out, hist_out, states, state_sem, sem):
     copies = []
     for o in range(CLUSTERS):
         copies.append(pltpu.make_async_copy(hist_rows.at[sources[o]], hist_out.at[o], sem.at[o]))
         copies[-1].start()
     for o in range(CLUSTERS):
-        rows = state_rows[sources[o]]
+        source = sources[o]
+        rows = jnp.where(source < CLUSTERS, state_rows[o], state_in[jnp.maximum(source - CLUSTERS, 0)])
         for f in range(4):
             for d in range(3):
                 states[f, d, o // CN, o % CN:o % CN + 1] = rows[3 * f + d:3 * f + d + 1]
@@ -352,18 +406,23 @@
     ref_local, displacement, velocity, acceleration, history, critical, active, partners, move_src, move_dst,
 ):
     vmem, smem, anywhere = (pl.BlockSpec(memory_space=m) for m in (pltpu.VMEM, pltpu.SMEM, pl.ANY))
-    total = STAYS + 8
-    hist_shape, state_shape = (total, SLOTS, POINTS, POINTS), (total, 16, POINTS)
+    total = CLUSTERS + 4
+    hist_shape = (total, SLOTS, POINTS, POINTS)
     operands = [
         ref_local, displacement, velocity, acceleration, critical, active, partners, move_src, move_dst,
         jnp.asarray(pairing(), BF16), history.reshape(CLUSTERS, SLOTS, POINTS, POINTS),
     ]
     operands = [pltpu.with_memory_space_constraint(x, pltpu.HBM) for x in operands]
-    hist_rows, state_rows, sources = pl.pallas_call(
+    hist_rows, state_rows, state_in, sources = pl.pallas_call(
         functools.partial(step_kernel, wide_size, narrow_size),
-        out_shape=(pltpu.VMEM(hist_shape, F32), pltpu.VMEM(state_shape, F32), pltpu.SMEM((CLUSTERS,), jnp.int32)),
+        out_shape=(
+            pltpu.VMEM(hist_shape, F32),
+            pltpu.VMEM((CLUSTERS, 16, POINTS), F32),
+            pltpu.VMEM((4, 16, POINTS), F32),
+            pltpu.SMEM((CLUSTERS,), jnp.int32),
+        ),
         in_specs=[anywhere] * len(operands),
-        out_specs=(vmem, vmem, smem),
+        out_specs=(vmem, vmem, vmem, smem),
         scratch_shapes=[
             pltpu.VMEM((CLUSTERS, SLOTS, POINTS, POINTS), F32),
             *[pltpu.VMEM(ref_local.shape, F32)] * 4,
@@ -375,22 +434,23 @@
             pltpu.VMEM((3, 96, 48), BF16),
             pltpu.SMEM(((CW + 2) * (CN + 2),), jnp.int32),
             pltpu.VMEM((CLUSTERS, 16, POINTS), F32),
-            pltpu.VMEM((TILES, 16, POINTS), F32),
+            pltpu.VMEM((TILES + 1, 16, POINTS), F32),
             pltpu.VMEM((TILES - CLUSTERS, 16, POINTS), F32),
             pltpu.VMEM((TILES + 1, 48, POINTS), BF16),
             pltpu.VMEM((CLUSTERS, 3 * POINTS, 96), BF16),
             pltpu.VMEM((SLOTS // 2, 3 * POINTS, 2 * POINTS), F32),
             pltpu.VMEM((POINTS, POINTS), F32),
             pltpu.SMEM((2, 16, POINTS), F32),
+            pltpu.VMEM((4, SLOTS, POINTS, POINTS), F32),
+            pltpu.VMEM((4, PACK_ROWS, POINTS), F32),
+            pltpu.VMEM((4, PACK_ROWS, POINTS), F32),
+            pltpu.VMEM((4, 16, POINTS), F32),
             pltpu.SemaphoreType.DMA((10,)),
             pltpu.SemaphoreType.DMA((2,)),
             pltpu.SemaphoreType.DMA((CLUSTERS,)),
             pltpu.SemaphoreType.DMA((8,)),
             pltpu.SemaphoreType.DMA((8,)),
-            pltpu.SemaphoreType.DMA((4,)),
-            pltpu.SemaphoreType.DMA((4,)),
-            pltpu.SemaphoreType.DMA((4,)),
-            pltpu.SemaphoreType.DMA((4,)),
+            *[pltpu.SemaphoreType.DMA((4,))] * 6,
         ],
         compiler_params=pltpu.CompilerParams(
             collective_id=0, has_side_effects=True, vmem_limit_bytes=20 << 20
@@ -399,12 +459,13 @@
     )(*operands)
     hist_rows = pltpu.with_memory_space_constraint(hist_rows, pltpu.VMEM)
     state_rows = pltpu.with_memory_space_constraint(state_rows, pltpu.VMEM)
+    state_in = pltpu.with_memory_space_constraint(state_in, pltpu.VMEM)
     sources = pltpu.with_memory_space_constraint(sources, pltpu.SMEM)
     state = jax.ShapeDtypeStruct(ref_local.shape, F32)
     outs = pl.pallas_call(
         place_kernel,
         out_shape=(state,) * 4 + (jax.ShapeDtypeStruct((CLUSTERS, SLOTS, POINTS, POINTS), F32),),
-        in_specs=[anywhere, vmem, smem],
+        in_specs=[anywhere, vmem, vmem, smem],
         out_specs=(anywhere,) * 5,
         scratch_shapes=[
             pltpu.VMEM((4,) + ref_local.shape, F32),
@@ -413,7 +474,7 @@
         ],
         compiler_params=pltpu.CompilerParams(vmem_limit_bytes=8 << 20),
         name="place",
-    )(hist_rows, state_rows, sources)
+    )(hist_rows, state_rows, state_in, sources)
     return outs[:4] + (outs[4].reshape(history.shape),)
 
 

time: 31 us -> 32.2 us (1.039)
  Pallas kernels: 30.2 us -> 31.4 us
    pallas_call x1, Pallas kernels: 27.4 us -> 28.6 us  [per_device(): pl.pallas_call(functools.partial(step_kernel, wide_size, narrow_size), ou...]
where the time goes in v4:
time: 32.2 us; the launch traced here: 32.1 us
  Pallas kernels  31.4 us (98%)
  between operations  0.64 us (2%)
    pallas_call x1, Pallas kernels, per_device(): pl.pallas_call(functools.partial(step_kernel, wide_size, narrow_size), ou...  28.6 us
    pallas_call x1, Pallas kernels, per_device(): pl.pallas_call(place_kernel, out_shape=(state,) * 4 + (jax.ShapeDtypeStru...  2.85 us

profile of v4, /device:TPU:0, one launch (start us, length us, event | category | flops | bytes accessed | tf_op | source)
XLA Modules:
  0.0 32.1 jit_solution(8945549075151007774)
XLA Ops:
  0.6 28.6 %step.1 = (f32[20,6,128,128]{3,2,1,0:T(8,128)S(1)}, f32[16,16,128]{2,1,0:T(8,128)S(1)}, f32[4,16,128]{2,1,0:T(8,128)S(1)}, s32[16]{0:T(128)S(4)}) custom-call(f32[3,4,4,128]{3,2,1,0:T(4,128)} %ref_hbm.1, f32[3,4,4,128]{3,2,1,0:T(4,128)} %disp_hbm.1, f32[3,4,4,128]{3,2,1,0:T(4,128)} %vel_hbm.1, f32[3,4,4,128]{3,2,1,0:T(4,128)} %acc_hbm.1, ...), custom_call_target="tpu_custom_call" | custom-call | tf_op jit(solution)/shard_map/step/pallas_call | solution.py:416
  29.2 2.8 %place.1 = (f32[3,4,4,128]{3,2,1,0:T(4,128)}, f32[3,4,4,128]{3,2,1,0:T(4,128)}, f32[3,4,4,128]{3,2,1,0:T(4,128)}, f32[3,4,4,128]{3,2,1,0:T(4,128)}, f32[16,6,128,128]{3,2,1,0:T(8,128)}) custom-call(f32[20,6,128,128]{3,2,1,0:T(8,128)S(1)} %get-tuple-element.14.hist_rows, f32[16,16,128]{2,1,0:T(8,128)S(1)} %get-tuple-element.15.state_rows, ...), custom_call_target="tpu_custom_call" | custom-call | tf_op jit(solution)/shard_map/place/pallas_call | solution.py:465

commit v5 on v4

--- a/solution.py
+++ b/solution.py
@@ -79,7 +79,7 @@
     ref_hbm, disp_hbm, vel_hbm, acc_hbm, critical_hbm, active_hbm, partners_hbm, src_hbm, dst_hbm, pairs_hbm, history,
     hist_rows, state_rows, state_in, sources,
     held, ref_local, displacement, velocity, acceleration, critical, active, partners, move_src, move_dst, pairs, where_is,
-    plain, table, leaving, split, left, forms, apart, tags, raw, pack, packed, sent_state,
+    plain, table, leaving, split, left, forms, forms_in, apart, tags, raw, pack, packed, sent_state,
     small_sem, tag_sem, load_sem, halo_send, halo_recv, hist_send, hist_recv, pack_send, pack_recv, state_send, state_recv,
 ):
     me_w, me_n = lax.axis_index("wide"), lax.axis_index("narrow")
@@ -114,7 +114,16 @@
     table[TILES] = jnp.where(row == ROW_ONE, 1.0, far)
     for i in range(CW + 2):
         for j in range(CN + 2):
-            where_is[i * (CN + 2) + j] = tile_index(i - 1, j - 1)
+            edges = [
+                edge for out, edge in (
+                    (i == 0, me_w == 0), (i == CW + 1, me_w == wide_size - 1),
+                    (j == 0, me_n == 0), (j == CN + 1, me_n == narrow_size - 1),
+                ) if out
+            ]
+            spot = tile_index(i - 1, j - 1)
+            for edge in edges:
+                spot = jnp.where(edge, TILES, spot)
+            where_is[i * (CN + 2) + j] = spot
 
     for copy in small[:5]:
         copy.wait()
@@ -222,6 +231,17 @@
 
     for copy in small[5:]:
         copy.wait()
+    lax.fori_loop(0, CLUSTERS, split_tile, 0, unroll=4)
+    split_tile(TILES, 0)
+
+    def left_side(c, carry):
+        for g in range(3):
+            rows = dot(pairs[g], split[c]).astype(BF16)
+            left[c, g * POINTS:(g + 1) * POINTS, :] = dot_t(eye, rows).astype(BF16)
+        return carry
+
+    lax.fori_loop(0, CLUSTERS, left_side, 0, unroll=4)
+
     for copy in loads:
         copy.wait()
 
@@ -234,63 +254,57 @@
 
     lax.fori_loop(0, 4, send_hist, 0)
 
-    lax.fori_loop(0, CLUSTERS, split_tile, 0, unroll=4)
-    split_tile(TILES, 0)
-
-    def left_side(c, carry):
-        for g in range(3):
-            rows = dot(pairs[g], split[c]).astype(BF16)
-            left[c, g * POINTS:(g + 1) * POINTS, :] = dot_t(eye, rows).astype(BF16)
-        return carry
-
-    lax.fori_loop(0, CLUSTERS, left_side, 0, unroll=4)
-
-    def partner_tiles(c):
-        a, b = c // CN, lax.rem(c, CN)
-        tiles, inverse = [], []
-        for k in range(SLOTS):
-            o = partners[a, b, k]
-            dw, dn = o // 3 - 1, lax.rem(o, 3) - 1
-            gw, gn = me_w * CW + a + dw, me_n * CN + b + dn
-            inside = (gw >= 0) & (gw < wide_size * CW) & (gn >= 0) & (gn < narrow_size * CN)
-            on = inside & (active[a, b, k] > 0)
-            spot = where_is[(a + 1 + dw) * (CN + 2) + b + 1 + dn]
-            tiles.append(jnp.where(on, spot, TILES))
-            inverse.append(jnp.where(on, 1.0, 0.0) / jnp.full((1, POINTS), critical[a, b, k], F32))
-        return tiles, inverse
+    def place_of(c):
+        a = lax.shift_right_logical(c, 2)
+        return a, c - CN * a
+
+    def partner(c, k):
+        a, b = place_of(c)
+        o = partners[a, b, k]
+        third = lax.shift_right_logical(o * 11, 5)
+        spot = where_is[(CN + 2) * (a + third) + b + o - 3 * third]
+        return jnp.where(active[a, b, k] > 0, spot, TILES)
+
+    def inverse_limit(c, k, spot):
+        a, b = place_of(c)
+        return jnp.where(spot == TILES, 0.0, 1.0) / jnp.full((1, POINTS), critical[a, b, k], F32)
 
     def right_side(tile):
         return jnp.concatenate([tile[q * 16:q * 16 + 16] for q, _ in PARTS], 0)
 
-    def cluster(c):
-        mine = left[c]
-        tiles, inverse = partner_tiles(c)
+    def prepare(c, buffer, pair):
+        theirs = [right_side(split[partner(c, k)]) for k in (2 * pair, 2 * pair + 1)]
+        forms[buffer, pair] = dot(left[c], jnp.concatenate(theirs, 1))
+
+    def pull(c, buffer, k):
+        pair, at = k // 2, pl.ds((k % 2) * POINTS, POINTS)
+        spot = partner(c, k)
+        rest_sq = forms[buffer, pair, 0:POINTS, at]
+        if k == 0:
+            rest_sq = rest_sq + apart[...]
+        now_sq = jnp.maximum(rest_sq + forms[buffer, pair, POINTS:2 * POINTS, at], TINY)
+        rate = forms[buffer, pair, 2 * POINTS:3 * POINTS, at]
+        now_inv = lax.rsqrt(now_sq)
+        stretch = now_sq * now_inv * lax.rsqrt(rest_sq) - 1.0
+        scaled = stretch * inverse_limit(c, k, spot)
+        if k == 0:
+            scaled = scaled - apart[...]
+        hist = jnp.maximum(held[c, k], scaled)
+        hist_rows[c, k] = hist
+        weight = jnp.exp2(rest_sq * FALLOFF) * jnp.minimum(jnp.maximum(2.0 - hist, 0.0), 1.0)
+        factor = weight * (stretch + rate * now_inv) * now_inv
+        high = factor.astype(BF16)
+        low = (factor - high.astype(F32)).astype(BF16)
+        tile = split[spot]
+        return dot_t(jnp.concatenate([high, low], 1), jnp.concatenate([tile, tile], 1))
+
+    def cluster(c, buffer, after, after_buffer):
+        sums = None
         for pair in range(SLOTS // 2):
-            theirs = [right_side(split[tiles[k]]) for k in (2 * pair, 2 * pair + 1)]
-            forms[pair] = dot(mine, jnp.concatenate(theirs, 1))
-        sums = None
-        for k in range(SLOTS):
-            pair, at = k // 2, pl.ds((k % 2) * POINTS, POINTS)
-            rest_sq = forms[pair, 0:POINTS, at]
-            if k == 0:
-                rest_sq = rest_sq + apart[...]
-            now_sq = jnp.maximum(rest_sq + forms[pair, POINTS:2 * POINTS, at], TINY)
-            rate = forms[pair, 2 * POINTS:3 * POINTS, at]
-            rest_inv = lax.rsqrt(rest_sq)
-            now_inv = lax.rsqrt(now_sq)
-            stretch = now_sq * now_inv * rest_inv - 1.0
-            scaled = stretch * inverse[k]
-            if k == 0:
-                scaled = scaled - apart[...]
-            hist = jnp.maximum(held[c, k], scaled)
-            hist_rows[c, k] = hist
-            weight = jnp.exp2(rest_sq * FALLOFF) * jnp.minimum(jnp.maximum(2.0 - hist, 0.0), 1.0)
-            factor = weight * (stretch + rate * now_inv) * now_inv
-            high = factor.astype(BF16)
-            low = (factor - high.astype(F32)).astype(BF16)
-            tile = split[tiles[k]]
-            term = dot_t(jnp.concatenate([high, low], 1), jnp.concatenate([tile, tile], 1))
-            sums = term if sums is None else sums + term
+            prepare(after, after_buffer, pair)
+            for k in (2 * pair, 2 * pair + 1):
+                term = pull(c, buffer, k)
+                sums = term if sums is None else sums + term
         sums = jnp.transpose(sums)
         sums = sums[0:16] + sums[16:32] + sums[32:48]
         here = table[c]
@@ -307,17 +321,25 @@
 
     def send_pack(e, carry):
         c = leaver(e)
-        tiles, inverse = partner_tiles(c)
         pack[e, 0:16] = table[c]
         for k in range(SLOTS):
-            pack[e, 16 + 8 * k:24 + 8 * k] = table[tiles[k], 0:8]
-            pack[e, 16 + 8 * SLOTS + k:17 + 8 * SLOTS + k] = inverse[k]
+            spot = partner(c, k)
+            pack[e, 16 + 8 * k:24 + 8 * k] = table[spot, 0:8]
+            pack[e, 16 + 8 * SLOTS + k:17 + 8 * SLOTS + k] = inverse_limit(c, k, spot)
         pack[e, 16 + 9 * SLOTS:PACK_ROWS] = jnp.zeros((8 - SLOTS, POINTS), F32)
         pack_copy(e).start()
         return carry
 
-    def one(i, carry):
-        @pl.when(i == 4)
+    def nth(i):
+        inner = 5 + lax.rem(i, 2) + 4 * (i // 2)
+        side = 4 + 4 * ((i - 8) // 2) + 3 * lax.rem(i, 2)
+        return jnp.where(i < 4, inner, jnp.where(i < 8, i - 4, jnp.where(i < 12, side, i)))
+
+    for pair in range(SLOTS // 2):
+        prepare(nth(0), 0, pair)
+
+    def two(i, carry):
+        @pl.when(i == 1)
         def _():
             for copy in halos:
                 copy.wait()
@@ -326,13 +348,12 @@
             lax.fori_loop(CLUSTERS, TILES, split_tile, 0, unroll=2)
             lax.fori_loop(0, 4, send_pack, 0)
 
-        inner = 5 + lax.rem(i, 2) + 4 * (i // 2)
-        side = 4 + 4 * ((i - 8) // 2) + 3 * lax.rem(i, 2)
-        c = jnp.where(i < 4, inner, jnp.where(i < 8, i - 4, jnp.where(i < 12, side, i)))
-        cluster(c)
-        return carry
-
-    lax.fori_loop(0, CLUSTERS, one, 0)
+        first, second = nth(2 * i), nth(2 * i + 1)
+        cluster(first, 0, second, 1)
+        cluster(second, 1, nth(jnp.minimum(2 * i + 2, CLUSTERS - 1)), 0)
+        return carry
+
+    lax.fori_loop(0, CLUSTERS // 2, two, 0)
 
     def send_state(e, carry):
         sent_state[e] = state_rows[leaver(e)]
@@ -343,34 +364,19 @@
 
     tail = jnp.where(lax.broadcasted_iota(jnp.int32, (8, POINTS), 0) == ROW_ONE - 8, 1.0, 0.0)
 
-    def arrive(e, carry):
+    def expect(e, carry):
         pack_copy(e).wait()
         own = jnp.concatenate(split_parts(packed[e, 0:16]), 0)
-        mine = []
-        for g in range(2):
-            mine.append(dot_t(eye, dot(pairs[g], own).astype(BF16)).astype(BF16))
-        mine = jnp.concatenate(mine, 0)
+        mine = jnp.concatenate([dot_t(eye, dot(pairs[g], own).astype(BF16)).astype(BF16) for g in range(2)], 0)
         for pair in range(SLOTS // 2):
             theirs = []
             for k in (2 * pair, 2 * pair + 1):
                 tile = jnp.concatenate([packed[e, 16 + 8 * k:24 + 8 * k], tail], 0)
                 theirs.append(right_side(jnp.concatenate(split_parts(tile), 0)))
-            forms[pair, 0:2 * POINTS] = dot(mine, jnp.concatenate(theirs, 1))
-        hist_copy(e).wait()
-        for k in range(SLOTS):
-            pair, at = k // 2, pl.ds((k % 2) * POINTS, POINTS)
-            rest_sq = forms[pair, 0:POINTS, at]
-            if k == 0:
-                rest_sq = rest_sq + apart[...]
-            now_sq = jnp.maximum(rest_sq + forms[pair, POINTS:2 * POINTS, at], TINY)
-            stretch = now_sq * lax.rsqrt(now_sq) * lax.rsqrt(rest_sq) - 1.0
-            scaled = stretch * packed[e, 16 + 8 * SLOTS + k:17 + 8 * SLOTS + k]
-            if k == 0:
-                scaled = scaled - apart[...]
-            hist_rows[CLUSTERS + e, k] = jnp.maximum(hist_rows[CLUSTERS + e, k], scaled)
-        return carry
-
-    lax.fori_loop(0, 4, arrive, 0)
+            forms_in[e, pair] = dot(mine, jnp.concatenate(theirs, 1))
+        return carry
+
+    lax.fori_loop(0, 4, expect, 0)
 
     for copy in tag_copies:
         copy.wait()
@@ -379,6 +385,24 @@
         for e in range(4):
             source = jnp.where(tags[e % 2, 8 * (e // 2), 0] == float(o), CLUSTERS + e, source)
         sources[o] = source
+
+    def arrive(e, carry):
+        hist_copy(e).wait()
+        for k in range(SLOTS):
+            pair, at = k // 2, pl.ds((k % 2) * POINTS, POINTS)
+            rest_sq = forms_in[e, pair, 0:POINTS, at]
+            if k == 0:
+                rest_sq = rest_sq + apart[...]
+            now_sq = jnp.maximum(rest_sq + forms_in[e, pair, POINTS:2 * POINTS, at], TINY)
+            stretch = now_sq * lax.rsqrt(now_sq) * lax.rsqrt(rest_sq) - 1.0
+            scaled = stretch * packed[e, 16 + 8 * SLOTS + k:17 + 8 * SLOTS + k]
+            if k == 0:
+                scaled = scaled - apart[...]
+            hist_rows[CLUSTERS + e, k] = jnp.maximum(hist_rows[CLUSTERS + e, k], scaled)
+        return carry
+
+    lax.fori_loop(0, 4, arrive, 0)
+
     for e in range(4):
         state_copy(e).wait()
 
@@ -438,7 +462,8 @@
             pltpu.VMEM((TILES - CLUSTERS, 16, POINTS), F32),
             pltpu.VMEM((TILES + 1, 48, POINTS), BF16),
             pltpu.VMEM((CLUSTERS, 3 * POINTS, 96), BF16),
-            pltpu.VMEM((SLOTS // 2, 3 * POINTS, 2 * POINTS), F32),
+            pltpu.VMEM((2, SLOTS // 2, 3 * POINTS, 2 * POINTS), F32),
+            pltpu.VMEM((4, SLOTS // 2, 2 * POINTS, 2 * POINTS), F32),
             pltpu.VMEM((POINTS, POINTS), F32),
             pltpu.SMEM((2, 16, POINTS), F32),
             pltpu.VMEM((4, SLOTS, POINTS, POINTS), F32),
@@ -453,7 +478,7 @@
             *[pltpu.SemaphoreType.DMA((4,))] * 6,
         ],
         compiler_params=pltpu.CompilerParams(
-            collective_id=0, has_side_effects=True, vmem_limit_bytes=20 << 20
+            collective_id=0, has_side_effects=True, vmem_limit_bytes=26 << 20
         ),
         name="step",
     )(*operands)

time: 32.2 us -> 31.1 us (0.966)
  Pallas kernels: 31.4 us -> 30.4 us
    pallas_call x1, Pallas kernels: 28.6 us -> 27.5 us  [per_device(): pl.pallas_call(functools.partial(step_kernel, wide_size, narrow_size), ou...]
where the time goes in v5:
time: 31.1 us; the launch traced here: 31 us
  Pallas kernels  30.4 us (98%)
  between operations  0.64 us (2%)
    pallas_call x1, Pallas kernels, per_device(): pl.pallas_call(functools.partial(step_kernel, wide_size, narrow_size), ou...  27.5 us
    pallas_call x1, Pallas kernels, per_device(): pl.pallas_call(place_kernel, out_shape=(state,) * 4 + (jax.ShapeDtypeStru...  2.85 us

profile of v5, /device:TPU:0, one launch (start us, length us, event | category | flops | bytes accessed | tf_op | source)
XLA Modules:
  0.0 31.0 jit_solution(16343746272350654716)
XLA Ops:
  0.6 27.5 %step.1 = (f32[20,6,128,128]{3,2,1,0:T(8,128)S(1)}, f32[16,16,128]{2,1,0:T(8,128)S(1)}, f32[4,16,128]{2,1,0:T(8,128)S(1)}, s32[16]{0:T(128)S(4)}) custom-call(f32[3,4,4,128]{3,2,1,0:T(4,128)} %ref_hbm.1, f32[3,4,4,128]{3,2,1,0:T(4,128)} %disp_hbm.1, f32[3,4,4,128]{3,2,1,0:T(4,128)} %vel_hbm.1, f32[3,4,4,128]{3,2,1,0:T(4,128)} %acc_hbm.1, ...), custom_call_target="tpu_custom_call" | custom-call | tf_op jit(solution)/shard_map/step/pallas_call | solution.py:440
  28.2 2.8 %place.1 = (f32[3,4,4,128]{3,2,1,0:T(4,128)}, f32[3,4,4,128]{3,2,1,0:T(4,128)}, f32[3,4,4,128]{3,2,1,0:T(4,128)}, f32[3,4,4,128]{3,2,1,0:T(4,128)}, f32[16,6,128,128]{3,2,1,0:T(8,128)}) custom-call(f32[20,6,128,128]{3,2,1,0:T(8,128)S(1)} %get-tuple-element.14.hist_rows, f32[16,16,128]{2,1,0:T(8,128)S(1)} %get-tuple-element.15.state_rows, ...), custom_call_target="tpu_custom_call" | custom-call | tf_op jit(solution)/shard_map/place/pallas_call | solution.py:490

commit v6 on v5

--- a/solution.py
+++ b/solution.py
@@ -36,7 +36,7 @@
 
 
 def pairing():
-    s = np.zeros((3, 96, 48), np.float32)
+    s = np.zeros((3, 128, 48), np.float32)
     for block, (q, p) in enumerate(PARTS):
         for d in range(3):
             s[0, block * 16 + ROW_R + d, p * 16 + ROW_R + d] = -2
@@ -48,7 +48,7 @@
         for part in range(3):
             s[g, PARTS.index((part, 0)) * 16 + ROW_SQ[g], ROW_ONE] = 1
             s[g, PARTS.index((0, part)) * 16 + ROW_ONE, part * 16 + ROW_SQ[g]] = 1
-    return s
+    return s.reshape(3 * 128, 48).T
 
 
 def around(i, size):
@@ -107,7 +107,6 @@
     sub = lax.broadcasted_iota(jnp.int32, (POINTS, POINTS), 0)
     lane = lax.broadcasted_iota(jnp.int32, (POINTS, POINTS), 1)
     apart[...] = jnp.where(sub == lane, APART, 0.0).astype(F32)
-    eye = jnp.where(sub == lane, 1.0, 0.0).astype(BF16)
     row = lax.broadcasted_iota(jnp.int32, (16, POINTS), 0)
     far = jnp.where((row == ROW_R) | (row == ROW_Y), FAR, 0.0)
     far = jnp.where(row == ROW_SQ[0], FAR * FAR, far)
@@ -234,10 +233,13 @@
     lax.fori_loop(0, CLUSTERS, split_tile, 0, unroll=4)
     split_tile(TILES, 0)
 
+    def left_rows(parts, count):
+        turned = jnp.transpose(parts.astype(F32)).astype(BF16)
+        wide = dot(turned, pairs[:, 0:count * POINTS]).astype(BF16)
+        return jnp.concatenate([wide[:, g * POINTS:(g + 1) * POINTS] for g in range(count)], 0)
+
     def left_side(c, carry):
-        for g in range(3):
-            rows = dot(pairs[g], split[c]).astype(BF16)
-            left[c, g * POINTS:(g + 1) * POINTS, :] = dot_t(eye, rows).astype(BF16)
+        left[c] = left_rows(split[c], 3)
         return carry
 
     lax.fori_loop(0, CLUSTERS, left_side, 0, unroll=4)
@@ -252,7 +254,7 @@
         hist_copy(e).start()
         return carry
 
-    lax.fori_loop(0, 4, send_hist, 0)
+    lax.fori_loop(0, 2, send_hist, 0)
 
     def place_of(c):
         a = lax.shift_right_logical(c, 2)
@@ -274,7 +276,7 @@
 
     def prepare(c, buffer, pair):
         theirs = [right_side(split[partner(c, k)]) for k in (2 * pair, 2 * pair + 1)]
-        forms[buffer, pair] = dot(left[c], jnp.concatenate(theirs, 1))
+        forms[buffer, pair] = dot(left[c, :, 0:96], jnp.concatenate(theirs, 1))
 
     def pull(c, buffer, k):
         pair, at = k // 2, pl.ds((k % 2) * POINTS, POINTS)
@@ -347,6 +349,7 @@
                 copy.start()
             lax.fori_loop(CLUSTERS, TILES, split_tile, 0, unroll=2)
             lax.fori_loop(0, 4, send_pack, 0)
+            lax.fori_loop(2, 4, send_hist, 0)
 
         first, second = nth(2 * i), nth(2 * i + 1)
         cluster(first, 0, second, 1)
@@ -367,7 +370,7 @@
     def expect(e, carry):
         pack_copy(e).wait()
         own = jnp.concatenate(split_parts(packed[e, 0:16]), 0)
-        mine = jnp.concatenate([dot_t(eye, dot(pairs[g], own).astype(BF16)).astype(BF16) for g in range(2)], 0)
+        mine = left_rows(own, 2)[:, 0:96]
         for pair in range(SLOTS // 2):
             theirs = []
             for k in (2 * pair, 2 * pair + 1):
@@ -376,7 +379,7 @@
             forms_in[e, pair] = dot(mine, jnp.concatenate(theirs, 1))
         return carry
 
-    lax.fori_loop(0, 4, expect, 0)
+    lax.fori_loop(0, 4, expect, 0, unroll=2)
 
     for copy in tag_copies:
         copy.wait()
@@ -455,13 +458,13 @@
             pltpu.SMEM(partners.shape, jnp.int32),
             pltpu.SMEM(move_src.shape, jnp.int32),
             pltpu.SMEM(move_dst.shape, jnp.int32),
-            pltpu.VMEM((3, 96, 48), BF16),
+            pltpu.VMEM((48, 3 * POINTS), BF16),
             pltpu.SMEM(((CW + 2) * (CN + 2),), jnp.int32),
             pltpu.VMEM((CLUSTERS, 16, POINTS), F32),
             pltpu.VMEM((TILES + 1, 16, POINTS), F32),
             pltpu.VMEM((TILES - CLUSTERS, 16, POINTS), F32),
             pltpu.VMEM((TILES + 1, 48, POINTS), BF16),
-            pltpu.VMEM((CLUSTERS, 3 * POINTS, 96), BF16),
+            pltpu.VMEM((CLUSTERS, 3 * POINTS, 128), BF16),
             pltpu.VMEM((2, SLOTS // 2, 3 * POINTS, 2 * POINTS), F32),
             pltpu.VMEM((4, SLOTS // 2, 2 * POINTS, 2 * POINTS), F32),
             pltpu.VMEM((POINTS, POINTS), F32),

time: 31.1 us -> 27.3 us (0.88)
  Pallas kernels: 30.4 us -> 26.5 us
    pallas_call x1, Pallas kernels: 27.5 us -> 23.7 us  [per_device(): pl.pallas_call(functools.partial(step_kernel, wide_size, narrow_size), ou...]
where the time goes in v6:
time: 27.3 us; the launch traced here: 27.2 us
  Pallas kernels  26.5 us (97%)
  between operations  0.64 us (2%)
    pallas_call x1, Pallas kernels, per_device(): pl.pallas_call(functools.partial(step_kernel, wide_size, narrow_size), ou...  23.7 us
    pallas_call x1, Pallas kernels, per_device(): pl.pallas_call(place_kernel, out_shape=(state,) * 4 + (jax.ShapeDtypeStru...  2.85 us

profile of v6, /device:TPU:0, one launch (start us, length us, event | category | flops | bytes accessed | tf_op | source)
XLA Modules:
  0.0 27.2 jit_solution(18413243034868636021)
XLA Ops:
  0.6 23.7 %step.1 = (f32[20,6,128,128]{3,2,1,0:T(8,128)S(1)}, f32[16,16,128]{2,1,0:T(8,128)S(1)}, f32[4,16,128]{2,1,0:T(8,128)S(1)}, s32[16]{0:T(128)S(4)}) custom-call(f32[3,4,4,128]{3,2,1,0:T(4,128)} %ref_hbm.1, f32[3,4,4,128]{3,2,1,0:T(4,128)} %disp_hbm.1, f32[3,4,4,128]{3,2,1,0:T(4,128)} %vel_hbm.1, f32[3,4,4,128]{3,2,1,0:T(4,128)} %acc_hbm.1, ...), custom_call_target="tpu_custom_call" | custom-call | tf_op jit(solution)/shard_map/step/pallas_call | solution.py:443
  24.3 2.8 %place.1 = (f32[3,4,4,128]{3,2,1,0:T(4,128)}, f32[3,4,4,128]{3,2,1,0:T(4,128)}, f32[3,4,4,128]{3,2,1,0:T(4,128)}, f32[3,4,4,128]{3,2,1,0:T(4,128)}, f32[16,6,128,128]{3,2,1,0:T(8,128)}) custom-call(f32[20,6,128,128]{3,2,1,0:T(8,128)S(1)} %get-tuple-element.14.hist_rows, f32[16,16,128]{2,1,0:T(8,128)S(1)} %get-tuple-element.15.state_rows, ...), custom_call_target="tpu_custom_call" | custom-call | tf_op jit(solution)/shard_map/place/pallas_call | solution.py:493

commit v7 on v6

--- a/solution.py
+++ b/solution.py
@@ -78,10 +78,11 @@
     wide_size, narrow_size,
     ref_hbm, disp_hbm, vel_hbm, acc_hbm, critical_hbm, active_hbm, partners_hbm, src_hbm, dst_hbm, pairs_hbm, history,
     hist_rows, state_rows, state_in, sources,
-    held, ref_local, displacement, velocity, acceleration, critical, active, partners, move_src, move_dst, pairs, where_is,
+    held_0, held_1, held_2, held_3, held_4, held_5, ref_local, displacement, velocity, acceleration, critical, active, partners, move_src, move_dst, pairs, where_is,
     plain, table, leaving, split, left, forms, forms_in, apart, tags, raw, pack, packed, sent_state,
     small_sem, tag_sem, load_sem, halo_send, halo_recv, hist_send, hist_recv, pack_send, pack_recv, state_send, state_recv,
 ):
+    held = (held_0, held_1, held_2, held_3, held_4, held_5)
     me_w, me_n = lax.axis_index("wide"), lax.axis_index("narrow")
     small = [
         pltpu.make_async_copy(source, target, small_sem.at[n])
@@ -93,7 +94,7 @@
     ]
     for copy in small:
         copy.start()
-    loads = [pltpu.make_async_copy(history.at[c], held.at[c], load_sem.at[c]) for c in range(CLUSTERS)]
+    loads = [pltpu.make_async_copy(history.at[:, k], held[k], load_sem.at[k]) for k in range(SLOTS)]
     for copy in loads:
         copy.start()
 
@@ -182,6 +183,57 @@
     for copy in halos:
         copy.start()
 
+    def split_parts(tile):
+        high = tile.astype(BF16)
+        rest = tile - high.astype(F32)
+        middle = rest.astype(BF16)
+        return high, middle, (rest - middle.astype(F32)).astype(BF16)
+
+    def split_tile(t, carry):
+        for n, part in enumerate(split_parts(table[t])):
+            split[t, n * 16:n * 16 + 16] = part
+        return carry
+
+    def toward(e):
+        return device(1 - 2 * lax.rem(e, 2), 0)
+
+    def hist_copy(e, k):
+        return pltpu.make_async_remote_copy(
+            src_ref=raw.at[e, k], dst_ref=hist_rows.at[CLUSTERS + e, k],
+            send_sem=hist_send.at[e, k], recv_sem=hist_recv.at[e, k],
+            device_id=toward(e), device_id_type=MESH,
+        )
+
+    def pack_copy(e):
+        return pltpu.make_async_remote_copy(
+            src_ref=pack.at[e], dst_ref=packed.at[e], send_sem=pack_send.at[e], recv_sem=pack_recv.at[e],
+            device_id=toward(e), device_id_type=MESH,
+        )
+
+    def state_copy(e):
+        return pltpu.make_async_remote_copy(
+            src_ref=sent_state.at[e], dst_ref=state_in.at[e],
+            send_sem=state_send.at[e], recv_sem=state_recv.at[e],
+            device_id=toward(e), device_id_type=MESH,
+        )
+
+    def leaver(e):
+        return jnp.maximum(move_src[0, 0, lax.rem(e, 2), e // 2], 0)
+
+    for copy in small[5:]:
+        copy.wait()
+
+    def send_hist(e, k):
+        raw[e, k] = held[k][leaver(e)]
+        hist_copy(e, k).start()
+
+    def send_first(k):
+        loads[k].wait()
+        for e in range(2):
+            send_hist(e, k)
+
+    send_first(0)
+    send_first(1)
     for a in range(CW):
         base, u, half, v = advanced(a)
         here = pl.ds(a * CN, CN)
@@ -192,46 +244,10 @@
         for f, row in enumerate(tile_rows(a, 0.0, 0.0, base, u, v)):
             table[here, f] = row
 
-    def split_parts(tile):
-        high = tile.astype(BF16)
-        rest = tile - high.astype(F32)
-        middle = rest.astype(BF16)
-        return high, middle, (rest - middle.astype(F32)).astype(BF16)
-
-    def split_tile(t, carry):
-        for n, part in enumerate(split_parts(table[t])):
-            split[t, n * 16:n * 16 + 16] = part
-        return carry
-
-    def toward(e):
-        return device(1 - 2 * lax.rem(e, 2), 0)
-
-    def hist_copy(e):
-        return pltpu.make_async_remote_copy(
-            src_ref=raw.at[e], dst_ref=hist_rows.at[CLUSTERS + e], send_sem=hist_send.at[e], recv_sem=hist_recv.at[e],
-            device_id=toward(e), device_id_type=MESH,
-        )
-
-    def pack_copy(e):
-        return pltpu.make_async_remote_copy(
-            src_ref=pack.at[e], dst_ref=packed.at[e], send_sem=pack_send.at[e], recv_sem=pack_recv.at[e],
-            device_id=toward(e), device_id_type=MESH,
-        )
-
-    def state_copy(e):
-        return pltpu.make_async_remote_copy(
-            src_ref=sent_state.at[e], dst_ref=state_in.at[e],
-            send_sem=state_send.at[e], recv_sem=state_recv.at[e],
-            device_id=toward(e), device_id_type=MESH,
-        )
-
-    def leaver(e):
-        return jnp.maximum(move_src[0, 0, lax.rem(e, 2), e // 2], 0)
-
-    for copy in small[5:]:
-        copy.wait()
     lax.fori_loop(0, CLUSTERS, split_tile, 0, unroll=4)
     split_tile(TILES, 0)
+    send_first(2)
+    send_first(3)
 
     def left_rows(parts, count):
         turned = jnp.transpose(parts.astype(F32)).astype(BF16)
@@ -243,18 +259,8 @@
         return carry
 
     lax.fori_loop(0, CLUSTERS, left_side, 0, unroll=4)
-
-    for copy in loads:
-        copy.wait()
-
-    def send_hist(e, carry):
-        c = leaver(e)
-        for k in range(SLOTS):
-            raw[e, k] = held[c, k]
-        hist_copy(e).start()
-        return carry
-
-    lax.fori_loop(0, 2, send_hist, 0)
+    send_first(4)
+    send_first(5)
 
     def place_of(c):
         a = lax.shift_right_logical(c, 2)
@@ -291,7 +297,7 @@
         scaled = stretch * inverse_limit(c, k, spot)
         if k == 0:
             scaled = scaled - apart[...]
-        hist = jnp.maximum(held[c, k], scaled)
+        hist = jnp.maximum(held[k][c], scaled)
         hist_rows[c, k] = hist
         weight = jnp.exp2(rest_sq * FALLOFF) * jnp.minimum(jnp.maximum(2.0 - hist, 0.0), 1.0)
         factor = weight * (stretch + rate * now_inv) * now_inv
@@ -349,7 +355,13 @@
                 copy.start()
             lax.fori_loop(CLUSTERS, TILES, split_tile, 0, unroll=2)
             lax.fori_loop(0, 4, send_pack, 0)
-            lax.fori_loop(2, 4, send_hist, 0)
+
+            def send_second(e, carry):
+                for k in range(SLOTS):
+                    send_hist(e, k)
+                return carry
+
+            lax.fori_loop(2, 4, send_second, 0)
 
         first, second = nth(2 * i), nth(2 * i + 1)
         cluster(first, 0, second, 1)
@@ -390,8 +402,8 @@
         sources[o] = source
 
     def arrive(e, carry):
-        hist_copy(e).wait()
         for k in range(SLOTS):
+            hist_copy(e, k).wait()
             pair, at = k // 2, pl.ds((k % 2) * POINTS, POINTS)
             rest_sq = forms_in[e, pair, 0:POINTS, at]
             if k == 0:
@@ -451,7 +463,7 @@
         in_specs=[anywhere] * len(operands),
         out_specs=(vmem, vmem, vmem, smem),
         scratch_shapes=[
-            pltpu.VMEM((CLUSTERS, SLOTS, POINTS, POINTS), F32),
+            *[pltpu.VMEM((CLUSTERS, POINTS, POINTS), F32)] * SLOTS,
             *[pltpu.VMEM(ref_local.shape, F32)] * 4,
             pltpu.SMEM(critical.shape, F32),
             pltpu.SMEM(active.shape, jnp.int32),
@@ -475,10 +487,11 @@
             pltpu.VMEM((4, 16, POINTS), F32),
             pltpu.SemaphoreType.DMA((10,)),
             pltpu.SemaphoreType.DMA((2,)),
-            pltpu.SemaphoreType.DMA((CLUSTERS,)),
+            pltpu.SemaphoreType.DMA((SLOTS,)),
             pltpu.SemaphoreType.DMA((8,)),
             pltpu.SemaphoreType.DMA((8,)),
-            *[pltpu.SemaphoreType.DMA((4,))] * 6,
+            *[pltpu.SemaphoreType.DMA((4, SLOTS))] * 2,
+            *[pltpu.SemaphoreType.DMA((4,))] * 4,
         ],
         compiler_params=pltpu.CompilerParams(
             collective_id=0, has_side_effects=True, vmem_limit_bytes=26 << 20

time: 27.3 us -> 27.8 us (1.018)
  Pallas kernels: 26.5 us -> 27 us
    pallas_call x1, Pallas kernels: 23.7 us -> 24.2 us  [per_device(): pl.pallas_call(functools.partial(step_kernel, wide_size, narrow_size), ou...]
where the time goes in v7:
time: 27.8 us; the launch traced here: 27.6 us
  Pallas kernels  27 us (97%)
  between operations  0.64 us (2%)
    pallas_call x1, Pallas kernels, per_device(): pl.pallas_call(functools.partial(step_kernel, wide_size, narrow_size), ou...  24.2 us
    pallas_call x1, Pallas kernels, per_device(): pl.pallas_call(place_kernel, out_shape=(state,) * 4 + (jax.ShapeDtypeStru...  2.85 us

profile of v7, /device:TPU:0, one launch (start us, length us, event | category | flops | bytes accessed | tf_op | source)
XLA Modules:
  0.0 27.6 jit_solution(15682445346852520997)
XLA Ops:
  0.6 24.2 %step.1 = (f32[20,6,128,128]{3,2,1,0:T(8,128)S(1)}, f32[16,16,128]{2,1,0:T(8,128)S(1)}, f32[4,16,128]{2,1,0:T(8,128)S(1)}, s32[16]{0:T(128)S(4)}) custom-call(f32[3,4,4,128]{3,2,1,0:T(4,128)} %ref_hbm.1, f32[3,4,4,128]{3,2,1,0:T(4,128)} %disp_hbm.1, f32[3,4,4,128]{3,2,1,0:T(4,128)} %vel_hbm.1, f32[3,4,4,128]{3,2,1,0:T(4,128)} %acc_hbm.1, ...), custom_call_target="tpu_custom_call" | custom-call | tf_op jit(solution)/shard_map/step/pallas_call | solution.py:455
  24.8 2.8 %place.1 = (f32[3,4,4,128]{3,2,1,0:T(4,128)}, f32[3,4,4,128]{3,2,1,0:T(4,128)}, f32[3,4,4,128]{3,2,1,0:T(4,128)}, f32[3,4,4,128]{3,2,1,0:T(4,128)}, f32[16,6,128,128]{3,2,1,0:T(8,128)}) custom-call(f32[20,6,128,128]{3,2,1,0:T(8,128)S(1)} %get-tuple-element.14.hist_rows, f32[16,16,128]{2,1,0:T(8,128)S(1)} %get-tuple-element.15.state_rows, ...), custom_call_target="tpu_custom_call" | custom-call | tf_op jit(solution)/shard_map/place/pallas_call | solution.py:506

commit v8 on v7

--- a/solution.py
+++ b/solution.py
@@ -49,11 +49,6 @@
             s[g, PARTS.index((part, 0)) * 16 + ROW_SQ[g], ROW_ONE] = 1
             s[g, PARTS.index((0, part)) * 16 + ROW_ONE, part * 16 + ROW_SQ[g]] = 1
     return s.reshape(3 * 128, 48).T
-
-
-def around(i, size):
-    i = jnp.where(i < 0, i + size, i)
-    return jnp.where(i >= size, i - size, i)
 
 
 def dot(a, b):
@@ -99,11 +94,26 @@
         copy.start()
 
     def device(dw, dn):
-        return (around(me_w + dw, wide_size), around(me_n + dn, narrow_size))
+        return (me_w + dw, me_n + dn)
+
+    at_edge = {-1: (me_w == 0, me_n == 0), 1: (me_w == wide_size - 1, me_n == narrow_size - 1)}
+
+    def beyond(dw, dn):
+        out = False
+        if dw:
+            out = out | at_edge[dw][0]
+        if dn:
+            out = out | at_edge[dn][1]
+        return out
 
     barrier = pltpu.get_barrier_semaphore()
+    greeted = 0
     for dw, dn in SIDES:
-        pl.semaphore_signal(barrier, inc=1, device_id=device(dw, dn), device_id_type=MESH)
+        greeted = greeted + jnp.where(beyond(dw, dn), 0, 1)
+
+        @pl.when(jnp.logical_not(beyond(dw, dn)))
+        def _():
+            pl.semaphore_signal(barrier, inc=1, device_id=device(dw, dn), device_id_type=MESH)
 
     sub = lax.broadcasted_iota(jnp.int32, (POINTS, POINTS), 0)
     lane = lax.broadcasted_iota(jnp.int32, (POINTS, POINTS), 1)
@@ -114,16 +124,8 @@
     table[TILES] = jnp.where(row == ROW_ONE, 1.0, far)
     for i in range(CW + 2):
         for j in range(CN + 2):
-            edges = [
-                edge for out, edge in (
-                    (i == 0, me_w == 0), (i == CW + 1, me_w == wide_size - 1),
-                    (j == 0, me_n == 0), (j == CN + 1, me_n == narrow_size - 1),
-                ) if out
-            ]
-            spot = tile_index(i - 1, j - 1)
-            for edge in edges:
-                spot = jnp.where(edge, TILES, spot)
-            where_is[i * (CN + 2) + j] = spot
+            out = beyond((i == CW + 1) - (i == 0), (j == CN + 1) - (j == 0))
+            where_is[i * (CN + 2) + j] = jnp.where(out, TILES, tile_index(i - 1, j - 1))
 
     for copy in small[:5]:
         copy.wait()
@@ -170,7 +172,7 @@
             tag = jnp.full((8, POINTS), move_dst[0, 0, 1 - side, m], jnp.int32).astype(F32)
             leaving[TAGS_AT[side] - CLUSTERS, 8 * m:8 * m + 8] = tag
 
-    pl.semaphore_wait(barrier, len(SIDES))
+    pl.semaphore_wait(barrier, greeted)
     halos = []
     for n, (dw, dn) in enumerate(SIDES):
         landing = SIDE_AT[SIDES.index((-dw, -dn))]
@@ -180,8 +182,13 @@
             send_sem=halo_send.at[n], recv_sem=halo_recv.at[n],
             device_id=device(dw, dn), device_id_type=MESH,
         ))
-    for copy in halos:
-        copy.start()
+    for side, copy in zip(SIDES, halos):
+        pl.when(jnp.logical_not(beyond(*side)))(copy.start)
+    for n in range(2):
+        @pl.when(beyond(*SIDES[n]))
+        def _():
+            table[TAGS_AT[n]] = jnp.full((16, POINTS), -1.0, F32)
+
 
     def split_parts(tile):
         high = tile.astype(BF16)
@@ -196,6 +203,12 @@
 
     def toward(e):
         return device(1 - 2 * lax.rem(e, 2), 0)
+
+    def goes(e):
+        return jnp.logical_not(jnp.where(lax.rem(e, 2) == 0, at_edge[1][0], at_edge[-1][0]))
+
+    def comes(e):
+        return jnp.logical_not(jnp.where(lax.rem(e, 2) == 0, at_edge[-1][0], at_edge[1][0]))
 
     def hist_copy(e, k):
         return pltpu.make_async_remote_copy(
@@ -230,7 +243,7 @@
     def send_first(k):
         loads[k].wait()
         for e in range(2):
-            send_hist(e, k)
+            pl.when(goes(e))(functools.partial(send_hist, e, k))
 
     send_first(0)
     send_first(1)
@@ -335,7 +348,7 @@
             pack[e, 16 + 8 * k:24 + 8 * k] = table[spot, 0:8]
             pack[e, 16 + 8 * SLOTS + k:17 + 8 * SLOTS + k] = inverse_limit(c, k, spot)
         pack[e, 16 + 9 * SLOTS:PACK_ROWS] = jnp.zeros((8 - SLOTS, POINTS), F32)
-        pack_copy(e).start()
+        pl.when(goes(e))(pack_copy(e).start)
         return carry
 
     def nth(i):
@@ -349,16 +362,19 @@
     def two(i, carry):
         @pl.when(i == 1)
         def _():
-            for copy in halos:
-                copy.wait()
+            for (dw, dn), copy in zip(SIDES, halos):
+                pl.when(jnp.logical_not(beyond(dw, dn)))(copy.wait_send)
+                pl.when(jnp.logical_not(beyond(-dw, -dn)))(copy.wait_recv)
             for copy in tag_copies:
                 copy.start()
             lax.fori_loop(CLUSTERS, TILES, split_tile, 0, unroll=2)
             lax.fori_loop(0, 4, send_pack, 0)
 
             def send_second(e, carry):
-                for k in range(SLOTS):
-                    send_hist(e, k)
+                @pl.when(goes(e))
+                def _():
+                    for k in range(SLOTS):
+                        send_hist(e, k)
                 return carry
 
             lax.fori_loop(2, 4, send_second, 0)
@@ -372,7 +388,7 @@
 
     def send_state(e, carry):
         sent_state[e] = state_rows[leaver(e)]
-        state_copy(e).start()
+        pl.when(goes(e))(state_copy(e).start)
         return carry
 
     lax.fori_loop(0, 4, send_state, 0)
@@ -380,7 +396,7 @@
     tail = jnp.where(lax.broadcasted_iota(jnp.int32, (8, POINTS), 0) == ROW_ONE - 8, 1.0, 0.0)
 
     def expect(e, carry):
-        pack_copy(e).wait()
+        pl.when(comes(e))(pack_copy(e).wait_recv)
         own = jnp.concatenate(split_parts(packed[e, 0:16]), 0)
         mine = left_rows(own, 2)[:, 0:96]
         for pair in range(SLOTS // 2):
@@ -403,7 +419,7 @@
 
     def arrive(e, carry):
         for k in range(SLOTS):
-            hist_copy(e, k).wait()
+            pl.when(comes(e))(hist_copy(e, k).wait_recv)
             pair, at = k // 2, pl.ds((k % 2) * POINTS, POINTS)
             rest_sq = forms_in[e, pair, 0:POINTS, at]
             if k == 0:
@@ -418,8 +434,18 @@
 
     lax.fori_loop(0, 4, arrive, 0)
 
-    for e in range(4):
-        state_copy(e).wait()
+    def finish(e, carry):
+        pl.when(comes(e))(state_copy(e).wait_recv)
+
+        @pl.when(goes(e))
+        def _():
+            for k in range(SLOTS):
+                hist_copy(e, k).wait_send()
+            pack_copy(e).wait_send()
+            state_copy(e).wait_send()
+        return carry
+
+    lax.fori_loop(0, 4, finish, 0)
 
 
 def place_kernel(hist_rows, state_rows, state_in, sources, ref_out, disp_out, vel_out, acc_out, hist_out, states, state_sem, sem):

time: 27.8 us -> 23.9 us (0.86)
  the two profiles are of different devices: /device:TPU:0 before, /device:TPU:6 now
where the time goes in v8:
time: 23.9 us; the launch traced here: 23.8 us
  Pallas kernels  23.1 us (97%)
  between operations  0.64 us (3%)
    pallas_call x1, Pallas kernels, per_device(): pl.pallas_call(functools.partial(step_kernel, wide_size, narrow_size), ou...  20.3 us
    pallas_call x1, Pallas kernels, per_device(): pl.pallas_call(place_kernel, out_shape=(state,) * 4 + (jax.ShapeDtypeStru...  2.85 us

profile of v8, /device:TPU:6, one launch (start us, length us, event | category | flops | bytes accessed | tf_op | source)
XLA Modules:
  0.0 23.8 jit_solution(1008867817774827001)
XLA Ops:
  0.6 20.3 %step.1 = (f32[20,6,128,128]{3,2,1,0:T(8,128)S(1)}, f32[16,16,128]{2,1,0:T(8,128)S(1)}, f32[4,16,128]{2,1,0:T(8,128)S(1)}, s32[16]{0:T(128)S(4)}) custom-call(f32[3,4,4,128]{3,2,1,0:T(4,128)} %ref_hbm.1, f32[3,4,4,128]{3,2,1,0:T(4,128)} %disp_hbm.1, f32[3,4,4,128]{3,2,1,0:T(4,128)} %vel_hbm.1, f32[3,4,4,128]{3,2,1,0:T(4,128)} %acc_hbm.1, ...), custom_call_target="tpu_custom_call" | custom-call | tf_op jit(solution)/shard_map/step/pallas_call | solution.py:481
  20.9 2.8 %place.1 = (f32[3,4,4,128]{3,2,1,0:T(4,128)}, f32[3,4,4,128]{3,2,1,0:T(4,128)}, f32[3,4,4,128]{3,2,1,0:T(4,128)}, f32[3,4,4,128]{3,2,1,0:T(4,128)}, f32[16,6,128,128]{3,2,1,0:T(8,128)}) custom-call(f32[20,6,128,128]{3,2,1,0:T(8,128)S(1)} %get-tuple-element.14.hist_rows, f32[16,16,128]{2,1,0:T(8,128)S(1)} %get-tuple-element.15.state_rows, ...), custom_call_target="tpu_custom_call" | custom-call | tf_op jit(solution)/shard_map/place/pallas_call | solution.py:532

commit v9 on v8

--- a/solution.py
+++ b/solution.py
@@ -79,6 +79,28 @@
 ):
     held = (held_0, held_1, held_2, held_3, held_4, held_5)
     me_w, me_n = lax.axis_index("wide"), lax.axis_index("narrow")
+    def device(dw, dn):
+        return (me_w + dw, me_n + dn)
+
+    at_edge = {-1: (me_w == 0, me_n == 0), 1: (me_w == wide_size - 1, me_n == narrow_size - 1)}
+
+    def beyond(dw, dn):
+        out = False
+        if dw:
+            out = out | at_edge[dw][0]
+        if dn:
+            out = out | at_edge[dn][1]
+        return out
+
+    barrier = pltpu.get_barrier_semaphore()
+    greeted = 0
+    for dw, dn in SIDES[::-1]:
+        greeted = greeted + jnp.where(beyond(dw, dn), 0, 1)
+
+        @pl.when(jnp.logical_not(beyond(dw, dn)))
+        def _():
+            pl.semaphore_signal(barrier, inc=1, device_id=device(dw, dn), device_id_type=MESH)
+
     small = [
         pltpu.make_async_copy(source, target, small_sem.at[n])
         for n, (source, target) in enumerate((
@@ -92,28 +114,6 @@
     loads = [pltpu.make_async_copy(history.at[:, k], held[k], load_sem.at[k]) for k in range(SLOTS)]
     for copy in loads:
         copy.start()
-
-    def device(dw, dn):
-        return (me_w + dw, me_n + dn)
-
-    at_edge = {-1: (me_w == 0, me_n == 0), 1: (me_w == wide_size - 1, me_n == narrow_size - 1)}
-
-    def beyond(dw, dn):
-        out = False
-        if dw:
-            out = out | at_edge[dw][0]
-        if dn:
-            out = out | at_edge[dn][1]
-        return out
-
-    barrier = pltpu.get_barrier_semaphore()
-    greeted = 0
-    for dw, dn in SIDES:
-        greeted = greeted + jnp.where(beyond(dw, dn), 0, 1)
-
-        @pl.when(jnp.logical_not(beyond(dw, dn)))
-        def _():
-            pl.semaphore_signal(barrier, inc=1, device_id=device(dw, dn), device_id_type=MESH)
 
     sub = lax.broadcasted_iota(jnp.int32, (POINTS, POINTS), 0)
     lane = lax.broadcasted_iota(jnp.int32, (POINTS, POINTS), 1)
@@ -182,7 +182,7 @@
             send_sem=halo_send.at[n], recv_sem=halo_recv.at[n],
             device_id=device(dw, dn), device_id_type=MESH,
         ))
-    for side, copy in zip(SIDES, halos):
+    for side, copy in reversed(list(zip(SIDES, halos))):
         pl.when(jnp.logical_not(beyond(*side)))(copy.start)
     for n in range(2):
         @pl.when(beyond(*SIDES[n]))
@@ -353,31 +353,45 @@
 
     def nth(i):
         inner = 5 + lax.rem(i, 2) + 4 * (i // 2)
-        side = 4 + 4 * ((i - 8) // 2) + 3 * lax.rem(i, 2)
-        return jnp.where(i < 4, inner, jnp.where(i < 8, i - 4, jnp.where(i < 12, side, i)))
+        row = 1 + lax.rem(i, 2) + 12 * ((i - 4) // 2)
+        column = 4 + 4 * lax.rem(i, 2) + 3 * ((i - 8) // 2)
+        corner = 3 * lax.rem(i, 2) + 12 * ((i - 12) // 2)
+        return jnp.where(i < 4, inner, jnp.where(i < 8, row, jnp.where(i < 12, column, corner)))
 
     for pair in range(SLOTS // 2):
         prepare(nth(0), 0, pair)
+
+    def landed(sides):
+        for n in sides:
+            (dw, dn), copy = SIDES[n], halos[n]
+            pl.when(jnp.logical_not(beyond(dw, dn)))(copy.wait_send)
+            pl.when(jnp.logical_not(beyond(-dw, -dn)))(copy.wait_recv)
+
+    def send_second(slots):
+        def go(e, carry):
+            @pl.when(goes(e))
+            def _():
+                for k in slots:
+                    send_hist(e, k)
+            return carry
+
+        lax.fori_loop(2, 4, go, 0)
 
     def two(i, carry):
         @pl.when(i == 1)
         def _():
-            for (dw, dn), copy in zip(SIDES, halos):
-                pl.when(jnp.logical_not(beyond(dw, dn)))(copy.wait_send)
-                pl.when(jnp.logical_not(beyond(-dw, -dn)))(copy.wait_recv)
+            send_second(range(0, 3))
+            landed(range(0, 4))
             for copy in tag_copies:
                 copy.start()
-            lax.fori_loop(CLUSTERS, TILES, split_tile, 0, unroll=2)
+            lax.fori_loop(CLUSTERS, SIDE_AT[4], split_tile, 0, unroll=2)
+
+        @pl.when(i == 4)
+        def _():
+            landed(range(4, 8))
             lax.fori_loop(0, 4, send_pack, 0)
-
-            def send_second(e, carry):
-                @pl.when(goes(e))
-                def _():
-                    for k in range(SLOTS):
-                        send_hist(e, k)
-                return carry
-
-            lax.fori_loop(2, 4, send_second, 0)
+            send_second(range(3, SLOTS))
+            lax.fori_loop(SIDE_AT[4], TILES, split_tile, 0, unroll=2)
 
         first, second = nth(2 * i), nth(2 * i + 1)
         cluster(first, 0, second, 1)
@@ -407,7 +421,7 @@
             forms_in[e, pair] = dot(mine, jnp.concatenate(theirs, 1))
         return carry
 
-    lax.fori_loop(0, 4, expect, 0, unroll=2)
+    lax.fori_loop(0, 4, expect, 0, unroll=4)
 
     for copy in tag_copies:
         copy.wait()

time: 23.9 us -> 22.9 us (0.958)
  the two profiles are of different devices: /device:TPU:6 before, /device:TPU:14 now
where the time goes in v9:
time: 22.9 us; the launch traced here: 22.8 us
  Pallas kernels  22.1 us (97%)
  between operations  0.64 us (3%)
    pallas_call x1, Pallas kernels, per_device(): pl.pallas_call(functools.partial(step_kernel, wide_size, narrow_size), ou...  19.3 us
    pallas_call x1, Pallas kernels, per_device(): pl.pallas_call(place_kernel, out_shape=(state,) * 4 + (jax.ShapeDtypeStru...  2.85 us

profile of v9, /device:TPU:14, one launch (start us, length us, event | category | flops | bytes accessed | tf_op | source)
XLA Modules:
  0.0 22.8 jit_solution(4575941520647884985)
XLA Ops:
  0.6 19.3 %step.1 = (f32[20,6,128,128]{3,2,1,0:T(8,128)S(1)}, f32[16,16,128]{2,1,0:T(8,128)S(1)}, f32[4,16,128]{2,1,0:T(8,128)S(1)}, s32[16]{0:T(128)S(4)}) custom-call(f32[3,4,4,128]{3,2,1,0:T(4,128)} %ref_hbm.1, f32[3,4,4,128]{3,2,1,0:T(4,128)} %disp_hbm.1, f32[3,4,4,128]{3,2,1,0:T(4,128)} %vel_hbm.1, f32[3,4,4,128]{3,2,1,0:T(4,128)} %acc_hbm.1, ...), custom_call_target="tpu_custom_call" | custom-call | tf_op jit(solution)/shard_map/step/pallas_call | solution.py:495
  19.9 2.8 %place.1 = (f32[3,4,4,128]{3,2,1,0:T(4,128)}, f32[3,4,4,128]{3,2,1,0:T(4,128)}, f32[3,4,4,128]{3,2,1,0:T(4,128)}, f32[3,4,4,128]{3,2,1,0:T(4,128)}, f32[16,6,128,128]{3,2,1,0:T(8,128)}) custom-call(f32[20,6,128,128]{3,2,1,0:T(8,128)S(1)} %get-tuple-element.14.hist_rows, f32[16,16,128]{2,1,0:T(8,128)S(1)} %get-tuple-element.15.state_rows, ...), custom_call_target="tpu_custom_call" | custom-call | tf_op jit(solution)/shard_map/place/pallas_call | solution.py:546

commit v10 on v9

--- a/solution.py
+++ b/solution.py
@@ -182,8 +182,8 @@
             send_sem=halo_send.at[n], recv_sem=halo_recv.at[n],
             device_id=device(dw, dn), device_id_type=MESH,
         ))
-    for side, copy in reversed(list(zip(SIDES, halos))):
-        pl.when(jnp.logical_not(beyond(*side)))(copy.start)
+    for n in (0, 1, 4, 5, 6, 7, 2, 3):
+        pl.when(jnp.logical_not(beyond(*SIDES[n])))(halos[n].start)
     for n in range(2):
         @pl.when(beyond(*SIDES[n]))
         def _():
@@ -353,10 +353,10 @@
 
     def nth(i):
         inner = 5 + lax.rem(i, 2) + 4 * (i // 2)
-        row = 1 + lax.rem(i, 2) + 12 * ((i - 4) // 2)
-        column = 4 + 4 * lax.rem(i, 2) + 3 * ((i - 8) // 2)
+        column = 4 + 4 * lax.rem(i, 2) + 3 * ((i - 4) // 2)
+        row = 1 + lax.rem(i, 2) + 12 * ((i - 8) // 2)
         corner = 3 * lax.rem(i, 2) + 12 * ((i - 12) // 2)
-        return jnp.where(i < 4, inner, jnp.where(i < 8, row, jnp.where(i < 12, column, corner)))
+        return jnp.where(i < 4, inner, jnp.where(i < 8, column, jnp.where(i < 12, row, corner)))
 
     for pair in range(SLOTS // 2):
         prepare(nth(0), 0, pair)
@@ -381,10 +381,15 @@
         @pl.when(i == 1)
         def _():
             send_second(range(0, 3))
-            landed(range(0, 4))
+            landed(range(2, 4))
+            lax.fori_loop(SIDE_AT[2], SIDE_AT[4], split_tile, 0, unroll=2)
+
+        @pl.when(i == 3)
+        def _():
+            landed(range(0, 2))
             for copy in tag_copies:
                 copy.start()
-            lax.fori_loop(CLUSTERS, SIDE_AT[4], split_tile, 0, unroll=2)
+            lax.fori_loop(CLUSTERS, SIDE_AT[2], split_tile, 0, unroll=2)
 
         @pl.when(i == 4)
         def _():

time: 22.9 us -> 22.2 us (0.969)
  the two profiles are of different devices: /device:TPU:14 before, /device:TPU:6 now
where the time goes in v10:
time: 22.2 us; the launch traced here: 22 us
  Pallas kernels  21.4 us (96%)
  between operations  0.64 us (3%)
    pallas_call x1, Pallas kernels, per_device(): pl.pallas_call(functools.partial(step_kernel, wide_size, narrow_size), ou...  18.6 us
    pallas_call x1, Pallas kernels, per_device(): pl.pallas_call(place_kernel, out_shape=(state,) * 4 + (jax.ShapeDtypeStru...  2.85 us

profile of v10, /device:TPU:6, one launch (start us, length us, event | category | flops | bytes accessed | tf_op | source)
XLA Modules:
  0.0 22.0 jit_solution(10304467167360023774)
XLA Ops:
  0.6 18.6 %step.1 = (f32[20,6,128,128]{3,2,1,0:T(8,128)S(1)}, f32[16,16,128]{2,1,0:T(8,128)S(1)}, f32[4,16,128]{2,1,0:T(8,128)S(1)}, s32[16]{0:T(128)S(4)}) custom-call(f32[3,4,4,128]{3,2,1,0:T(4,128)} %ref_hbm.1, f32[3,4,4,128]{3,2,1,0:T(4,128)} %disp_hbm.1, f32[3,4,4,128]{3,2,1,0:T(4,128)} %vel_hbm.1, f32[3,4,4,128]{3,2,1,0:T(4,128)} %acc_hbm.1, ...), custom_call_target="tpu_custom_call" | custom-call | tf_op jit(solution)/shard_map/step/pallas_call | solution.py:500
  19.2 2.8 %place.1 = (f32[3,4,4,128]{3,2,1,0:T(4,128)}, f32[3,4,4,128]{3,2,1,0:T(4,128)}, f32[3,4,4,128]{3,2,1,0:T(4,128)}, f32[3,4,4,128]{3,2,1,0:T(4,128)}, f32[16,6,128,128]{3,2,1,0:T(8,128)}) custom-call(f32[20,6,128,128]{3,2,1,0:T(8,128)S(1)} %get-tuple-element.14.hist_rows, f32[16,16,128]{2,1,0:T(8,128)S(1)} %get-tuple-element.15.state_rows, ...), custom_call_target="tpu_custom_call" | custom-call | tf_op jit(solution)/shard_map/place/pallas_call | solution.py:551

commit v11 on v10

--- a/solution.py
+++ b/solution.py
@@ -72,9 +72,9 @@
 def step_kernel(
     wide_size, narrow_size,
     ref_hbm, disp_hbm, vel_hbm, acc_hbm, critical_hbm, active_hbm, partners_hbm, src_hbm, dst_hbm, pairs_hbm, history,
-    hist_rows, state_rows, state_in, sources,
+    hist_rows, state_rows, state_in, packed, forms_in, sources,
     held_0, held_1, held_2, held_3, held_4, held_5, ref_local, displacement, velocity, acceleration, critical, active, partners, move_src, move_dst, pairs, where_is,
-    plain, table, leaving, split, left, forms, forms_in, apart, tags, raw, pack, packed, sent_state,
+    plain, table, leaving, split, left, forms, apart, tags, raw, pack, sent_state,
     small_sem, tag_sem, load_sem, halo_send, halo_recv, hist_send, hist_recv, pack_send, pack_recv, state_send, state_recv,
 ):
     held = (held_0, held_1, held_2, held_3, held_4, held_5)
@@ -104,9 +104,8 @@
     small = [
         pltpu.make_async_copy(source, target, small_sem.at[n])
         for n, (source, target) in enumerate((
-            (ref_hbm, ref_local), (disp_hbm, displacement), (vel_hbm, velocity), (acc_hbm, acceleration),
+            (src_hbm, move_src), (ref_hbm, ref_local), (disp_hbm, displacement), (vel_hbm, velocity), (acc_hbm, acceleration),
             (dst_hbm, move_dst), (pairs_hbm, pairs), (critical_hbm, critical), (active_hbm, active), (partners_hbm, partners),
-            (src_hbm, move_src),
         ))
     ]
     for copy in small:
@@ -127,7 +126,53 @@
             out = beyond((i == CW + 1) - (i == 0), (j == CN + 1) - (j == 0))
             where_is[i * (CN + 2) + j] = jnp.where(out, TILES, tile_index(i - 1, j - 1))
 
-    for copy in small[:5]:
+    def toward(e):
+        return device(1 - 2 * lax.rem(e, 2), 0)
+
+    def goes(e):
+        return jnp.logical_not(jnp.where(lax.rem(e, 2) == 0, at_edge[1][0], at_edge[-1][0]))
+
+    def comes(e):
+        return jnp.logical_not(jnp.where(lax.rem(e, 2) == 0, at_edge[-1][0], at_edge[1][0]))
+
+    def hist_copy(e, k, count):
+        return pltpu.make_async_remote_copy(
+            src_ref=raw.at[e, pl.ds(k, count)], dst_ref=hist_rows.at[CLUSTERS + e, pl.ds(k, count)],
+            send_sem=hist_send.at[e, k], recv_sem=hist_recv.at[e, k],
+            device_id=toward(e), device_id_type=MESH,
+        )
+
+    def pack_copy(e):
+        return pltpu.make_async_remote_copy(
+            src_ref=pack.at[e], dst_ref=packed.at[e], send_sem=pack_send.at[e], recv_sem=pack_recv.at[e],
+            device_id=toward(e), device_id_type=MESH,
+        )
+
+    def state_copy(e):
+        return pltpu.make_async_remote_copy(
+            src_ref=sent_state.at[e], dst_ref=state_in.at[e],
+            send_sem=state_send.at[e], recv_sem=state_recv.at[e],
+            device_id=toward(e), device_id_type=MESH,
+        )
+
+    def leaver(e):
+        return jnp.maximum(move_src[0, 0, lax.rem(e, 2), e // 2], 0)
+
+    def send_hist(e, k, count):
+        for n in range(k, k + count):
+            raw[e, n] = held[n][leaver(e)]
+        hist_copy(e, k, count).start()
+
+    def send_first(k, count):
+        for n in range(k, k + count):
+            loads[n].wait()
+        for e in range(2):
+            pl.when(goes(e))(functools.partial(send_hist, e, k, count))
+
+    small[0].wait()
+    pl.semaphore_wait(barrier, greeted)
+    send_first(0, 1)
+    for copy in small[1:6]:
         copy.wait()
     column = lax.broadcasted_iota(jnp.int32, (CN, POINTS), 0)
     anchor_n = column.astype(F32) * CELL_SPAN - CELL_SPAN * CN / 2
@@ -172,7 +217,6 @@
             tag = jnp.full((8, POINTS), move_dst[0, 0, 1 - side, m], jnp.int32).astype(F32)
             leaving[TAGS_AT[side] - CLUSTERS, 8 * m:8 * m + 8] = tag
 
-    pl.semaphore_wait(barrier, greeted)
     halos = []
     for n, (dw, dn) in enumerate(SIDES):
         landing = SIDE_AT[SIDES.index((-dw, -dn))]
@@ -201,52 +245,10 @@
             split[t, n * 16:n * 16 + 16] = part
         return carry
 
-    def toward(e):
-        return device(1 - 2 * lax.rem(e, 2), 0)
-
-    def goes(e):
-        return jnp.logical_not(jnp.where(lax.rem(e, 2) == 0, at_edge[1][0], at_edge[-1][0]))
-
-    def comes(e):
-        return jnp.logical_not(jnp.where(lax.rem(e, 2) == 0, at_edge[-1][0], at_edge[1][0]))
-
-    def hist_copy(e, k):
-        return pltpu.make_async_remote_copy(
-            src_ref=raw.at[e, k], dst_ref=hist_rows.at[CLUSTERS + e, k],
-            send_sem=hist_send.at[e, k], recv_sem=hist_recv.at[e, k],
-            device_id=toward(e), device_id_type=MESH,
-        )
-
-    def pack_copy(e):
-        return pltpu.make_async_remote_copy(
-            src_ref=pack.at[e], dst_ref=packed.at[e], send_sem=pack_send.at[e], recv_sem=pack_recv.at[e],
-            device_id=toward(e), device_id_type=MESH,
-        )
-
-    def state_copy(e):
-        return pltpu.make_async_remote_copy(
-            src_ref=sent_state.at[e], dst_ref=state_in.at[e],
-            send_sem=state_send.at[e], recv_sem=state_recv.at[e],
-            device_id=toward(e), device_id_type=MESH,
-        )
-
-    def leaver(e):
-        return jnp.maximum(move_src[0, 0, lax.rem(e, 2), e // 2], 0)
-
-    for copy in small[5:]:
+    for copy in small[6:]:
         copy.wait()
 
-    def send_hist(e, k):
-        raw[e, k] = held[k][leaver(e)]
-        hist_copy(e, k).start()
-
-    def send_first(k):
-        loads[k].wait()
-        for e in range(2):
-            pl.when(goes(e))(functools.partial(send_hist, e, k))
-
-    send_first(0)
-    send_first(1)
+    send_first(1, 1)
     for a in range(CW):
         base, u, half, v = advanced(a)
         here = pl.ds(a * CN, CN)
@@ -259,8 +261,7 @@
 
     lax.fori_loop(0, CLUSTERS, split_tile, 0, unroll=4)
     split_tile(TILES, 0)
-    send_first(2)
-    send_first(3)
+    send_first(2, 2)
 
     def left_rows(parts, count):
         turned = jnp.transpose(parts.astype(F32)).astype(BF16)
@@ -272,8 +273,7 @@
         return carry
 
     lax.fori_loop(0, CLUSTERS, left_side, 0, unroll=4)
-    send_first(4)
-    send_first(5)
+    send_first(4, 2)
 
     def place_of(c):
         a = lax.shift_right_logical(c, 2)
@@ -367,12 +367,9 @@
             pl.when(jnp.logical_not(beyond(dw, dn)))(copy.wait_send)
             pl.when(jnp.logical_not(beyond(-dw, -dn)))(copy.wait_recv)
 
-    def send_second(slots):
+    def send_second(k):
         def go(e, carry):
-            @pl.when(goes(e))
-            def _():
-                for k in slots:
-                    send_hist(e, k)
+            pl.when(goes(e))(functools.partial(send_hist, e, k, 3))
             return carry
 
         lax.fori_loop(2, 4, go, 0)
@@ -380,7 +377,7 @@
     def two(i, carry):
         @pl.when(i == 1)
         def _():
-            send_second(range(0, 3))
+            send_second(0)
             landed(range(2, 4))
             lax.fori_loop(SIDE_AT[2], SIDE_AT[4], split_tile, 0, unroll=2)
 
@@ -395,7 +392,7 @@
         def _():
             landed(range(4, 8))
             lax.fori_loop(0, 4, send_pack, 0)
-            send_second(range(3, SLOTS))
+            send_second(3)
             lax.fori_loop(SIDE_AT[4], TILES, split_tile, 0, unroll=2)
 
         first, second = nth(2 * i), nth(2 * i + 1)
@@ -436,53 +433,83 @@
             source = jnp.where(tags[e % 2, 8 * (e // 2), 0] == float(o), CLUSTERS + e, source)
         sources[o] = source
 
-    def arrive(e, carry):
+    def arrive(entries, parts):
+        for k, count in parts:
+            for e in entries:
+                pl.when(comes(e))(hist_copy(e, k, count).wait_recv)
+
+    first, second = ((0, 1), (1, 1), (2, 2), (4, 2)), ((0, 3), (3, 3))
+    arrive((0, 1), first)
+    arrive((2, 3), second)
+
+    for e in range(4):
+        @pl.when(goes(e))
+        def _():
+            for k, count in first if e < 2 else second:
+                hist_copy(e, k, count).wait_send()
+
+    def finish(e, carry):
+        pl.when(comes(e))(state_copy(e).wait_recv)
+
+        @pl.when(goes(e))
+        def _():
+            pack_copy(e).wait_send()
+            state_copy(e).wait_send()
+        return carry
+
+    lax.fori_loop(0, 4, finish, 0)
+
+
+def place_kernel(
+    hist_rows, state_rows, state_in, packed, forms, sources,
+    ref_out, disp_out, vel_out, acc_out, hist_out,
+    states, arrived, state_sem, sem,
+):
+    def stays(o):
+        return pltpu.make_async_copy(hist_rows.at[o], hist_out.at[o], sem.at[o])
+
+    def arrives(o):
+        return pltpu.make_async_copy(arrived.at[jnp.maximum(sources[o] - CLUSTERS, 0)], hist_out.at[o], sem.at[o])
+
+    for o in range(CLUSTERS):
+        pl.when(sources[o] < CLUSTERS)(stays(o).start)
+
+    sub = lax.broadcasted_iota(jnp.int32, (POINTS, POINTS), 0)
+    lane = lax.broadcasted_iota(jnp.int32, (POINTS, POINTS), 1)
+    same = jnp.where(sub == lane, APART, 0.0).astype(F32)
+
+    def take(e, carry):
         for k in range(SLOTS):
-            pl.when(comes(e))(hist_copy(e, k).wait_recv)
             pair, at = k // 2, pl.ds((k % 2) * POINTS, POINTS)
-            rest_sq = forms_in[e, pair, 0:POINTS, at]
+            rest_sq = forms[e, pair, 0:POINTS, at]
             if k == 0:
-                rest_sq = rest_sq + apart[...]
-            now_sq = jnp.maximum(rest_sq + forms_in[e, pair, POINTS:2 * POINTS, at], TINY)
+                rest_sq = rest_sq + same
+            now_sq = jnp.maximum(rest_sq + forms[e, pair, POINTS:2 * POINTS, at], TINY)
             stretch = now_sq * lax.rsqrt(now_sq) * lax.rsqrt(rest_sq) - 1.0
             scaled = stretch * packed[e, 16 + 8 * SLOTS + k:17 + 8 * SLOTS + k]
             if k == 0:
-                scaled = scaled - apart[...]
-            hist_rows[CLUSTERS + e, k] = jnp.maximum(hist_rows[CLUSTERS + e, k], scaled)
-        return carry
-
-    lax.fori_loop(0, 4, arrive, 0)
-
-    def finish(e, carry):
-        pl.when(comes(e))(state_copy(e).wait_recv)
-
-        @pl.when(goes(e))
-        def _():
-            for k in range(SLOTS):
-                hist_copy(e, k).wait_send()
-            pack_copy(e).wait_send()
-            state_copy(e).wait_send()
-        return carry
-
-    lax.fori_loop(0, 4, finish, 0)
-
-
-def place_kernel(hist_rows, state_rows, state_in, sources, ref_out, disp_out, vel_out, acc_out, hist_out, states, state_sem, sem):
-    copies = []
+                scaled = scaled - same
+            arrived[e, k] = jnp.maximum(hist_rows[CLUSTERS + e, k], scaled)
+        return carry
+
+    lax.fori_loop(0, 4, take, 0)
     for o in range(CLUSTERS):
-        copies.append(pltpu.make_async_copy(hist_rows.at[sources[o]], hist_out.at[o], sem.at[o]))
-        copies[-1].start()
+        pl.when(sources[o] >= CLUSTERS)(arrives(o).start)
     for o in range(CLUSTERS):
         source = sources[o]
         rows = jnp.where(source < CLUSTERS, state_rows[o], state_in[jnp.maximum(source - CLUSTERS, 0)])
         for f in range(4):
             for d in range(3):
                 states[f, d, o // CN, o % CN:o % CN + 1] = rows[3 * f + d:3 * f + d + 1]
+    copies = []
     for f, ref in enumerate((ref_out, disp_out, vel_out, acc_out)):
         copies.append(pltpu.make_async_copy(states.at[f], ref, state_sem.at[f]))
         copies[-1].start()
     for copy in copies:
         copy.wait()
+    for o in range(CLUSTERS):
+        pl.when(sources[o] < CLUSTERS)(stays(o).wait)
+        pl.when(sources[o] >= CLUSTERS)(arrives(o).wait)
 
 
 def per_device(
@@ -497,16 +524,18 @@
         jnp.asarray(pairing(), BF16), history.reshape(CLUSTERS, SLOTS, POINTS, POINTS),
     ]
     operands = [pltpu.with_memory_space_constraint(x, pltpu.HBM) for x in operands]
-    hist_rows, state_rows, state_in, sources = pl.pallas_call(
+    *rows, sources = pl.pallas_call(
         functools.partial(step_kernel, wide_size, narrow_size),
         out_shape=(
             pltpu.VMEM(hist_shape, F32),
             pltpu.VMEM((CLUSTERS, 16, POINTS), F32),
             pltpu.VMEM((4, 16, POINTS), F32),
+            pltpu.VMEM((4, PACK_ROWS, POINTS), F32),
+            pltpu.VMEM((4, SLOTS // 2, 2 * POINTS, 2 * POINTS), F32),
             pltpu.SMEM((CLUSTERS,), jnp.int32),
         ),
         in_specs=[anywhere] * len(operands),
-        out_specs=(vmem, vmem, vmem, smem),
+        out_specs=(vmem,) * 5 + (smem,),
         scratch_shapes=[
             *[pltpu.VMEM((CLUSTERS, POINTS, POINTS), F32)] * SLOTS,
             *[pltpu.VMEM(ref_local.shape, F32)] * 4,
@@ -523,11 +552,9 @@
             pltpu.VMEM((TILES + 1, 48, POINTS), BF16),
             pltpu.VMEM((CLUSTERS, 3 * POINTS, 128), BF16),
             pltpu.VMEM((2, SLOTS // 2, 3 * POINTS, 2 * POINTS), F32),
-            pltpu.VMEM((4, SLOTS // 2, 2 * POINTS, 2 * POINTS), F32),
             pltpu.VMEM((POINTS, POINTS), F32),
             pltpu.SMEM((2, 16, POINTS), F32),
             pltpu.VMEM((4, SLOTS, POINTS, POINTS), F32),
-            pltpu.VMEM((4, PACK_ROWS, POINTS), F32),
             pltpu.VMEM((4, PACK_ROWS, POINTS), F32),
             pltpu.VMEM((4, 16, POINTS), F32),
             pltpu.SemaphoreType.DMA((10,)),
@@ -543,24 +570,23 @@
         ),
         name="step",
     )(*operands)
-    hist_rows = pltpu.with_memory_space_constraint(hist_rows, pltpu.VMEM)
-    state_rows = pltpu.with_memory_space_constraint(state_rows, pltpu.VMEM)
-    state_in = pltpu.with_memory_space_constraint(state_in, pltpu.VMEM)
+    rows = [pltpu.with_memory_space_constraint(x, pltpu.VMEM) for x in rows]
     sources = pltpu.with_memory_space_constraint(sources, pltpu.SMEM)
     state = jax.ShapeDtypeStruct(ref_local.shape, F32)
     outs = pl.pallas_call(
         place_kernel,
         out_shape=(state,) * 4 + (jax.ShapeDtypeStruct((CLUSTERS, SLOTS, POINTS, POINTS), F32),),
-        in_specs=[anywhere, vmem, vmem, smem],
+        in_specs=[vmem] * 5 + [smem],
         out_specs=(anywhere,) * 5,
         scratch_shapes=[
             pltpu.VMEM((4,) + ref_local.shape, F32),
+            pltpu.VMEM((4, SLOTS, POINTS, POINTS), F32),
             pltpu.SemaphoreType.DMA((4,)),
             pltpu.SemaphoreType.DMA((CLUSTERS,)),
         ],
         compiler_params=pltpu.CompilerParams(vmem_limit_bytes=8 << 20),
         name="place",
-    )(hist_rows, state_rows, state_in, sources)
+    )(*rows, sources)
     return outs[:4] + (outs[4].reshape(history.shape),)
 
 

time: 22.2 us -> 21.9 us (0.986)
    pallas_call x1, Pallas kernels: 18.6 us -> 18.3 us  [per_device(): pl.pallas_call(functools.partial(step_kernel, wide_size, narrow_size), ou...]
where the time goes in v11:
time: 21.9 us; the launch traced here: 21.8 us
  Pallas kernels  21.2 us (97%)
  between operations  0.64 us (3%)
    pallas_call x1, Pallas kernels, per_device(): pl.pallas_call(functools.partial(step_kernel, wide_size, narrow_size), ou...  18.3 us
    pallas_call x1, Pallas kernels, per_device(): pl.pallas_call(place_kernel, out_shape=(state,) * 4 + (jax.ShapeDtypeStru...  2.9 us

profile of v11, /device:TPU:6, one launch (start us, length us, event | category | flops | bytes accessed | tf_op | source)
XLA Modules:
  0.0 21.8 jit_solution(7772506448438914814)
XLA Ops:
  0.6 18.3 %step.1 = (f32[20,6,128,128]{3,2,1,0:T(8,128)S(1)}, f32[16,16,128]{2,1,0:T(8,128)S(1)}, f32[4,16,128]{2,1,0:T(8,128)S(1)}, f32[4,72,128]{2,1,0:T(8,128)S(1)}, f3...) custom-call(f32[3,4,4,128]{3,2,1,0:T(4,128)} %ref_hbm.1, f32[3,4,4,128]{3,2,1,0:T(4,128)} %disp_hbm.1, ...), custom_call_target="tpu_custom_call" | custom-call | tf_op jit(solution)/shard_map/step/pallas_call | solution.py:527
  18.9 2.9 %place.1 = (f32[3,4,4,128]{3,2,1,0:T(4,128)}, f32[3,4,4,128]{3,2,1,0:T(4,128)}, f32[3,4,4,128]{3,2,1,0:T(4,128)}, f32[3,4,4,128]{3,2,1,0:T(4,128)}, f32[16,6,128,128]{3,2,1,0:T(8,128)}) custom-call(f32[20,6,128,128]{3,2,1,0:T(8,128)S(1)} %get-tuple-element.16.hist_rows, f32[16,16,128]{2,1,0:T(8,128)S(1)} %get-tuple-element.17.state_rows, ...), custom_call_target="tpu_custom_call" | custom-call | tf_op jit(solution)/shard_map/place/pallas_call | solution.py:576

commit v12 on v11

--- a/solution.py
+++ b/solution.py
@@ -367,9 +367,9 @@
             pl.when(jnp.logical_not(beyond(dw, dn)))(copy.wait_send)
             pl.when(jnp.logical_not(beyond(-dw, -dn)))(copy.wait_recv)
 
-    def send_second(k):
+    def send_second(k, count):
         def go(e, carry):
-            pl.when(goes(e))(functools.partial(send_hist, e, k, 3))
+            pl.when(goes(e))(functools.partial(send_hist, e, k, count))
             return carry
 
         lax.fori_loop(2, 4, go, 0)
@@ -377,7 +377,7 @@
     def two(i, carry):
         @pl.when(i == 1)
         def _():
-            send_second(0)
+            send_second(0, 2)
             landed(range(2, 4))
             lax.fori_loop(SIDE_AT[2], SIDE_AT[4], split_tile, 0, unroll=2)
 
@@ -392,7 +392,7 @@
         def _():
             landed(range(4, 8))
             lax.fori_loop(0, 4, send_pack, 0)
-            send_second(3)
+            send_second(2, 4)
             lax.fori_loop(SIDE_AT[4], TILES, split_tile, 0, unroll=2)
 
         first, second = nth(2 * i), nth(2 * i + 1)
@@ -438,7 +438,7 @@
             for e in entries:
                 pl.when(comes(e))(hist_copy(e, k, count).wait_recv)
 
-    first, second = ((0, 1), (1, 1), (2, 2), (4, 2)), ((0, 3), (3, 3))
+    first, second = ((0, 1), (1, 1), (2, 2), (4, 2)), ((0, 2), (2, 4))
     arrive((0, 1), first)
     arrive((2, 3), second)
 

time: 21.9 us -> 21.9 us (level)
  no operation moved by 1% of the time
where the time goes in v12:
time: 21.9 us; the launch traced here: 21.8 us
  Pallas kernels  21.2 us (97%)
  between operations  0.64 us (3%)
    pallas_call x1, Pallas kernels, per_device(): pl.pallas_call(functools.partial(step_kernel, wide_size, narrow_size), ou...  18.3 us
    pallas_call x1, Pallas kernels, per_device(): pl.pallas_call(place_kernel, out_shape=(state,) * 4 + (jax.ShapeDtypeStru...  2.9 us

profile of v12, /device:TPU:6, one launch (start us, length us, event | category | flops | bytes accessed | tf_op | source)
XLA Modules:
  0.0 21.8 jit_solution(16569945871692085557)
XLA Ops:
  0.6 18.3 %step.1 = (f32[20,6,128,128]{3,2,1,0:T(8,128)S(1)}, f32[16,16,128]{2,1,0:T(8,128)S(1)}, f32[4,16,128]{2,1,0:T(8,128)S(1)}, f32[4,72,128]{2,1,0:T(8,128)S(1)}, f3...) custom-call(f32[3,4,4,128]{3,2,1,0:T(4,128)} %ref_hbm.1, f32[3,4,4,128]{3,2,1,0:T(4,128)} %disp_hbm.1, ...), custom_call_target="tpu_custom_call" | custom-call | tf_op jit(solution)/shard_map/step/pallas_call | solution.py:527
  18.9 2.9 %place.1 = (f32[3,4,4,128]{3,2,1,0:T(4,128)}, f32[3,4,4,128]{3,2,1,0:T(4,128)}, f32[3,4,4,128]{3,2,1,0:T(4,128)}, f32[3,4,4,128]{3,2,1,0:T(4,128)}, f32[16,6,128,128]{3,2,1,0:T(8,128)}) custom-call(f32[20,6,128,128]{3,2,1,0:T(8,128)S(1)} %get-tuple-element.16.hist_rows, f32[16,16,128]{2,1,0:T(8,128)S(1)} %get-tuple-element.17.state_rows, ...), custom_call_target="tpu_custom_call" | custom-call | tf_op jit(solution)/shard_map/place/pallas_call | solution.py:576

commit v13 on v12

--- a/solution.py
+++ b/solution.py
@@ -108,10 +108,8 @@
             (dst_hbm, move_dst), (pairs_hbm, pairs), (critical_hbm, critical), (active_hbm, active), (partners_hbm, partners),
         ))
     ]
-    for copy in small:
-        copy.start()
     loads = [pltpu.make_async_copy(history.at[:, k], held[k], load_sem.at[k]) for k in range(SLOTS)]
-    for copy in loads:
+    for copy in [small[0], loads[0]] + small[1:] + loads[1:]:
         copy.start()
 
     sub = lax.broadcasted_iota(jnp.int32, (POINTS, POINTS), 0)

time: 21.9 us -> 21.9 us (level)
  no operation moved by 1% of the time
where the time goes in v13:
time: 21.9 us; the launch traced here: 21.8 us
  Pallas kernels  21.2 us (97%)
  between operations  0.64 us (3%)
    pallas_call x1, Pallas kernels, per_device(): pl.pallas_call(functools.partial(step_kernel, wide_size, narrow_size), ou...  18.3 us
    pallas_call x1, Pallas kernels, per_device(): pl.pallas_call(place_kernel, out_shape=(state,) * 4 + (jax.ShapeDtypeStru...  2.9 us

profile of v13, /device:TPU:6, one launch (start us, length us, event | category | flops | bytes accessed | tf_op | source)
XLA Modules:
  0.0 21.8 jit_solution(17575845915392058047)
XLA Ops:
  0.6 18.3 %step.1 = (f32[20,6,128,128]{3,2,1,0:T(8,128)S(1)}, f32[16,16,128]{2,1,0:T(8,128)S(1)}, f32[4,16,128]{2,1,0:T(8,128)S(1)}, f32[4,72,128]{2,1,0:T(8,128)S(1)}, f3...) custom-call(f32[3,4,4,128]{3,2,1,0:T(4,128)} %ref_hbm.1, f32[3,4,4,128]{3,2,1,0:T(4,128)} %disp_hbm.1, ...), custom_call_target="tpu_custom_call" | custom-call | tf_op jit(solution)/shard_map/step/pallas_call | solution.py:525
  18.9 2.9 %place.1 = (f32[3,4,4,128]{3,2,1,0:T(4,128)}, f32[3,4,4,128]{3,2,1,0:T(4,128)}, f32[3,4,4,128]{3,2,1,0:T(4,128)}, f32[3,4,4,128]{3,2,1,0:T(4,128)}, f32[16,6,128,128]{3,2,1,0:T(8,128)}) custom-call(f32[20,6,128,128]{3,2,1,0:T(8,128)S(1)} %get-tuple-element.16.hist_rows, f32[16,16,128]{2,1,0:T(8,128)S(1)} %get-tuple-element.17.state_rows, ...), custom_call_target="tpu_custom_call" | custom-call | tf_op jit(solution)/shard_map/place/pallas_call | solution.py:574
